TPU v7x, 512 devices: a whole 4x4x16 slice. The times are simulated.
512 devices in a mesh: tm: 64 (over z_lo, y, core), col: 8 (over z_hi, x).
Axes of the slice: x: 4, y: 4, z: 16 (z_hi: 2, z_lo: 8; z = z_hi * 8 + z_lo), core: 2. Of those that a mesh axis runs over, the one named last changes fastest.
Arguments:
- u_vel: float32 [4, 1024, 8, 1024], P(None, 'tm', None, 'col'), may hold values from -48 to 48
- v_vel: float32 [4, 1024, 8, 1024], P(None, 'tm', None, 'col'), may hold values from -48 to 48
- density: float32 [4, 1024, 8, 1024], P(None, 'tm', None, 'col'), may hold values from -48 to 48
- land_mask: int32 [8, 1024], P(None, 'col'), may hold values 0 or 1
- start_hour: int32 [8, 1024], P(None, 'col'), may hold values from 0 to 255
- levels: int32 [4], replicated, may hold values from 0 to 89, as said below
Outputs:
- pressure: float32 [4, 1024, 8, 1024], P(None, 'tm', None, 'col')
- flux_div: float32 [4, 1024, 8, 1024], P(None, 'tm', None, 'col')
Inputs may be any that keep to these rules, and one draw needn't show every extreme that they name: `levels`: strictly increasing; the first is 0 and the last is 89.
All inputs are finite; a program needn't handle non-finite values. No bound on the sum of `land_mask` on one device may be relied on, other than what follows from the above.
Results may differ from a plain program's by a relative error of at most 0.0003.
Values sent between devices are 32-bit elements; how exact they have to be, the bound alone decides.
No kernel may reach another device: no remote copies, remote signals or barrier semaphores. Data moves between devices by JAX's collectives and lax.ppermute only.
A program may use at most 64 MiB of HBM per device.

v0:
```python
import math

import jax
import jax.numpy as jnp
import numpy as np
from jax import lax
from jax.sharding import PartitionSpec as P

BLOCK = 64


def extended(cells, sides, width):
    for axis, dim in sides:
        count = lax.axis_size(axis)
        ends = count - 1
        head = lax.slice_in_dim(cells, 0, width, axis=dim)
        tail = lax.slice_in_dim(cells, cells.shape[dim] - width, cells.shape[dim], axis=dim)
        cells = jnp.concatenate(
            [
                lax.ppermute(tail, axis, [(i, (i + 1) % count) for i in range(ends)]),
                cells,
                lax.ppermute(head, axis, [((i + 1) % count, i) for i in range(ends)]),
            ],
            axis=dim,
        )
    return cells


def expand_roots(roots):
    coefficients = [complex(1.0, 0.0)]
    for root in roots:
        widened = coefficients + [complex(0.0, 0.0)]
        for position in range(1, len(widened)):
            widened[position] = widened[position] - root * coefficients[position - 1]
        coefficients = widened
    return [coefficient.real for coefficient in coefficients]


def horner_value(coefficients, point):
    running = complex(0.0, 0.0)
    for coefficient in coefficients:
        running = running * point + coefficient
    return running


def derive_coeffs(coefficients):
    degree = len(coefficients) - 1
    return [coefficients[position] * (degree - position) for position in range(degree)]


def filter_design():
    low_edge = 1.0 / 12.9
    high_edge = 1.0 / 12.0
    warped_low = 2.0 * math.tan(math.pi * low_edge)
    warped_high = 2.0 * math.tan(math.pi * high_edge)
    centre = math.sqrt(warped_low * warped_high)
    spread = warped_high - warped_low
    digital = []
    for octant in (3, 5):
        proto = complex(math.cos(octant * math.pi / 4.0), math.sin(octant * math.pi / 4.0)) * spread
        radical = (proto * proto - 4.0 * centre * centre) ** 0.5
        for analog in ((proto + radical) / 2.0, (proto - radical) / 2.0):
            digital.append((2.0 + analog) / (2.0 - analog))
    denom = expand_roots(digital)
    numer = [1.0, 0.0, -2.0, 0.0, 1.0]
    omega = 2.0 * math.atan(centre / 2.0)
    zcentre = complex(math.cos(omega), math.sin(omega))
    respond = horner_value(numer, zcentre) / horner_value(denom, zcentre)
    numer = [coefficient / abs(respond) for coefficient in numer]
    remain = [numer[position] - numer[0] * denom[position] for position in range(1, 5)]
    slope = derive_coeffs(denom)
    amat = np.zeros((4, 4))
    bvec = np.zeros(4)
    cvec = np.zeros(4)
    upper = [pole for pole in digital if pole.imag > 0]
    for index, pole in enumerate(upper):
        resid = horner_value(remain, pole) / horner_value(slope, pole)
        first = 2 * index
        amat[first, first] = pole.real
        amat[first, first + 1] = -pole.imag
        amat[first + 1, first] = pole.imag
        amat[first + 1, first + 1] = pole.real
        bvec[first] = 1.0
        cvec[first] = 2.0 * resid.real
        cvec[first + 1] = -2.0 * resid.imag
    return (amat, bvec, cvec, float(numer[0]))


def block_tables(length):
    amat, bvec, cvec, direct = filter_design()
    powers = [np.eye(4)]
    for step in range(length):
        powers.append(powers[-1] @ amat)
    impulse = [direct] + [float(cvec @ powers[step - 1] @ bvec) for step in range(1, length)]
    toeplitz = np.zeros((length, length))
    for row in range(length):
        for column in range(row + 1):
            toeplitz[row, column] = impulse[row - column]
    ending = np.stack([powers[length - 1 - column] @ bvec for column in range(length)], axis=1)
    entering = np.stack([cvec @ powers[row] for row in range(length)], axis=0)
    tables = (toeplitz, ending, entering, powers[length])
    return tuple((jnp.asarray(table, jnp.float32) for table in tables))


def join_blocks(earlier, later):
    jump = jnp.einsum("nij,njl->nil", later[0], earlier[0], precision=lax.Precision.HIGHEST)
    state = (
        jnp.einsum("nij,nkjc->nkic", later[0], earlier[1], precision=lax.Precision.HIGHEST)
        + later[1]
    )
    return (jump, state)


def carried_states(jumps, leaving):
    summed = lax.associative_scan(join_blocks, (jumps, leaving), axis=0)[1]
    return jnp.concatenate([jnp.zeros_like(summed[:1]), summed[:-1]], axis=0)


def whole_filter(series):
    count, total, cells = series.shape
    blocks = total // BLOCK
    toeplitz, ending, entering, jump = block_tables(BLOCK)
    high = lax.Precision.HIGHEST
    jumps = jnp.broadcast_to(jump, (blocks, 4, 4))
    pieces = series.reshape(count, blocks, BLOCK, cells)
    forward = jnp.einsum("ts,knsc->kntc", toeplitz, pieces, precision=high)
    leaving = jnp.einsum("js,knsc->nkjc", ending, pieces, precision=high)
    arriving = carried_states(jumps, leaving)
    forward = forward + jnp.einsum("tj,nkjc->kntc", entering, arriving, precision=high)
    banded = jnp.einsum("ts,knsc->kntc", toeplitz[::-1, ::-1], forward, precision=high)
    leaving = jnp.einsum("js,knsc->nkjc", ending[:, ::-1], forward, precision=high)
    arriving = carried_states(jumps, leaving[::-1])[::-1]
    banded = banded + jnp.einsum("tj,nkjc->kntc", entering[::-1, :], arriving, precision=high)
    return banded.reshape(count, total, cells)


def baroclinic(east_band, north_band, rho, levels):
    level_float = levels.astype(jnp.float32)
    depth = (level_float + level_float * level_float / 90.0) / 90.0
    press = [rho[0] * depth[0]]
    for level in range(1, rho.shape[0]):
        press.append(
            press[-1] + 0.5 * (rho[level - 1] + rho[level]) * (depth[level] - depth[level - 1])
        )
    press = jnp.stack(press)
    press = press - jnp.mean(press, axis=0, keepdims=True)
    east = east_band - jnp.mean(east_band, axis=0, keepdims=True)
    north = north_band - jnp.mean(north_band, axis=0, keepdims=True)
    return (east, north, press)


def on_device(u_vel, v_vel, density, land_mask, start_hour, levels):
    depth_count, hours, rows, columns = u_vel.shape
    first = lax.axis_index("tm") * hours
    moments = first + jnp.arange(hours, dtype=jnp.int32)
    live = ((moments[:, None, None] >= start_hour[None]) & (land_mask[None] == 1)).astype(
        jnp.float32
    )
    flat = [
        (field * live[None]).reshape(depth_count, hours, rows * columns)
        for field in (u_vel, v_vel, density)
    ]
    gathered = (
        lax.all_to_all(flat[0], "tm", split_axis=2, concat_axis=1, tiled=True),
        lax.all_to_all(flat[1], "tm", split_axis=2, concat_axis=1, tiled=True),
        lax.all_to_all(flat[2], "tm", split_axis=2, concat_axis=1, tiled=True),
    )
    banded = [whole_filter(series) for series in gathered]
    east, north, press = baroclinic(banded[0], banded[1], banded[2], levels)
    east, north, press = (
        lax.all_to_all(east, "tm", split_axis=1, concat_axis=2, tiled=True),
        lax.all_to_all(north, "tm", split_axis=1, concat_axis=2, tiled=True),
        lax.all_to_all(press, "tm", split_axis=1, concat_axis=2, tiled=True),
    )
    shape = (depth_count, hours, rows, columns)
    east = east.reshape(shape)
    north = north.reshape(shape)
    pressure = press.reshape(shape)
    east_flux = east * pressure
    north_flux = north * pressure
    edges = jnp.concatenate([east_flux[..., :1], east_flux[..., -1:]], axis=3)
    outside = extended(edges, (("col", 3),), 1)
    east_next = jnp.concatenate([east_flux[..., 1:], outside[..., 3:4]], axis=3)
    east_prev = jnp.concatenate([outside[..., 0:1], east_flux[..., :-1]], axis=3)
    empty_row = jnp.zeros((depth_count, hours, 1, columns), jnp.float32)
    north_next = jnp.concatenate([north_flux[:, :, 1:, :], empty_row], axis=2)
    north_prev = jnp.concatenate([empty_row, north_flux[:, :, :-1, :]], axis=2)
    spread = 0.5 * (east_next - east_prev) + 0.5 * (north_next - north_prev)
    flux_div = spread * land_mask.astype(jnp.float32)[None, None]
    return (pressure, flux_div)


def solution(mesh):
    return jax.shard_map(
        on_device,
        mesh=mesh,
        in_specs=(
            P(None, "tm", None, "col"),
            P(None, "tm", None, "col"),
            P(None, "tm", None, "col"),
            P(None, "col"),
            P(None, "col"),
            P(),
        ),
        out_specs=(P(None, "tm", None, "col"), P(None, "tm", None, "col")),
        check_vma=False,
    )
```

profile of v0, /device:TPU:449, one launch (start us, length us, event | category | flops | bytes accessed | tf_op | source)
XLA Modules:
  0.0 406.4 jit_solution(1380748073847091141)
XLA Ops:
  6.3 13.2 %all-to-all-start.2 = ((f32[64,1,1024]{2,1,0:T(1,128)}), f32[64,1,1024]{2,1,0:T(1,128)S(1)}, u32[]{:S(2)}, u32[]{:S(2)}) async-start(f32[64,1,1024]{2,1,0:T(1,128)} %reshape.363), calls=%async_computation.2 | async-start | bytes 524288 | tf_op jit(solution)/shard_map/all_to_all | solution.py:164
  20.2 2.3 reshape.367
  23.3 2.3 reshape.359
  30.4 3.6 all-to-all-done.2
  34.0 11.5 %all-to-all-start.4 = ((f32[64,1,1024]{2,1,0:T(1,128)}), f32[64,1,1024]{2,1,0:T(1,128)S(1)}, u32[]{:S(2)}, u32[]{:S(2)}) async-start(f32[64,1,1024]{2,1,0:T(1,128)} %reshape.367), calls=%async_computation.4 | async-start | bytes 524288 | tf_op jit(solution)/shard_map/all_to_all | solution.py:165
  47.4 2.8 reshape.364
  50.2 2.8 copy.529
  53.7 3.7 convolution_bitcast_fusion.15
  64.6 5.2 %pad.177 = f32[4,4,4,16]{0,2,3,1:T(4,128)S(1)} pad(f32[2,4,4,16]{0,2,3,1:T(4,128)S(1)} %pad_add_fusion.1, f32[]{:T(128)} %constant.30.clone.1), padding=1_0_1x0_0_0x0_0_0x0_0_0 | pad | bytes 6148 | tf_op jit(solution)/shard_map/pad | solution.py:115
  70.1 5.2 %pad.176 = f32[4,4,4,16]{0,2,3,1:T(4,128)S(1)} pad(f32[2,4,4,16]{0,2,3,1:T(4,128)S(1)} %pad_maximum_fusion.3, f32[]{:T(128)} %constant.30.clone.1), padding=0_1_1x0_0_0x0_0_0x0_0_0 | pad | bytes 6148 | tf_op jit(solution)/shard_map/pad | solution.py:115
  76.1 5.3 %pad.178 = f32[8,4,4,16]{0,2,3,1:T(4,128)S(1)} pad(f32[4,4,4,16]{0,2,3,1:T(4,128)S(1)} %pad_maximum_fusion.4, f32[]{:T(128)} %constant.30.clone.1), padding=0_1_1x0_0_0x0_0_0x0_0_0 | pad | bytes 12292 | tf_op jit(solution)/shard_map/pad | solution.py:115
  81.4 5.4 %pad.179 = f32[8,4,4,16]{0,2,3,1:T(4,128)S(1)} pad(f32[4,4,4,16]{0,2,3,1:T(4,128)S(1)} %add.505, f32[]{:T(128)} %constant.30.clone.1), padding=1_0_1x0_0_0x0_0_0x0_0_0 | pad | bytes 12292 | tf_op jit(solution)/shard_map/pad | solution.py:115
  87.6 5.7 %pad.362 = f32[16,4,4,16]{0,2,3,1:T(4,128)S(1)} pad(f32[8,4,4,16]{0,2,3,1:T(4,128)S(1)} %add.507, f32[]{:T(128)} %constant.30.clone.1), padding=1_0_1x0_0_0x0_0_0x0_0_0 | pad | bytes 24580
  94.1 5.6 %pad.260 = f32[15,4,4,16]{0,2,3,1:T(4,128)S(1)} pad(f32[8,4,4,16]{0,2,3,1:T(4,128)S(1)} %pad_maximum_fusion.5, f32[]{:T(128)} %constant.30.clone.1), padding=0_0_1x0_0_0x0_0_0x0_0_0 | pad | bytes 23556 | tf_op jit(solution)/shard_map/slice | solution.py:116
  101.7 3.7 convolution_bitcast_fusion.14
  108.4 13.4 %all-to-all-start = ((f32[64,1,1024]{2,1,0:T(1,128)}), f32[64,1,1024]{2,1,0:T(1,128)S(1)}, u32[]{:S(2)}, u32[]{:S(2)}) async-start(f32[64,1,1024]{2,1,0:T(1,128)} %reshape.359), calls=%async_computation | async-start | bytes 524288 | tf_op jit(solution)/shard_map/all_to_all | solution.py:166
  124.0 2.8 reshape.368
  126.8 2.8 copy.527
  130.1 4.4 %convolution_bitcast_fusion.13 = f32[16,4,4,16]{0,2,3,1:T(4,128)S(1)} fusion(f32[4,16,64,16]{2,1,3,0:T(8,128)S(1)} %reshape.337, f32[4,64,1,1]{1,0,3,2:T(4,128)} %constant.157), kind=kOutput, calls=%fused_computation.25 | convolution fusion | flops 3145728 | bytes 279552 | tf_op jit(solution)/shard_map/js,knsc->nkjc/dot_general | solution.py:127
  141.1 5.2 %pad.193 = f32[4,4,4,16]{0,2,3,1:T(4,128)S(1)} pad(f32[2,4,4,16]{0,2,3,1:T(4,128)S(1)} %pad_add_fusion, f32[]{:T(128)} %constant.30.clone.1), padding=1_0_1x0_0_0x0_0_0x0_0_0 | pad | bytes 6148 | tf_op jit(solution)/shard_map/pad | solution.py:115
  147.2 5.2 %pad.192 = f32[4,4,4,16]{0,2,3,1:T(4,128)S(1)} pad(f32[2,4,4,16]{0,2,3,1:T(4,128)S(1)} %pad_maximum_fusion.6, f32[]{:T(128)} %constant.30.clone.1), padding=0_1_1x0_0_0x0_0_0x0_0_0 | pad | bytes 6148 | tf_op jit(solution)/shard_map/pad | solution.py:115
  153.2 5.3 %pad.194 = f32[8,4,4,16]{0,2,3,1:T(4,128)S(1)} pad(f32[4,4,4,16]{0,2,3,1:T(4,128)S(1)} %pad_maximum_fusion.7, f32[]{:T(128)} %constant.30.clone.1), padding=0_1_1x0_0_0x0_0_0x0_0_0 | pad | bytes 12292 | tf_op jit(solution)/shard_map/pad | solution.py:115
  158.5 5.4 %pad.195 = f32[8,4,4,16]{0,2,3,1:T(4,128)S(1)} pad(f32[4,4,4,16]{0,2,3,1:T(4,128)S(1)} %add.529, f32[]{:T(128)} %constant.30.clone.1), padding=1_0_1x0_0_0x0_0_0x0_0_0 | pad | bytes 12292 | tf_op jit(solution)/shard_map/pad | solution.py:115
  164.7 5.7 %pad.364 = f32[16,4,4,16]{0,2,3,1:T(4,128)S(1)} pad(f32[8,4,4,16]{0,2,3,1:T(4,128)S(1)} %add.531, f32[]{:T(128)} %constant.30.clone.1), padding=1_0_1x0_0_0x0_0_0x0_0_0 | pad | bytes 24580
  171.2 5.6 %pad.264 = f32[15,4,4,16]{0,2,3,1:T(4,128)S(1)} pad(f32[8,4,4,16]{0,2,3,1:T(4,128)S(1)} %pad_maximum_fusion.8, f32[]{:T(128)} %constant.30.clone.1), padding=0_0_1x0_0_0x0_0_0x0_0_0 | pad | bytes 23556 | tf_op jit(solution)/shard_map/slice | solution.py:116
  178.8 3.7 convolution_bitcast_fusion.12
  186.0 5.4 %pad.187 = f32[8,4,4,16]{3,2,0,1:T(4,128)} pad(f32[4,4,4,16]{3,2,0,1:T(4,128)S(1)} %add.517, f32[]{:T(128)} %constant.30.clone.1), padding=1_0_1x0_0_0x0_0_0x0_0_0 | pad | bytes 12292 | tf_op jit(solution)/shard_map/pad | solution.py:115
  191.6 5.4 %pad.203 = f32[8,4,4,16]{3,2,0,1:T(4,128)} pad(f32[4,4,4,16]{3,2,0,1:T(4,128)S(1)} %add.541, f32[]{:T(128)} %constant.30.clone.1), padding=1_0_1x0_0_0x0_0_0x0_0_0 | pad | bytes 12292 | tf_op jit(solution)/shard_map/pad | solution.py:115
  202.7 2.8 reshape.360
  205.5 2.8 copy.531
  209.0 3.7 convolution_bitcast_fusion.17
  219.3 5.2 %pad.161 = f32[4,4,4,16]{0,2,3,1:T(4,128)S(1)} pad(f32[2,4,4,16]{0,2,3,1:T(4,128)S(1)} %pad_add_fusion.2, f32[]{:T(128)} %constant.30.clone.1), padding=1_0_1x0_0_0x0_0_0x0_0_0 | pad | bytes 6148 | tf_op jit(solution)/shard_map/pad | solution.py:115
  225.4 5.2 %pad.160 = f32[4,4,4,16]{0,2,3,1:T(4,128)S(1)} pad(f32[2,4,4,16]{0,2,3,1:T(4,128)S(1)} %pad_maximum_fusion, f32[]{:T(128)} %constant.30.clone.1), padding=0_1_1x0_0_0x0_0_0x0_0_0 | pad | bytes 6148 | tf_op jit(solution)/shard_map/pad | solution.py:115
  231.4 5.3 %pad.162 = f32[8,4,4,16]{0,2,3,1:T(4,128)S(1)} pad(f32[4,4,4,16]{0,2,3,1:T(4,128)S(1)} %pad_maximum_fusion.1, f32[]{:T(128)} %constant.30.clone.1), padding=0_1_1x0_0_0x0_0_0x0_0_0 | pad | bytes 12292 | tf_op jit(solution)/shard_map/pad | solution.py:115
  236.7 5.4 %pad.163 = f32[8,4,4,16]{0,2,3,1:T(4,128)S(1)} pad(f32[4,4,4,16]{0,2,3,1:T(4,128)S(1)} %add.471, f32[]{:T(128)} %constant.30.clone.1), padding=1_0_1x0_0_0x0_0_0x0_0_0 | pad | bytes 12292 | tf_op jit(solution)/shard_map/pad | solution.py:115
  242.9 5.7 %pad.360 = f32[16,4,4,16]{0,2,3,1:T(4,128)S(1)} pad(f32[8,4,4,16]{0,2,3,1:T(4,128)S(1)} %add.473, f32[]{:T(128)} %constant.30.clone.1), padding=1_0_1x0_0_0x0_0_0x0_0_0 | pad | bytes 24580
  249.4 5.8 %pad.256 = f32[15,4,4,16]{0,2,3,1:T(4,128)S(1)} pad(f32[8,4,4,16]{0,2,3,1:T(4,128)S(1)} %pad_maximum_fusion.2, f32[]{:T(128)} %constant.30.clone.1), padding=0_0_1x0_0_0x0_0_0x0_0_0 | pad | bytes 23556 | tf_op jit(solution)/shard_map/slice | solution.py:116
  257.2 3.7 convolution_bitcast_fusion.16
  269.6 13.6 %all-to-all-start.3 = ((f32[64,1,1024]{2,1,0:T(1,128)}), f32[64,1,1024]{2,1,0:T(1,128)S(1)}, u32[]{:S(2)}, u32[]{:S(2)}) async-start(f32[64,1,1024]{2,1,0:T(1,128)} %reshape.365), calls=%async_computation.3 | async-start | bytes 524288 | tf_op jit(solution)/shard_map/all_to_all | solution.py:171
  297.6 12.5 %all-to-all-start.5 = ((f32[64,1,1024]{2,1,0:T(1,128)}), f32[64,1,1024]{2,1,0:T(1,128)S(1)}, u32[]{:S(2)}, u32[]{:S(2)}) async-start(f32[64,1,1024]{2,1,0:T(1,128)} %reshape.369), calls=%async_computation.5 | async-start | bytes 524288 | tf_op jit(solution)/shard_map/all_to_all | solution.py:172
  316.0 8.6 %all-to-all-done.5 = f32[64,1,1024]{2,1,0:T(1,128)S(1)} async-done(((f32[64,1,1024]{2,1,0:T(1,128)}), f32[64,1,1024]{2,1,0:T(1,128)S(1)}, u32[]{:S(2)}, u32[]{:S(2)}) %all-to-all-start.5) | async-done | bytes 262176 | tf_op jit(solution)/shard_map/all_to_all | solution.py:172
  324.6 11.6 %all-to-all-start.1 = ((f32[64,1,1024]{2,1,0:T(1,128)}), f32[64,1,1024]{2,1,0:T(1,128)S(1)}, u32[]{:S(2)}, u32[]{:S(2)}) async-start(f32[64,1,1024]{2,1,0:T(1,128)} %reshape.361), calls=%async_computation.1 | async-start | bytes 524288 | tf_op jit(solution)/shard_map/all_to_all | solution.py:173
  339.0 2.6 copy.528
  346.5 2.6 copy.526
  354.0 2.6 copy.530
  359.1 8.3 %collective-permute-start = (f32[4,16,8,1]{3,2,1,0:T(8,128)S(1)}, f32[4,16,8,1]{3,2,1,0:T(8,128)S(1)}, u32[]{:S(2)}, u32[]{:S(2)}) collective-permute-start(f32[4,16,8,1]{3,2,1,0:T(8,128)S(1)} %get-tuple-element.14), channel_id=1, source_target_pairs={{1,0},{2,1},{3,2},{4,3},{5,4},{6,5},{7,6},{9,8},{10,9},{11,10},{12... | collective-permute-start | bytes 6152 | tf_op jit(solution)/shard_map/ppermute | solution.py:22
  369.4 20.8 %collective-permute-done = f32[4,16,8,1]{3,2,1,0:T(8,128)S(1)} collective-permute-done((f32[4,16,8,1]{3,2,1,0:T(8,128)S(1)}, f32[4,16,8,1]{3,2,1,0:T(8,128)S(1)}, u32[]{:S(2)}, u32[]{:S(2)}) %collective-permute-start) | collective-permute-done | bytes 2080 | tf_op jit(solution)/shard_map/ppermute | solution.py:22
  390.2 14.9 %collective-permute-done.1 = f32[4,16,8,1]{3,2,1,0:T(8,128)S(1)} collective-permute-done((f32[4,16,8,1]{3,2,1,0:T(8,128)S(1)}, f32[4,16,8,1]{3,2,1,0:T(8,128)S(1)}, u32[]{:S(2)}, u32[]{:S(2)}) %collective-permute-start.1) | collective-permute-done | bytes 2080 | tf_op jit(solution)/shard_map/ppermute | solution.py:20
  (406 shorter events, 107.4 us)
Async XLA Ops:
  6.3 27.7 %all-to-all-start.2 = ((f32[64,1,1024]{2,1,0:T(1,128)}), f32[64,1,1024]{2,1,0:T(1,128)S(1)}, u32[]{:S(2)}, u32[]{:S(2)}) async-start(f32[64,1,1024]{2,1,0:T(1,128)} %reshape.363), calls=%async_computation.2 | async-start | bytes 524288 | tf_op jit(solution)/shard_map/all_to_all | solution.py:164
  22.5 3.0 copy-start.40
  22.5 7.4 %copy-start.16 = (f32[4,4]{1,0:T(4,128)S(1)}, f32[4,4]{1,0:T(4,128)}, u32[]{:S(2)}) copy-start(f32[4,4]{1,0:T(4,128)} %constant.37.clone) | copy-start | bytes 196
  30.3 194.5 %copy-start.6 = (f32[4,4,4]{2,1,0:T(4,128)}, f32[4,4,4]{2,1,0:T(4,128)S(1)}, u32[]{:S(2)}) copy-start(f32[4,4,4]{2,1,0:T(4,128)S(1)} %fusion.84) | copy-start | bytes 772
  30.4 187.6 %copy-start.21 = (f32[4,4,1]{1,0,2:T(4,128)}, f32[4,4,1]{1,0,2:T(4,128)S(1)}, u32[]{:S(2)}) copy-start(f32[4,4,1]{1,0,2:T(4,128)S(1)} %convolution_bitcast_fusion.45) | copy-start | bytes 196
  34.0 73.7 %all-to-all-start.4 = ((f32[64,1,1024]{2,1,0:T(1,128)}), f32[64,1,1024]{2,1,0:T(1,128)S(1)}, u32[]{:S(2)}, u32[]{:S(2)}) async-start(f32[64,1,1024]{2,1,0:T(1,128)} %reshape.367), calls=%async_computation.4 | async-start | bytes 524288 | tf_op jit(solution)/shard_map/all_to_all | solution.py:165
  76.1 23.9 %copy-start.34 = (f32[64,4,1,1]{0,1,2,3:T(4,128)S(1)}, f32[64,4,1,1]{0,1,2,3:T(4,128)}, u32[]{:S(2)}) copy-start(f32[64,4,1,1]{0,1,2,3:T(4,128)} %constant.158) | copy-start | bytes 3076
  86.8 14.2 %copy-start.10 = (f32[64,64,1,1]{1,0,3,2:T(8,128)S(1)}, f32[64,64,1,1]{1,0,3,2:T(8,128)}, u32[]{:S(2)}) copy-start(f32[64,64,1,1]{1,0,3,2:T(8,128)} %constant.156) | copy-start | bytes 49156
  93.7 7.9 %copy-start.31 = (f32[4,64,1,1]{1,0,3,2:T(4,128)S(1)}, f32[4,64,1,1]{1,0,3,2:T(4,128)}, u32[]{:S(2)}) copy-start(f32[4,64,1,1]{1,0,3,2:T(4,128)} %constant.160) | copy-start | bytes 3076
  105.4 3.0 copy-start.5
  105.7 91.3 %copy-start.11 = (f32[8,4,4,16]{3,2,0,1:T(4,128)}, f32[8,4,4,16]{3,2,0,1:T(4,128)S(1)}, u32[]{:S(2)}) copy-start(f32[8,4,4,16]{3,2,0,1:T(4,128)S(1)} %fusion.7) | copy-start | bytes 24580
  106.6 1.8 copy-start.20
  108.4 93.0 %all-to-all-start = ((f32[64,1,1024]{2,1,0:T(1,128)}), f32[64,1,1024]{2,1,0:T(1,128)S(1)}, u32[]{:S(2)}, u32[]{:S(2)}) async-start(f32[64,1,1024]{2,1,0:T(1,128)} %reshape.359), calls=%async_computation | async-start | bytes 524288 | tf_op jit(solution)/shard_map/all_to_all | solution.py:166
  153.2 23.9 %copy-start.35 = (f32[64,4,1,1]{0,1,2,3:T(4,128)S(1)}, f32[64,4,1,1]{0,1,2,3:T(4,128)}, u32[]{:S(2)}) copy-start(f32[64,4,1,1]{0,1,2,3:T(4,128)} %constant.158) | copy-start | bytes 3076
  170.8 7.9 %copy-start.32 = (f32[4,64,1,1]{1,0,3,2:T(4,128)S(1)}, f32[4,64,1,1]{1,0,3,2:T(4,128)}, u32[]{:S(2)}) copy-start(f32[4,64,1,1]{1,0,3,2:T(4,128)} %constant.160) | copy-start | bytes 3076
  176.9 9.0 %slice-start.5 = ((f32[4,4,4,16]{3,2,0,1:T(4,128)}), f32[1,4,4,16]{3,2,0,1:T(4,128)S(1)}, s32[]{:S(2)}) async-start(f32[4,4,4,16]{3,2,0,1:T(4,128)} %copy-done.20), calls=%async_computation.11 | async-start | bytes 16384 | tf_op jit(solution)/shard_map/slice | solution.py:115
  176.9 9.0 %copy-start.26 = (f32[1,4,4,16]{3,2,0,1:T(4,128)S(1)}, f32[1,4,4,16]{3,2,0,1:T(4,128)}, u32[]{:S(2)}) copy-start(f32[1,4,4,16]{3,2,0,1:T(4,128)} %fusion.24) | copy-start | bytes 3076
  178.1 20.6 %copy-start.8 = (f32[64,64,1,1]{1,0,3,2:T(8,128)S(1)}, f32[64,64,1,1]{1,0,3,2:T(8,128)}, u32[]{:S(2)}) copy-start(f32[64,64,1,1]{1,0,3,2:T(8,128)} %constant.159) | copy-start | bytes 49156
  231.4 24.1 %copy-start.36 = (f32[64,4,1,1]{0,1,2,3:T(4,128)S(1)}, f32[64,4,1,1]{0,1,2,3:T(4,128)}, u32[]{:S(2)}) copy-start(f32[64,4,1,1]{0,1,2,3:T(4,128)} %constant.158) | copy-start | bytes 3076
  249.0 8.2 %copy-start.33 = (f32[4,64,1,1]{1,0,3,2:T(4,128)S(1)}, f32[4,64,1,1]{1,0,3,2:T(4,128)}, u32[]{:S(2)}) copy-start(f32[4,64,1,1]{1,0,3,2:T(4,128)} %constant.160) | copy-start | bytes 3076
  255.2 5.9 %copy-start.17 = (f32[4,4]{1,0:T(4,128)S(1)}, f32[4,4]{1,0:T(4,128)}, u32[]{:S(2)}) copy-start(f32[4,4]{1,0:T(4,128)} %constant.37.clone) | copy-start | bytes 196
  255.2 6.3 %copy-start.7 = (f32[4,4,4]{2,1,0:T(4,128)S(1)}, f32[4,4,4]{2,1,0:T(4,128)}, u32[]{:S(2)}) copy-start(f32[4,4,4]{2,1,0:T(4,128)} %copy-done.6) | copy-start | bytes 772
  255.2 6.5 %copy-start.22 = (f32[4,4,1]{1,0,2:T(4,128)S(1)}, f32[4,4,1]{1,0,2:T(4,128)}, u32[]{:S(2)}) copy-start(f32[4,4,1]{1,0,2:T(4,128)} %copy-done.21) | copy-start | bytes 196
  255.2 8.0 %slice-start.2 = ((f32[8,4,4,16]{3,2,0,1:T(4,128)}), f32[1,4,4,16]{3,2,0,1:T(4,128)S(1)}, s32[]{:S(2)}) async-start(f32[8,4,4,16]{3,2,0,1:T(4,128)} %copy-done.11), calls=%async_computation.8 | async-start | bytes 16384 | tf_op jit(solution)/shard_map/slice | solution.py:115
  255.3 8.0 %copy-start.23 = (f32[3,4,4,16]{3,2,0,1:T(4,128)S(1)}, f32[3,4,4,16]{3,2,0,1:T(4,128)}, u32[]{:S(2)}) copy-start(f32[3,4,4,16]{3,2,0,1:T(4,128)} %fusion.16) | copy-start | bytes 9220
  255.3 8.2 %copy-start.15 = (f32[7,4,4,16]{3,2,0,1:T(4,128)S(1)}, f32[7,4,4,16]{3,2,0,1:T(4,128)}, u32[]{:S(2)}) copy-start(f32[7,4,4,16]{3,2,0,1:T(4,128)} %slice.651) | copy-start | bytes 21508
  255.5 8.0 %copy-start.12 = (f32[8,4,4,16]{3,2,0,1:T(4,128)S(1)}, f32[8,4,4,16]{3,2,0,1:T(4,128)}, u32[]{:S(2)}) copy-start(f32[8,4,4,16]{3,2,0,1:T(4,128)} %pad.187) | copy-start | bytes 24580
  256.5 7.8 %slice-start.1 = ((f32[16,4,4,16]{3,2,0,1:T(4,128)}), f32[1,4,4,16]{3,2,0,1:T(4,128)S(1)}, s32[]{:S(2)}) async-start(f32[16,4,4,16]{3,2,0,1:T(4,128)} %copy-done.5), calls=%async_computation.7 | async-start | bytes 16384 | tf_op jit(solution)/shard_map/slice | solution.py:115
  257.2 7.7 %copy-start.1 = (f32[4,16,64,16]{2,3,1,0:T(8,128)S(1)}, f32[4,16,64,16]{2,3,1,0:T(8,128)}, u32[]{:S(2)}) copy-start(f32[4,16,64,16]{2,3,1,0:T(8,128)} %convolution_bitcast_fusion.4) | copy-start | bytes 786436
  257.2 7.7 %copy-start.28 = (f32[64,4,1,1]{0,1,2,3:T(4,128)S(1)}, f32[64,4,1,1]{0,1,2,3:T(4,128)}, u32[]{:S(2)}) copy-start(f32[64,4,1,1]{0,1,2,3:T(4,128)} %constant.161) | copy-start | bytes 3076
  260.9 30.6 %copy-start.4 = (f32[16,4,4,16]{3,2,0,1:T(4,128)}, f32[16,4,4,16]{3,2,0,1:T(4,128)S(1)}, u32[]{:S(2)}) copy-start(f32[16,4,4,16]{3,2,0,1:T(4,128)S(1)} %convolution_bitcast_fusion.16) | copy-start | bytes 49156
  261.3 2.1 copy-start.13
  267.3 21.3 %copy-start = (f32[4,16,64,16]{2,3,1,0:T(8,128)S(1)}, f32[4,16,64,16]{2,3,1,0:T(8,128)}, u32[]{:S(2)}) copy-start(f32[4,16,64,16]{2,3,1,0:T(8,128)} %convolution_bitcast_fusion.1) | copy-start | bytes 786436
  269.6 19.0 %copy-start.29 = (f32[64,4,1,1]{0,1,2,3:T(4,128)S(1)}, f32[64,4,1,1]{0,1,2,3:T(4,128)}, u32[]{:S(2)}) copy-start(f32[64,4,1,1]{0,1,2,3:T(4,128)} %constant.161) | copy-start | bytes 3076
  269.6 28.0 %all-to-all-start.3 = ((f32[64,1,1024]{2,1,0:T(1,128)}), f32[64,1,1024]{2,1,0:T(1,128)S(1)}, u32[]{:S(2)}, u32[]{:S(2)}) async-start(f32[64,1,1024]{2,1,0:T(1,128)} %reshape.365), calls=%async_computation.3 | async-start | bytes 524288 | tf_op jit(solution)/shard_map/all_to_all | solution.py:171
  288.6 1.9 copy-start.14
  291.5 3.2 slice-start.3
  291.5 3.2 copy-start.24
  292.4 3.0 copy-start.18
  292.4 3.3 slice-start
  292.4 3.9 copy-start.9
  294.7 15.4 %copy-start.30 = (f32[64,4,1,1]{0,1,2,3:T(4,128)S(1)}, f32[64,4,1,1]{0,1,2,3:T(4,128)}, u32[]{:S(2)}) copy-start(f32[64,4,1,1]{0,1,2,3:T(4,128)} %constant.161) | copy-start | bytes 3076
  297.6 27.0 %all-to-all-start.5 = ((f32[64,1,1024]{2,1,0:T(1,128)}), f32[64,1,1024]{2,1,0:T(1,128)S(1)}, u32[]{:S(2)}, u32[]{:S(2)}) async-start(f32[64,1,1024]{2,1,0:T(1,128)} %reshape.369), calls=%async_computation.5 | async-start | bytes 524288 | tf_op jit(solution)/shard_map/all_to_all | solution.py:172
  312.9 23.4 %copy-start.39 = (s32[8,128]{1,0:T(8,128)S(1)}, s32[8,128]{1,0:T(8,128)}, u32[]{:S(2)}) copy-start(s32[8,128]{1,0:T(8,128)} %param.21) | copy-start | bytes 12292
  324.6 26.7 %all-to-all-start.1 = ((f32[64,1,1024]{2,1,0:T(1,128)}), f32[64,1,1024]{2,1,0:T(1,128)S(1)}, u32[]{:S(2)}, u32[]{:S(2)}) async-start(f32[64,1,1024]{2,1,0:T(1,128)} %reshape.361), calls=%async_computation.1 | async-start | bytes 524288 | tf_op jit(solution)/shard_map/all_to_all | solution.py:173
  358.8 10.6 %copy-start.2 = (f32[4,16,8,128]{3,2,1,0:T(8,128)}, f32[4,16,8,128]{3,2,1,0:T(8,128)S(1)}, u32[]{:S(2)}) copy-start(f32[4,16,8,128]{3,2,1,0:T(8,128)S(1)} %reshape.325) | copy-start | bytes 786436
  359.1 31.0 %collective-permute-start = (f32[4,16,8,1]{3,2,1,0:T(8,128)S(1)}, f32[4,16,8,1]{3,2,1,0:T(8,128)S(1)}, u32[]{:S(2)}, u32[]{:S(2)}) collective-permute-start(f32[4,16,8,1]{3,2,1,0:T(8,128)S(1)} %get-tuple-element.14), channel_id=1, source_target_pairs={{1,0},{2,1},{3,2},{4,3},{5,4},{6,5},{7,6},{9,8},{10,9},{11,10},{12... | collective-permute-start | bytes 6152 | tf_op jit(solution)/shard_map/ppermute | solution.py:22
  367.4 37.7 %collective-permute-start.1 = (f32[4,16,8,1]{3,2,1,0:T(8,128)S(1)}, f32[4,16,8,1]{3,2,1,0:T(8,128)S(1)}, u32[]{:S(2)}, u32[]{:S(2)}) collective-permute-start(f32[4,16,8,1]{3,2,1,0:T(8,128)S(1)} %get-tuple-element.13), channel_id=1, source_target_pairs={{0,1},{1,2},{2,3},{3,4},{4,5},{5,6},{6,7},{8,9},{9,10},{10,11},{11... | collective-permute-start | bytes 6152 | tf_op jit(solution)/shard_map/ppermute | solution.py:20
  (7 other events, 8.9 us)
where the time goes:
time: 414 us; the launch traced here: 406 us
  local copies, waits for them, and re-layouts  197 us (48%)
  starting transfers between devices  85.9 us (21%)
  waiting for transfers between devices  48.6 us (12%)
  matrix products  47.1 us (11%)
  other arithmetic  20.4 us (5%)
  between operations  6.84 us (2%)
    pad x24, local copies, waits for them, and re-layouts, carried_states(): summed = lax.associative_scan(join_blocks, (jumps, leaving), axis=0)[1]  75.8 us
    unnamed x103, local copies, waits for them, and re-layouts  46.6 us
    ppermute x1, waiting for transfers between devices, extended(): lax.ppermute(head, axis, [((i + 1) % count, i) for i in range(ends)])  20.8 us
    slice x78, local copies, waits for them, and re-layouts, carried_states(): summed = lax.associative_scan(join_blocks, (jumps, leaving), axis=0)[1]  20.7 us
    slice x6, local copies, waits for them, and re-layouts, carried_states(): return jnp.concatenate([jnp.zeros_like(summed[:1]), summed[:-1]], axis=0)  18.3 us
    ppermute x1, waiting for transfers between devices, extended(): lax.ppermute(tail, axis, [(i, (i + 1) % count) for i in range(ends)])  14.9 us
    all_to_all x1, starting transfers between devices, on_device(): lax.all_to_all(east, 'tm', split_axis=1, concat_axis=2, tiled=True)  13.6 us
    all_to_all x1, starting transfers between devices, on_device(): lax.all_to_all(flat[2], 'tm', split_axis=2, concat_axis=1, tiled=True)  13.4 us
  transfers between devices with their start and end apart: 8, of which 5 were waited for; matrix products, arithmetic and copies ran while one was open for 45% of the time, Pallas kernels for 0%

commit v1 on v0

v1 whole, which is shorter than its diff:
```python
import functools
import math

import jax
import jax.numpy as jnp
import numpy as np
from jax import lax
from jax.experimental import pallas as pl
from jax.experimental.pallas import tpu as pltpu
from jax.sharding import PartitionSpec as P

HOURS = 16
GROUP = 8
RUNS = 8
SERIES = 9
PAIRS = 5
ROWS = 8
LANES = 128
HIGH = lax.Precision.HIGHEST


def expand_roots(roots):
    coefficients = [complex(1.0, 0.0)]
    for root in roots:
        widened = coefficients + [complex(0.0, 0.0)]
        for position in range(1, len(widened)):
            widened[position] = widened[position] - root * coefficients[position - 1]
        coefficients = widened
    return [coefficient.real for coefficient in coefficients]


def horner_value(coefficients, point):
    running = complex(0.0, 0.0)
    for coefficient in coefficients:
        running = running * point + coefficient
    return running


def derive_coeffs(coefficients):
    degree = len(coefficients) - 1
    return [coefficients[position] * (degree - position) for position in range(degree)]


def filter_design():
    low_edge = 1.0 / 12.9
    high_edge = 1.0 / 12.0
    warped_low = 2.0 * math.tan(math.pi * low_edge)
    warped_high = 2.0 * math.tan(math.pi * high_edge)
    centre = math.sqrt(warped_low * warped_high)
    spread = warped_high - warped_low
    digital = []
    for octant in (3, 5):
        proto = complex(math.cos(octant * math.pi / 4.0), math.sin(octant * math.pi / 4.0)) * spread
        radical = (proto * proto - 4.0 * centre * centre) ** 0.5
        for analog in ((proto + radical) / 2.0, (proto - radical) / 2.0):
            digital.append((2.0 + analog) / (2.0 - analog))
    denom = expand_roots(digital)
    numer = [1.0, 0.0, -2.0, 0.0, 1.0]
    omega = 2.0 * math.atan(centre / 2.0)
    zcentre = complex(math.cos(omega), math.sin(omega))
    respond = horner_value(numer, zcentre) / horner_value(denom, zcentre)
    numer = [coefficient / abs(respond) for coefficient in numer]
    remain = [numer[position] - numer[0] * denom[position] for position in range(1, 5)]
    slope = derive_coeffs(denom)
    amat = np.zeros((4, 4))
    bvec = np.zeros(4)
    cvec = np.zeros(4)
    upper = [pole for pole in digital if pole.imag > 0]
    for index, pole in enumerate(upper):
        resid = horner_value(remain, pole) / horner_value(slope, pole)
        first = 2 * index
        amat[first, first] = pole.real
        amat[first, first + 1] = -pole.imag
        amat[first + 1, first] = pole.imag
        amat[first + 1, first + 1] = pole.real
        bvec[first] = 1.0
        cvec[first] = 2.0 * resid.real
        cvec[first + 1] = -2.0 * resid.imag
    return (amat, bvec, cvec, float(numer[0]))


def power(matrix, exponent):
    return np.linalg.matrix_power(matrix, exponent)


@functools.lru_cache(maxsize=None)
def plan():
    amat, bvec, cvec, direct = filter_design()
    n = HOURS
    impulse = [direct] + [float(cvec @ power(amat, step - 1) @ bvec) for step in range(1, n)]
    toeplitz = np.array([[impulse[row - col] if col <= row else 0.0 for col in range(n)] for row in range(n)])
    left = np.stack([power(amat, n - 1 - hour) @ bvec for hour in range(n)], axis=1)
    entering = np.stack([cvec @ power(amat, hour) for hour in range(n)], axis=0)
    back = np.stack([power(amat, hour) @ bvec for hour in range(n)], axis=1)
    summary = np.concatenate([left, back @ toeplitz], axis=0)
    coupling = back @ entering
    step = power(amat, n)
    width = GROUP * 8 + 8
    forward = np.zeros((GROUP + 1, 4, width))
    forward[0][:, GROUP * 8 : GROUP * 8 + 4] = np.eye(4)
    for j in range(GROUP):
        forward[j + 1] = step @ forward[j]
        forward[j + 1][:, j * 8 : j * 8 + 4] += np.eye(4)
    backward = np.zeros((GROUP + 1, 4, width))
    backward[GROUP][:, GROUP * 8 + 4 :] = np.eye(4)
    for j in reversed(range(GROUP)):
        backward[j] = step @ backward[j + 1] + coupling @ forward[j]
        backward[j][:, j * 8 + 4 : j * 8 + 8] += np.eye(4)
    own = GROUP * 8
    inner = np.zeros((GROUP * 8, width))
    for j in range(GROUP):
        inner[j * 8 : j * 8 + 4] = forward[j]
        inner[j * 8 + 4 : j * 8 + 8] = backward[j + 1]
    run_left = forward[GROUP][:, :own]
    run_right = backward[0][:, :own]
    run_coupling = backward[0][:, own : own + 4]
    run_step = power(step, GROUP)
    suffix = [np.zeros((4, 4))]
    for m in range(RUNS):
        suffix.append(suffix[-1] + power(run_step, m) @ run_coupling @ power(run_step, m))
    pair = 2 * own
    send = np.zeros((RUNS, 16, pair))
    gather = np.zeros((RUNS, 16, RUNS * 8))
    local = np.zeros((RUNS, 16, pair))
    for z in range(RUNS):
        after = suffix[RUNS - 1 - z]
        right = run_right + run_step @ after @ run_left
        for m in range(2):
            send[z, 4 * m : 4 * m + 4, m * own : (m + 1) * own] = run_left
            send[z, 8 + 4 * m : 12 + 4 * m, m * own : (m + 1) * own] = right
            local[z, 8 + 4 * m : 12 + 4 * m, m * own : (m + 1) * own] = after @ run_left
            for other in range(RUNS):
                here = slice(other * 8 + 4 * m, other * 8 + 4 * m + 4)
                if other < z:
                    came = power(run_step, z - 1 - other)
                    gather[z, 4 * m : 4 * m + 4, here] = came
                    gather[z, 8 + 4 * m : 12 + 4 * m, here] = after @ run_step @ came
                if other > z:
                    gather[z, 8 + 4 * m : 12 + 4 * m, here] = power(run_step, other - z - 1)
    spread = np.zeros((pair, pair))
    inject = np.zeros((pair, 16))
    for m in range(2):
        rows = slice(m * own, (m + 1) * own)
        spread[rows, rows] = inner[:, :own]
        inject[rows, 4 * m : 4 * m + 4] = inner[:, own : own + 4]
        inject[rows, 8 + 4 * m : 12 + 4 * m] = inner[:, own + 4 :]
    single = np.float32
    return {
        "amat": amat,
        "cvec": cvec,
        "direct": direct,
        "summary": summary,
        "send": send.astype(single),
        "gather": gather.astype(single),
        "local": local.astype(single),
        "spread": spread.astype(single),
        "inject": inject.astype(single),
    }


def live_hours(mask, start):
    first = lax.axis_index("tm") * HOURS
    ocean = mask == 1
    return [jnp.where(ocean & (start <= first + hour), 1.0, 0.0) for hour in range(HOURS)]


def depths(levels_ref):
    out = []
    for level in range(4):
        number = jnp.full((ROWS, LANES), levels_ref[level], jnp.int32).astype(jnp.float32)
        out.append((number + number * number / 90.0) / 90.0)
    return out


def anomalies(field, live):
    mean = 0.25 * ((field[0] + field[1]) + (field[2] + field[3]))
    return [(field[level] - mean) * live for level in range(3)]


def pressures(rho, depth):
    press = [rho[0] * depth[0]]
    for level in range(1, 4):
        press.append(press[-1] + 0.5 * (rho[level - 1] + rho[level]) * (depth[level] - depth[level - 1]))
    return press


def summary_kernel(levels_ref, u_ref, v_ref, rho_ref, mask_ref, start_ref, out_ref):
    summary = plan()["summary"]
    live = live_hours(mask_ref[...], start_ref[...])
    depth = depths(levels_ref)
    for which, ref in enumerate((u_ref, v_ref, rho_ref)):
        sums = [[None] * 8 for _ in range(3)]
        for hour in range(HOURS):
            field = [ref[level, hour] for level in range(4)]
            if which == 2:
                field = pressures(field, depth)
            for level, value in enumerate(anomalies(field, live[hour])):
                for k in range(8):
                    term = float(summary[k, hour]) * value
                    sums[level][k] = term if hour == 0 else sums[level][k] + term
        for level in range(3):
            for k in range(8):
                row = (which * 3 + level) * 8 + k
                out_ref[pl.ds(row, ROWS, stride=SERIES * 8), :] = sums[level][k]


def paired(ref):
    empty = jnp.zeros((8, LANES), jnp.float32)
    columns = []
    for q in range(PAIRS):
        parts = []
        for m in range(2):
            s = 2 * q + m
            for j in range(GROUP):
                parts.append(ref[j, pl.ds(s * 8, 8), :] if s < SERIES else empty)
        columns.append(jnp.concatenate(parts, axis=0))
    return jnp.concatenate(columns, axis=1)


def dot(lhs, rhs):
    return jnp.dot(lhs, rhs, precision=HIGH, preferred_element_type=jnp.float32)


def run_kernel(in_ref, send_ref, out_ref):
    z = lax.axis_index("tm") // GROUP
    totals = dot(send_ref[z], paired(in_ref))
    for other in range(RUNS):
        later = other > z
        for q in range(PAIRS):
            lanes = slice(q * LANES, (q + 1) * LANES)
            out_ref[other, pl.ds(q * 8, 8), :] = jnp.where(later, totals[0:8, lanes], totals[8:16, lanes])


def border_kernel(in_ref, runs_ref, gather_ref, local_ref, spread_ref, inject_ref, out_ref):
    z = lax.axis_index("tm") // GROUP
    blocks = paired(in_ref)
    runs = jnp.concatenate(
        [
            jnp.concatenate([runs_ref[other, pl.ds(q * 8, 8), :] for other in range(RUNS)], axis=0)
            for q in range(PAIRS)
        ],
        axis=1,
    )
    states = dot(gather_ref[z], runs) + dot(local_ref[z], blocks)
    borders = dot(spread_ref[...], blocks) + dot(inject_ref[...], states)
    for s in range(SERIES):
        q, m = s // 2, s % 2
        for j in range(GROUP):
            row = m * GROUP * 8 + j * 8
            out_ref[j, pl.ds(s * 8, 8), :] = borders[row : row + 8, q * LANES : (q + 1) * LANES]


def filter_steps(state, samples):
    amat, cvec, direct = plan()["amat"], plan()["cvec"], plan()["direct"]
    out = []
    for sample in samples:
        value = direct * sample
        for k in range(4):
            value = value + float(cvec[k]) * state[k]
        out.append(value)
        fresh = []
        for first in (0, 2):
            real, imag = float(amat[first, first]), float(amat[first + 1, first])
            fresh.append((real * state[first] - imag * state[first + 1]) + sample)
            fresh.append(imag * state[first] + real * state[first + 1])
        state = fresh
    return out


def band_kernel(
    levels_ref, u_ref, v_ref, rho_ref, mask_ref, start_ref, borders_ref, press_ref, flux_ref, edge_ref, held, east, north
):
    mask = mask_ref[...]
    start = start_ref[...]
    live = live_hours(mask, start)
    depth = depths(levels_ref)
    for which, ref in ((2, rho_ref), (0, u_ref), (1, v_ref)):
        for hour in range(HOURS):
            field = [ref[level, hour] for level in range(4)]
            if which == 2:
                field = pressures(field, depth)
            for level, value in enumerate(anomalies(field, live[hour])):
                held[level, hour] = value
        target = (east, north, press_ref)[which]
        for level in range(3):
            states = [
                borders_ref[pl.ds((which * 3 + level) * 8 + k, ROWS, stride=SERIES * 8), :] for k in range(8)
            ]
            samples = filter_steps(states[:4], [held[level, hour] for hour in range(HOURS)])
            samples = filter_steps(states[4:], samples[::-1])[::-1]
            for hour in range(HOURS):
                target[level, hour] = samples[hour]
    lane = lax.broadcasted_iota(jnp.int32, (ROWS, LANES), 1)
    row = lax.broadcasted_iota(jnp.int32, (ROWS, LANES), 0)
    half = 0.5 * mask.astype(jnp.float32)
    last = lane == LANES - 1
    edges = jnp.zeros((ROWS, LANES), jnp.float32)
    for hour in range(HOURS):
        u_all = [east[level, hour] for level in range(3)]
        v_all = [north[level, hour] for level in range(3)]
        p_all = [press_ref[level, hour] for level in range(3)]
        for values in (u_all, v_all, p_all):
            values.append(-((values[0] + values[1]) + values[2]))
        press_ref[3, hour] = p_all[3]
        for level in range(4):
            fx = u_all[level] * p_all[level]
            fy = v_all[level] * p_all[level]
            position = 2 * (level * HOURS + hour)
            turned = pltpu.roll(fx, (position + 1) % LANES, 1)
            edges = jnp.where((lane == position) | (lane == position + 1), turned, edges)
            along_x = jnp.where(last, 0.0, pltpu.roll(fx, LANES - 1, 1)) - jnp.where(
                lane == 0, 0.0, pltpu.roll(fx, 1, 1)
            )
            along_y = jnp.where(row == ROWS - 1, 0.0, pltpu.roll(fy, ROWS - 1, 0)) - jnp.where(
                row == 0, 0.0, pltpu.roll(fy, 1, 0)
            )
            flux_ref[level, hour] = half * (along_x + along_y)
    edge_ref[...] = edges


def seam_kernel(flux_ref, mask_ref, west_ref, east_ref, out_ref):
    lane = lax.broadcasted_iota(jnp.int32, (ROWS, LANES), 1)
    half = 0.5 * mask_ref[...].astype(jnp.float32)
    weight = jnp.where(lane == LANES - 1, half, jnp.where(lane == 0, -half, 0.0))
    halo = jnp.where(
        lane % 2 == 0, pltpu.roll(east_ref[...], LANES - 1, 1), pltpu.roll(west_ref[...], 1, 1)
    )
    for level in range(4):
        for hour in range(HOURS):
            position = 2 * (level * HOURS + hour)
            turned = pltpu.roll(halo, LANES - 1 - position, 1)
            out_ref[level, hour] = flux_ref[level, hour] + weight * turned


def swap(array):
    groups = [[z * GROUP + i for i in range(GROUP)] for z in range(RUNS)]
    return lax.all_to_all(array, "tm", 0, 0, tiled=True, axis_index_groups=groups)


def swap_runs(array):
    groups = [[z * GROUP + i for z in range(RUNS)] for i in range(GROUP)]
    return lax.all_to_all(array, "tm", 0, 0, tiled=True, axis_index_groups=groups)


VMEM = pl.BlockSpec(memory_space=pltpu.VMEM)
SMEM = pl.BlockSpec(memory_space=pltpu.SMEM)


def call(kernel, shapes, n_in, scalars=0, scratch=()):
    shapes = [jax.ShapeDtypeStruct(shape, jnp.float32) for shape in shapes]
    single = len(shapes) == 1
    return pl.pallas_call(
        kernel,
        out_shape=shapes[0] if single else shapes,
        in_specs=[SMEM] * scalars + [VMEM] * (n_in - scalars),
        out_specs=VMEM if single else [VMEM] * len(shapes),
        scratch_shapes=[pltpu.VMEM(shape, jnp.float32) for shape in scratch],
        compiler_params=pltpu.CompilerParams(vmem_limit_bytes=32 * 1024 * 1024),
    )


def on_device(u_vel, v_vel, density, land_mask, start_hour, levels):
    tables = plan()
    whole = (4, HOURS, ROWS, LANES)
    part = (3, HOURS, ROWS, LANES)
    slots = (ROWS, SERIES * 8, LANES)
    flat = (ROWS * SERIES * 8, LANES)
    fields = (levels, u_vel, v_vel, density, land_mask, start_hour)
    own = call(summary_kernel, [flat], 6, 1)(*fields)
    blocks = swap(own.reshape(slots))
    runs = call(run_kernel, [(RUNS, PAIRS * 8, LANES)], 2)(blocks, tables["send"])
    runs = swap_runs(runs)
    borders = call(border_kernel, [slots], 6)(
        blocks, runs, tables["gather"], tables["local"], tables["spread"], tables["inject"]
    )
    borders = swap(borders).reshape(flat)
    pressure, flux, edges = call(band_kernel, [whole, whole, (ROWS, LANES)], 7, 1, [part, part, part])(
        *fields, borders
    )
    count = lax.axis_size("col")
    west = lax.ppermute(edges, "col", [(i, i + 1) for i in range(count - 1)])
    east = lax.ppermute(edges, "col", [(i + 1, i) for i in range(count - 1)])
    flux = call(seam_kernel, [whole], 4)(flux, land_mask, west, east)
    return (pressure, flux)


def solution(mesh):
    return jax.shard_map(
        on_device,
        mesh=mesh,
        in_specs=(
            P(None, "tm", None, "col"),
            P(None, "tm", None, "col"),
            P(None, "tm", None, "col"),
            P(None, "col"),
            P(None, "col"),
            P(),
        ),
        out_specs=(P(None, "tm", None, "col"), P(None, "tm", None, "col")),
        check_vma=False,
    )
```

time: 414 us -> 78.5 us (0.19)
  the two profiles are of different devices: /device:TPU:449 before, /device:TPU:6 now
where the time goes in v1:
time: 78.5 us; the launch traced here: 78 us
  blocking collectives  48.1 us (61%)
  starting transfers between devices  16.7 us (21%)
  local copies, waits for them, and re-layouts  5.57 us (7%)
  Pallas kernels  5.56 us (7%)
  waiting for transfers between devices  1.3 us (2%)
    all_to_all x1, blocking collectives, swap_runs(): lax.all_to_all(array, 'tm', 0, 0, tiled=True, axis_index_groups=groups)  25.4 us
    all_to_all x2, blocking collectives, swap(): lax.all_to_all(array, 'tm', 0, 0, tiled=True, axis_index_groups=groups)  22.7 us
    ppermute x1, starting transfers between devices, on_device(): west = lax.ppermute(edges, 'col', [(i, i + 1) for i in range(count - 1)])  13.9 us
    unnamed x30, local copies, waits for them, and re-layouts  5.57 us
    ppermute x1, starting transfers between devices, on_device(): east = lax.ppermute(edges, 'col', [(i + 1, i) for i in range(count - 1)])  2.72 us
    pallas_call x1, Pallas kernels, on_device(): call(band_kernel, [whole, whole, (ROWS, LANES)], 7, 1, [part, part, part])  2.35 us
  transfers between devices with their start and end apart: 2, of which 1 were waited for; matrix products, arithmetic and copies ran while one was open for 0% of the time, Pallas kernels for 0%

profile of v1, /device:TPU:6, one launch (start us, length us, event | category | flops | bytes accessed | tf_op | source)
XLA Modules:
  0.0 78.0 jit_solution(3419907237598105886)
XLA Ops:
  0.6 0.0 copy-start
  0.6 0.9 %copy-done = f32[4,16,8,128]{3,2,1,0:T(8,128)S(1)} copy-done((f32[4,16,8,128]{3,2,1,0:T(8,128)S(1)}, f32[4,16,8,128]{3,2,1,0:T(8,128)}, u32[]{:S(2)}) %copy-start) | copy-done | bytes 262168
  1.6 0.0 copy-start.2
  1.6 0.9 %copy-done.2 = f32[4,16,8,128]{3,2,1,0:T(8,128)S(1)} copy-done((f32[4,16,8,128]{3,2,1,0:T(8,128)S(1)}, f32[4,16,8,128]{3,2,1,0:T(8,128)}, u32[]{:S(2)}) %copy-start.2) | copy-done | bytes 262168
  2.5 0.0 copy-start.4
  2.5 0.9 %copy-done.4 = f32[4,16,8,128]{3,2,1,0:T(8,128)S(1)} copy-done((f32[4,16,8,128]{3,2,1,0:T(8,128)S(1)}, f32[4,16,8,128]{3,2,1,0:T(8,128)}, u32[]{:S(2)}) %copy-start.4) | copy-done | bytes 262168
  3.5 0.0 copy-start.11
  3.5 0.7 copy-done.11
  4.2 0.0 copy-start.12
  4.2 0.7 copy-done.12
  4.9 0.0 copy-start.13
  4.9 0.7 copy-done.13
  5.5 1.0 %shard_map.122 = f32[576,128]{1,0:T(8,128)S(1)} custom-call(s32[4]{0:T(128)S(1)} %copy-done.13, f32[4,16,8,128]{3,2,1,0:T(8,128)S(1)} %copy-done, f32[4,16,8,128]{3,2,1,0:T(8,128)S(1)} %copy-done.2, f32[4,16,8,128]{3,2,1,0:T(8,128)S(1)} %copy-done.4, s32[8,128]{1,0:T(8,128)S(1)} %copy-done.11, s32[8,128]{1,0:T(8,128)S(1)} %copy-done.12), custom_call_target="tpu_custom_call" | custom-call | tf_op jit(solution)/shard_map/pallas_call | solution.py:369
  6.5 0.0 copy-start.10
  6.5 12.3 %all_to_all.15.in_ref = f32[8,72,128]{2,1,0:T(8,128)S(1)} all-to-all(f32[8,72,128]{2,1,0:T(8,128)S(1)} %bitcast.3), channel_id=1, replica_groups={{0,8,16,24,32,40,48,56},{64,72,80,88,96,104,112,120},{128,136,144,152,1..., dimensions={0} | all-to-all | bytes 589824 | tf_op jit(solution)/shard_map/all_to_all | solution.py:337
  18.8 0.0 copy-done.10
  18.8 0.3 shard_map.123
  19.1 0.0 copy-start.6
  19.1 0.0 copy-start.7
  19.1 0.0 copy-start.8
  19.1 0.0 copy-start.9
  19.1 25.4 %all_to_all.16.runs_ref = f32[8,40,128]{2,1,0:T(8,128)S(1)} all-to-all(f32[8,40,128]{2,1,0:T(8,128)S(1)} %shard_map.123), channel_id=1, replica_groups={{0,64,128,192,256,320,384,448},{8,72,136,200,264,328,392,456},{16,80,14..., dimensions={0} | all-to-all | bytes 327680 | tf_op jit(solution)/shard_map/all_to_all | solution.py:342
  44.6 0.0 copy-done.6
  44.6 0.0 copy-done.7
  44.6 0.0 copy-done.8
  44.6 0.0 copy-done.9
  44.6 0.0 copy-start.5
  44.6 1.1 %shard_map.124 = f32[8,72,128]{2,1,0:T(8,128)S(1)} custom-call(f32[8,72,128]{2,1,0:T(8,128)S(1)} %all_to_all.15.in_ref, f32[8,40,128]{2,1,0:T(8,128)S(1)} %all_to_all.16.runs_ref, f32[8,16,64]{2,1,0:T(8,128)S(1)} %copy-done.9, f32[8,16,128]{2,1,0:T(8,128)S(1)} %copy-done.8, f32[128,128]{1,0:T(8,128)S(1)} %copy-done.7, f32[128,16]{1,0:T(8,128)S(1)} %copy-done.6), custom_call_target="tpu_custom_call" | custom-call | tf_op jit(solution)/shard_map/pallas_call | solution.py:373
  45.7 0.0 copy-start.1
  45.7 0.0 copy-start.3
  45.7 10.4 %all_to_all.17 = f32[8,72,128]{2,1,0:T(8,128)S(1)} all-to-all(f32[8,72,128]{2,1,0:T(8,128)S(1)} %shard_map.124), channel_id=1, replica_groups={{0,8,16,24,32,40,48,56},{64,72,80,88,96,104,112,120},{128,136,144,152,1..., dimensions={0} | all-to-all | bytes 589824 | tf_op jit(solution)/shard_map/all_to_all | solution.py:337
  56.1 0.0 copy-start.14
  56.1 0.0 copy-done.5
  56.1 0.0 copy-done.1
  56.1 0.0 copy-done.3
  56.1 0.6 copy-done.14
  56.8 2.3 %shard_map.125 = (f32[4,16,8,128]{3,2,1,0:T(8,128)}, f32[4,16,8,128]{3,2,1,0:T(8,128)S(1)}, f32[8,128]{1,0:T(8,128)S(1)}) custom-call(s32[4]{0:T(128)S(1)} %copy-done.14, f32[4,16,8,128]{3,2,1,0:T(8,128)S(1)} %copy-done.1, f32[4,16,8,128]{3,2,1,0:T(8,128)S(1)} %copy-done.3, f32[4,16,8,128]{3,2,1,0:T(8,128)S(1)} %copy-done.5, s32[8,128]{1,0:T(8,128)S(1)} %copy-done.11, ...), custom_call_target="tpu_custom_call" | custom-call | tf_op jit(solution)/shard_map/pallas_call | solution.py:377
  59.1 2.7 %collective-permute-start.1 = (f32[8,128]{1,0:T(8,128)S(1)}, f32[8,128]{1,0:T(8,128)S(1)}, u32[]{:S(2)}, u32[]{:S(2)}) collective-permute-start(f32[8,128]{1,0:T(8,128)S(1)} %get-tuple-element.7), channel_id=1, source_target_pairs={{1,0},{2,1},{3,2},{4,3},{5,4},{6,5},{7,6},{9,8},{10,9},{11,10},{12... | collective-permute-start | bytes 12296 | tf_op jit(solution)/shard_map/ppermute | solution.py:382
  61.8 13.9 %collective-permute-start = (f32[8,128]{1,0:T(8,128)S(1)}, f32[8,128]{1,0:T(8,128)S(1)}, u32[]{:S(2)}, u32[]{:S(2)}) collective-permute-start(f32[8,128]{1,0:T(8,128)S(1)} %get-tuple-element.7), channel_id=1, source_target_pairs={{0,1},{1,2},{2,3},{3,4},{4,5},{5,6},{6,7},{8,9},{9,10},{10,11},{11... | collective-permute-start | bytes 12296 | tf_op jit(solution)/shard_map/ppermute | solution.py:381
  75.8 0.0 collective-permute-done.1.east_ref
  75.8 1.3 %collective-permute-done.west_ref = f32[8,128]{1,0:T(8,128)S(1)} collective-permute-done((f32[8,128]{1,0:T(8,128)S(1)}, f32[8,128]{1,0:T(8,128)S(1)}, u32[]{:S(2)}, u32[]{:S(2)}) %collective-permute-start) | collective-permute-done | bytes 4128 | tf_op jit(solution)/shard_map/ppermute | solution.py:381
  77.1 0.9 %shard_map.126 = f32[4,16,8,128]{3,2,1,0:T(8,128)} custom-call(f32[4,16,8,128]{3,2,1,0:T(8,128)S(1)} %get-tuple-element.6.flux_ref, s32[8,128]{1,0:T(8,128)S(1)} %copy-done.11, f32[8,128]{1,0:T(8,128)S(1)} %collective-permute-done.west_ref, f32[8,128]{1,0:T(8,128)S(1)} %collective-permute-done.1.east_ref), custom_call_target="tpu_custom_call" | custom-call | tf_op jit(solution)/shard_map/pallas_call | solution.py:383
Async XLA Ops:
  0.6 1.0 %copy-start = (f32[4,16,8,128]{3,2,1,0:T(8,128)S(1)}, f32[4,16,8,128]{3,2,1,0:T(8,128)}, u32[]{:S(2)}) copy-start(f32[4,16,8,128]{3,2,1,0:T(8,128)} %u_ref.3) | copy-start | bytes 786436
  1.6 0.9 %copy-start.2 = (f32[4,16,8,128]{3,2,1,0:T(8,128)S(1)}, f32[4,16,8,128]{3,2,1,0:T(8,128)}, u32[]{:S(2)}) copy-start(f32[4,16,8,128]{3,2,1,0:T(8,128)} %v_ref.3) | copy-start | bytes 786436
  2.5 0.9 %copy-start.4 = (f32[4,16,8,128]{3,2,1,0:T(8,128)S(1)}, f32[4,16,8,128]{3,2,1,0:T(8,128)}, u32[]{:S(2)}) copy-start(f32[4,16,8,128]{3,2,1,0:T(8,128)} %rho_ref.3) | copy-start | bytes 786436
  3.5 0.7 copy-start.11
  4.2 0.7 copy-start.12
  4.9 0.7 copy-start.13
  6.5 12.3 %copy-start.10 = (f32[8,16,128]{2,1,0:T(8,128)S(1)}, f32[8,16,128]{2,1,0:T(8,128)}, u32[]{:S(2)}) copy-start(f32[8,16,128]{2,1,0:T(8,128)} %constant.10.clone.send_ref) | copy-start | bytes 196612
  19.1 25.5 %copy-start.6 = (f32[128,16]{1,0:T(8,128)S(1)}, f32[128,16]{1,0:T(8,128)}, u32[]{:S(2)}) copy-start(f32[128,16]{1,0:T(8,128)} %constant.14.clone.inject_ref) | copy-start | bytes 24580
  19.1 25.5 %copy-start.7 = (f32[128,128]{1,0:T(8,128)S(1)}, f32[128,128]{1,0:T(8,128)}, u32[]{:S(2)}) copy-start(f32[128,128]{1,0:T(8,128)} %constant.13.clone.spread_ref) | copy-start | bytes 196612
  19.1 25.5 %copy-start.8 = (f32[8,16,128]{2,1,0:T(8,128)S(1)}, f32[8,16,128]{2,1,0:T(8,128)}, u32[]{:S(2)}) copy-start(f32[8,16,128]{2,1,0:T(8,128)} %constant.12.clone.local_ref) | copy-start | bytes 196612
  19.1 25.5 %copy-start.9 = (f32[8,16,64]{2,1,0:T(8,128)S(1)}, f32[8,16,64]{2,1,0:T(8,128)}, u32[]{:S(2)}) copy-start(f32[8,16,64]{2,1,0:T(8,128)} %constant.11.clone.gather_ref) | copy-start | bytes 98308
  44.6 11.5 %copy-start.5 = (f32[4,16,8,128]{3,2,1,0:T(8,128)S(1)}, f32[4,16,8,128]{3,2,1,0:T(8,128)}, u32[]{:S(2)}) copy-start(f32[4,16,8,128]{3,2,1,0:T(8,128)} %rho_ref.3) | copy-start | bytes 786436
  45.7 10.4 %copy-start.1 = (f32[4,16,8,128]{3,2,1,0:T(8,128)S(1)}, f32[4,16,8,128]{3,2,1,0:T(8,128)}, u32[]{:S(2)}) copy-start(f32[4,16,8,128]{3,2,1,0:T(8,128)} %u_ref.3) | copy-start | bytes 786436
  45.7 10.4 %copy-start.3 = (f32[4,16,8,128]{3,2,1,0:T(8,128)S(1)}, f32[4,16,8,128]{3,2,1,0:T(8,128)}, u32[]{:S(2)}) copy-start(f32[4,16,8,128]{3,2,1,0:T(8,128)} %v_ref.3) | copy-start | bytes 786436
  56.1 0.7 copy-start.14
  59.1 16.7 %collective-permute-start.1 = (f32[8,128]{1,0:T(8,128)S(1)}, f32[8,128]{1,0:T(8,128)S(1)}, u32[]{:S(2)}, u32[]{:S(2)}) collective-permute-start(f32[8,128]{1,0:T(8,128)S(1)} %get-tuple-element.7), channel_id=1, source_target_pairs={{1,0},{2,1},{3,2},{4,3},{5,4},{6,5},{7,6},{9,8},{10,9},{11,10},{12... | collective-permute-start | bytes 12296 | tf_op jit(solution)/shard_map/ppermute | solution.py:382
  61.8 15.2 %collective-permute-start = (f32[8,128]{1,0:T(8,128)S(1)}, f32[8,128]{1,0:T(8,128)S(1)}, u32[]{:S(2)}, u32[]{:S(2)}) collective-permute-start(f32[8,128]{1,0:T(8,128)S(1)} %get-tuple-element.7), channel_id=1, source_target_pairs={{0,1},{1,2},{2,3},{3,4},{4,5},{5,6},{6,7},{8,9},{9,10},{10,11},{11... | collective-permute-start | bytes 12296 | tf_op jit(solution)/shard_map/ppermute | solution.py:381

commit v2 on v1

v2 whole, which is shorter than its diff:
```python
import functools
import math

import jax
import jax.numpy as jnp
import numpy as np
from jax import lax
from jax.experimental import pallas as pl
from jax.experimental.pallas import tpu as pltpu
from jax.sharding import PartitionSpec as P

HOURS = 16
GROUP = 16
RUNS = 4
OWNERS = 2 * GROUP
SERIES = 9
ROWS = 8
LANES = 128
QUARTER = 32
SLOT = 24
SPAN = GROUP * HOURS
QUARTERS = (0, 3, 1, 2)
PAIRS = ((0, 1), (2, 3), (4, 5), (6, 7))
FAR = ((1, 2), (3, 4), (5, 6), (7, 0))
HIGH = lax.Precision.HIGHEST


def expand_roots(roots):
    coefficients = [complex(1.0, 0.0)]
    for root in roots:
        widened = coefficients + [complex(0.0, 0.0)]
        for position in range(1, len(widened)):
            widened[position] = widened[position] - root * coefficients[position - 1]
        coefficients = widened
    return [coefficient.real for coefficient in coefficients]


def horner_value(coefficients, point):
    running = complex(0.0, 0.0)
    for coefficient in coefficients:
        running = running * point + coefficient
    return running


def derive_coeffs(coefficients):
    degree = len(coefficients) - 1
    return [coefficients[position] * (degree - position) for position in range(degree)]


def filter_design():
    low_edge = 1.0 / 12.9
    high_edge = 1.0 / 12.0
    warped_low = 2.0 * math.tan(math.pi * low_edge)
    warped_high = 2.0 * math.tan(math.pi * high_edge)
    centre = math.sqrt(warped_low * warped_high)
    spread = warped_high - warped_low
    digital = []
    for octant in (3, 5):
        proto = complex(math.cos(octant * math.pi / 4.0), math.sin(octant * math.pi / 4.0)) * spread
        radical = (proto * proto - 4.0 * centre * centre) ** 0.5
        for analog in ((proto + radical) / 2.0, (proto - radical) / 2.0):
            digital.append((2.0 + analog) / (2.0 - analog))
    denom = expand_roots(digital)
    numer = [1.0, 0.0, -2.0, 0.0, 1.0]
    omega = 2.0 * math.atan(centre / 2.0)
    zcentre = complex(math.cos(omega), math.sin(omega))
    respond = horner_value(numer, zcentre) / horner_value(denom, zcentre)
    numer = [coefficient / abs(respond) for coefficient in numer]
    remain = [numer[position] - numer[0] * denom[position] for position in range(1, 5)]
    slope = derive_coeffs(denom)
    amat = np.zeros((4, 4))
    bvec = np.zeros(4)
    cvec = np.zeros(4)
    upper = [pole for pole in digital if pole.imag > 0]
    for index, pole in enumerate(upper):
        resid = horner_value(remain, pole) / horner_value(slope, pole)
        first = 2 * index
        amat[first, first] = pole.real
        amat[first, first + 1] = -pole.imag
        amat[first + 1, first] = pole.imag
        amat[first + 1, first + 1] = pole.real
        bvec[first] = 1.0
        cvec[first] = 2.0 * resid.real
        cvec[first + 1] = -2.0 * resid.imag
    return (amat, bvec, cvec, float(numer[0]))


def power(matrix, exponent):
    return np.linalg.matrix_power(matrix, exponent)


def power(matrix, exponent):
    return np.linalg.matrix_power(matrix, exponent)


def block_maps(hours):
    amat, bvec, cvec, direct = filter_design()
    impulse = [direct] + [float(cvec @ power(amat, step - 1) @ bvec) for step in range(1, hours)]
    toeplitz = np.zeros((hours, hours))
    for row in range(hours):
        for column in range(row + 1):
            toeplitz[row, column] = impulse[row - column]
    powers = [np.eye(4)]
    for hour in range(hours):
        powers.append(powers[-1] @ amat)
    left = np.stack([powers[hours - 1 - hour] @ bvec for hour in range(hours)], axis=1)
    entering = np.stack([cvec @ powers[hour] for hour in range(hours)], axis=0)
    back = np.stack([powers[hour] @ bvec for hour in range(hours)], axis=1)
    summary = np.concatenate([left, back @ toeplitz], axis=0)
    response = toeplitz.T @ toeplitz
    injected = np.concatenate([toeplitz.T @ entering, entering[::-1]], axis=1)
    return summary, back @ entering, powers[hours], response, injected


@functools.lru_cache(maxsize=None)
def plan():
    amat, bvec, cvec, direct = filter_design()
    summary, coupling, step, _, _ = block_maps(HOURS)
    own = GROUP * 8
    forward = np.zeros((GROUP + 1, 4, own + 8))
    forward[0][:, own : own + 4] = np.eye(4)
    for j in range(GROUP):
        forward[j + 1] = step @ forward[j]
        forward[j + 1][:, j * 8 : j * 8 + 4] += np.eye(4)
    backward = np.zeros((GROUP + 1, 4, own + 8))
    backward[GROUP][:, own + 4 :] = np.eye(4)
    for j in reversed(range(GROUP)):
        backward[j] = step @ backward[j + 1] + coupling @ forward[j]
        backward[j][:, j * 8 + 4 : j * 8 + 8] += np.eye(4)
    inner = np.zeros((own, own + 8))
    for j in range(GROUP):
        inner[j * 8 : j * 8 + 4] = forward[j]
        inner[j * 8 + 4 : j * 8 + 8] = backward[j + 1]
    run_left = forward[GROUP][:, :own]
    run_right = backward[0][:, :own]
    run_summary, run_coupling, run_step, response, injected = block_maps(SPAN)
    suffix = [np.zeros((4, 4))]
    for m in range(RUNS):
        suffix.append(suffix[-1] + power(run_step, m) @ run_coupling @ power(run_step, m))
    send = np.zeros((RUNS, 16, 2 * own))
    local = np.zeros((RUNS, 16, 2 * own))
    gather = np.zeros((RUNS, 16, RUNS * 8))
    edge_gather = np.zeros((RUNS, LANES, LANES))
    for z in range(RUNS):
        after = suffix[RUNS - 1 - z]
        for tile in range(2):
            columns = slice(tile * own, (tile + 1) * own)
            ahead = slice(4 * tile, 4 * tile + 4)
            behind = slice(8 + 4 * tile, 12 + 4 * tile)
            send[z, ahead, columns] = run_left
            send[z, behind, columns] = run_right + run_step @ after @ run_left
            local[z, behind, columns] = after @ run_left
            for other in range(RUNS):
                here = slice(other * 8 + 4 * tile, other * 8 + 4 * tile + 4)
                if other < z:
                    came = power(run_step, z - 1 - other)
                    gather[z, ahead, here] = came
                    gather[z, behind, here] = after @ run_step @ came
                if other > z:
                    gather[z, behind, here] = power(run_step, other - z - 1)
        for other in range(RUNS):
            from_left = slice(other * 8, other * 8 + 4)
            from_right = slice(other * 8 + 4, other * 8 + 8)
            if other < z:
                came = power(run_step, z - 1 - other)
                edge_gather[z, from_left, 0:4] = came.T
                edge_gather[z, from_left, 4:8] = (after @ run_step @ came).T
            if other == z:
                edge_gather[z, from_left, 4:8] = after.T
            if other > z:
                came = power(run_step, other - z - 1)
                edge_gather[z, from_right, 4:8] = came.T
                edge_gather[z, from_left, 4:8] = (came @ run_step @ suffix[RUNS - 1 - other]).T
    spread = inner[:, :own]
    inject = np.zeros((2, own, 16))
    for tile in range(2):
        inject[tile, :, 4 * tile : 4 * tile + 4] = inner[:, own : own + 4]
        inject[tile, :, 8 + 4 * tile : 12 + 4 * tile] = inner[:, own + 4 :]
    edge_sum = np.zeros((SPAN, LANES))
    edge_sum[:, QUARTER : QUARTER + 8] = run_summary.T
    edge_out = np.zeros((SPAN + LANES, SPAN))
    edge_out[:SPAN] = response.T
    edge_out[SPAN : SPAN + 8] = injected.T
    tables = dict(
        send=send,
        local=local,
        gather=gather,
        spread=spread,
        inject=inject,
        edge_sum=edge_sum,
        edge_gather=edge_gather,
        edge_out=edge_out,
    )
    tables = {name: table.astype(np.float32) for name, table in tables.items()}
    return dict(tables, amat=amat, cvec=cvec, direct=direct, summary=summary)


def place():
    tile = lax.axis_index("col") % 2
    return lax.axis_index("tm") // GROUP, tile, 1 - tile


def lanes_of(shape=(ROWS, LANES)):
    return lax.broadcasted_iota(jnp.int32, shape, 1)


def live_hours(mask, start):
    first = lax.axis_index("tm") * HOURS
    ocean = mask == 1
    return [jnp.where(ocean & (start <= first + hour), 1.0, 0.0) for hour in range(HOURS)]


def depths(levels_ref):
    out = []
    for level in range(4):
        number = jnp.full((ROWS, LANES), levels_ref[level], jnp.int32).astype(jnp.float32)
        out.append((number + number * number / 90.0) / 90.0)
    return out


def anomalies(field, live):
    mean = 0.25 * ((field[0] + field[1]) + (field[2] + field[3]))
    return [(field[level] - mean) * live for level in range(3)]


def pressures(rho, depth):
    press = [rho[0] * depth[0]]
    for level in range(1, 4):
        press.append(press[-1] + 0.5 * (rho[level - 1] + rho[level]) * (depth[level] - depth[level - 1]))
    return press


def last_level(values):
    return -((values[0] + values[1]) + values[2])


def turn(value, shift):
    shift = shift % LANES
    return value if shift == 0 else pltpu.roll(value, shift, 1)


def transposed(parts, lane):
    low = lane < 2 * QUARTER
    even = (lane // QUARTER) % 2 == 0
    halves = [None] * 4
    for i in range(2):
        first, second = parts[i], parts[i + 2]
        halves[i] = jnp.where(low, first, turn(second, 64))
        halves[i + 2] = jnp.where(low, turn(first, 64), second)
    out = [None] * 4
    for i in (0, 2):
        first, second = halves[i], halves[i + 1]
        out[i] = jnp.where(even, first, turn(second, QUARTER))
        out[i + 1] = jnp.where(even, turn(first, -QUARTER), second)
    return out


def summary_kernel(
    levels_hbm, u_hbm, v_hbm, rho_hbm, mask_hbm, start_hbm, out_ref, levels_ref, u_ref, v_ref, rho_ref, mask_ref, start_ref, sums_ref, sems
):
    summary = plan()["summary"]
    copies = [
        pltpu.make_async_copy(source, target, sems.at[index])
        for index, (source, target) in enumerate(
            (
                (mask_hbm, mask_ref),
                (start_hbm, start_ref),
                (levels_hbm, levels_ref),
                (u_hbm, u_ref),
                (rho_hbm, rho_ref),
                (v_hbm, v_ref),
            )
        )
    ]
    for copy in copies:
        copy.start()
    for copy in copies[:3]:
        copy.wait()
    live = live_hours(mask_ref[...], start_ref[...])
    depth = depths(levels_ref)
    lane = lanes_of()
    west = [jnp.zeros((ROWS, LANES), jnp.float32) for _ in range(8)]
    east = list(west)
    for which, ref in enumerate((u_ref, rho_ref, v_ref)):
        copies[3 + which].wait()
        sums = [[None] * 8 for _ in range(3)]
        for hour in range(HOURS):
            field = [ref[level, hour] for level in range(4)]
            if which == 1:
                field = pressures(field, depth)
            values = anomalies(field, live[hour])
            for level, value in enumerate(values):
                for k in range(8):
                    term = float(summary[k, hour]) * value
                    sums[level][k] = term if hour == 0 else sums[level][k] + term
            if which < 2:
                for level, value in enumerate(values + [last_level(values)]):
                    turned = turn(value, QUARTER + hour)
                    at = which * 4 + level
                    west[at] = jnp.where(lane == QUARTER + hour, turned, west[at])
                    east[at] = jnp.where(lane == QUARTER - 1 + hour, turned, east[at])
        for level in range(3):
            for k in range(8):
                sums_ref[(which * 3 + level) * 8 + k] = sums[level][k]
    first = lane < QUARTER
    for k in range(8):
        for v in range(2):
            parts = transposed([sums_ref[(4 * v + a) * 8 + k] for a in range(4)], lane)
            for index, quarter in enumerate(QUARTERS):
                out_ref[pl.ds(index * SLOT + v * 8 + k, ROWS, stride=4 * SLOT), :] = parts[quarter]
        single = sums_ref[64 + k]
        others = {0: west[k], 3: turn(east[k], 1)}
        for index, quarter in enumerate(QUARTERS):
            part = jnp.where(first, turn(single, -QUARTER * quarter), others.get(quarter, 0.0))
            out_ref[pl.ds(index * SLOT + 16 + k, ROWS, stride=4 * SLOT), :] = part


def blocks_of(in_ref, tile):
    return jnp.concatenate(
        [
            jnp.concatenate([in_ref[2 * j + tile, pl.ds(v * 8, 8), :] for j in range(GROUP)], axis=0)
            for v in range(3)
        ],
        axis=1,
    )


def edge_hours(in_ref, tile):
    lane = lanes_of()
    halves = []
    for half in range(2):
        total = jnp.zeros((ROWS, LANES), jnp.float32)
        for i in range(8):
            turned = turn(in_ref[2 * (half * 8 + i) + tile, pl.ds(16, 8), :], i * HOURS - QUARTER)
            total = jnp.where(lane // HOURS == i, turned, total)
        halves.append(total)
    return jnp.concatenate(halves, axis=1)


def dot(lhs, rhs):
    return jnp.dot(lhs, rhs, precision=HIGH, preferred_element_type=jnp.float32)


def run_kernel(in_ref, send_ref, edge_sum_ref, out_ref):
    run, tile, side = place()
    blocks = jnp.concatenate([blocks_of(in_ref, 0), blocks_of(in_ref, 1)], axis=0)
    totals = dot(send_ref[run], blocks)
    near = edge_hours(in_ref, 1 - tile)
    far = edge_hours(in_ref, tile)
    sums = dot(jnp.concatenate([near, far], axis=0), edge_sum_ref[...])
    first = lanes_of() < QUARTER
    for other in range(RUNS):
        for v in range(3):
            lanes = slice(v * LANES, (v + 1) * LANES)
            mine = jnp.where(other > run, totals[0:8, lanes], totals[8:16, lanes])
            if v == 2:
                mine = jnp.where(first, mine, sums[0:8])
                across = sums[8:16]
            else:
                across = far[:, lanes]
            for slot_side in range(2):
                out_ref[2 * other + slot_side, pl.ds(v * 8, 8), :] = jnp.where(side == slot_side, mine, across)


def edge_flux(in_ref, runs_ref, run, tile, side, edge_gather, edge_out):
    lane = lanes_of()
    own = [runs_ref[2 * other + side, pl.ds(16, 8), :] for other in range(RUNS)]
    across = [runs_ref[2 * other + 1 - side, pl.ds(16, 8), :] for other in range(RUNS)]
    sums = []
    for parts in (own, across):
        total = jnp.zeros((ROWS, LANES), jnp.float32)
        for other in range(RUNS):
            total = jnp.where(lane // 8 == other, turn(parts[other], other * 8 - QUARTER), total)
        sums.append(total)
    states = dot(jnp.concatenate(sums, axis=0), edge_gather)
    near = edge_hours(in_ref, 1 - tile)
    far = jnp.concatenate([runs_ref[2 * run + 1 - side, pl.ds(v * 8, 8), :] for v in range(2)], axis=1)
    hours = jnp.concatenate([near, far], axis=0)
    banded = dot(jnp.concatenate([hours, states], axis=1), edge_out)
    row = lax.broadcasted_iota(jnp.int32, (ROWS, SPAN), 0)
    products = [part * pltpu.roll(part, 4, 0) for part in (banded[0:8], banded[8:16])]
    return jnp.where(row < 4, products[0], products[1])


def border_kernel(
    in_ref, runs_ref, gather_ref, local_ref, spread_ref, inject_ref, edge_gather_ref, edge_out_ref, out_ref
):
    run, tile, side = place()
    flux = edge_flux(in_ref, runs_ref, run, tile, side, edge_gather_ref[run], edge_out_ref[...])
    tiles = [blocks_of(in_ref, 0), blocks_of(in_ref, 1)]
    runs = jnp.concatenate([runs_ref[2 * other + side].reshape(3, 8, LANES) for other in range(RUNS)], axis=1)
    runs = jnp.concatenate([runs[v] for v in range(3)], axis=1)
    states = dot(gather_ref[run], runs) + dot(local_ref[run], jnp.concatenate(tiles, axis=0))
    first = lanes_of() < QUARTER
    for which in range(2):
        borders = dot(spread_ref[...], tiles[which]) + dot(inject_ref[which], states)
        for j in range(GROUP):
            for v in range(3):
                value = borders[j * 8 : j * 8 + 8, v * LANES : (v + 1) * LANES]
                if v == 2:
                    half = flux[:, (j // 8) * LANES : (j // 8 + 1) * LANES]
                    value = jnp.where(first, value, turn(half, QUARTER - (j % 8) * HOURS))
                out_ref[2 * j + which, pl.ds(v * 8, 8), :] = value


def filter_steps(state, samples):
    amat, cvec, direct = plan()["amat"], plan()["cvec"], plan()["direct"]
    out = []
    for sample in samples:
        value = direct * sample
        for k in range(4):
            value = value + float(cvec[k]) * state[k]
        out.append(value)
        fresh = []
        for first in (0, 2):
            real, imag = float(amat[first, first]), float(amat[first + 1, first])
            fresh.append((real * state[first] - imag * state[first + 1]) + sample)
            fresh.append(imag * state[first] + real * state[first + 1])
        state = fresh
    return out


def band_kernel(
    levels_ref, u_ref, v_ref, rho_ref, mask_ref, start_ref, borders_ref, press_ref, flux_ref, held, east, north, states_ref
):
    _, tile, _ = place()
    column = lax.axis_index("col")
    mask = mask_ref[...]
    live = live_hours(mask, start_ref[...])
    depth = depths(levels_ref)
    lane = lanes_of()
    for k in range(8):
        for v in range(3):
            parts = [None] * 4
            for index, quarter in enumerate(QUARTERS):
                parts[quarter] = borders_ref[pl.ds(index * SLOT + v * 8 + k, ROWS, stride=4 * SLOT), :]
            if v < 2:
                for a, part in enumerate(transposed(parts, lane)):
                    states_ref[(4 * v + a) * 8 + k] = part
            else:
                total = parts[0]
                for quarter in range(1, 4):
                    total = jnp.where(lane // QUARTER == quarter, turn(parts[quarter], QUARTER * quarter), total)
                states_ref[64 + k] = total
    for which, ref in ((1, rho_ref), (0, u_ref), (2, v_ref)):
        for hour in range(HOURS):
            field = [ref[level, hour] for level in range(4)]
            if which == 1:
                field = pressures(field, depth)
            for level, value in enumerate(anomalies(field, live[hour])):
                held[level, hour] = value
        target = (east, press_ref, north)[which]
        for level in range(3):
            states = [states_ref[(which * 3 + level) * 8 + k] for k in range(8)]
            samples = filter_steps(states[:4], [held[level, hour] for hour in range(HOURS)])
            samples = filter_steps(states[4:], samples[::-1])[::-1]
            for hour in range(HOURS):
                target[level, hour] = samples[hour]
    row = lax.broadcasted_iota(jnp.int32, (ROWS, LANES), 0)
    half = 0.5 * mask.astype(jnp.float32)
    last = lane == LANES - 1
    halos = []
    for level in range(4):
        near = borders_ref[pl.ds(tile * SLOT + 16 + level, ROWS, stride=4 * SLOT), :]
        far = borders_ref[pl.ds(tile * SLOT + 20 + level, ROWS, stride=4 * SLOT), :]
        from_west = jnp.where(column == 0, 0.0, jnp.where(tile == 0, far, near))
        from_east = jnp.where(column == 2 * len(PAIRS) - 1, 0.0, jnp.where(tile == 0, near, far))
        halos.append((from_west, from_east))
    for hour in range(HOURS):
        u_all = [east[level, hour] for level in range(3)]
        v_all = [north[level, hour] for level in range(3)]
        p_all = [press_ref[level, hour] for level in range(3)]
        for values in (u_all, v_all, p_all):
            values.append(last_level(values))
        press_ref[3, hour] = p_all[3]
        for level in range(4):
            fx = u_all[level] * p_all[level]
            fy = v_all[level] * p_all[level]
            from_west, from_east = halos[level]
            next_x = jnp.where(last, turn(from_east, LANES - 1 - QUARTER - hour), turn(fx, -1))
            prev_x = jnp.where(lane == 0, turn(from_west, -QUARTER - hour), turn(fx, 1))
            next_y = jnp.where(row == ROWS - 1, 0.0, pltpu.roll(fy, ROWS - 1, 0))
            prev_y = jnp.where(row == 0, 0.0, pltpu.roll(fy, 1, 0))
            flux_ref[level, hour] = half * ((next_x - prev_x) + (next_y - prev_y))


def swap(array, devices, columns):
    groups = [[tm * 8 + col for tm in some for col in pair] for some in devices for pair in columns]
    return lax.all_to_all(array, ("tm", "col"), 0, 0, tiled=True, axis_index_groups=groups)


VMEM = pl.BlockSpec(memory_space=pltpu.VMEM)
SMEM = pl.BlockSpec(memory_space=pltpu.SMEM)
ANY = pl.BlockSpec(memory_space=pl.ANY)


def call(kernel, shapes, in_specs, scratch=()):
    shapes = [jax.ShapeDtypeStruct(shape, jnp.float32) for shape in shapes]
    single = len(shapes) == 1
    return pl.pallas_call(
        kernel,
        out_shape=shapes[0] if single else shapes,
        in_specs=in_specs,
        out_specs=VMEM if single else [VMEM] * len(shapes),
        scratch_shapes=scratch,
        compiler_params=pltpu.CompilerParams(vmem_limit_bytes=32 * 1024 * 1024),
    )


def on_device(u_vel, v_vel, density, land_mask, start_hour, levels):
    tables = plan()
    whole = (4, HOURS, ROWS, LANES)
    slots = (OWNERS, SLOT, LANES)
    flat = (OWNERS * SLOT, LANES)
    runs = [[z * GROUP + j for j in range(GROUP)] for z in range(RUNS)]
    across = [[z * GROUP + j for z in range(RUNS)] for j in range(GROUP)]
    fields = (levels, u_vel, v_vel, density, land_mask, start_hour)
    state_scratch = pltpu.VMEM((SERIES * 8, ROWS, LANES), jnp.float32)
    part_scratch = pltpu.VMEM((3, HOURS, ROWS, LANES), jnp.float32)
    own = call(
        summary_kernel,
        [flat],
        [ANY] * 6,
        [
            pltpu.SMEM((4,), jnp.int32),
            pltpu.VMEM(whole, jnp.float32),
            pltpu.VMEM(whole, jnp.float32),
            pltpu.VMEM(whole, jnp.float32),
            pltpu.VMEM((ROWS, LANES), jnp.int32),
            pltpu.VMEM((ROWS, LANES), jnp.int32),
            state_scratch,
            pltpu.SemaphoreType.DMA((6,)),
        ],
    )(*fields)
    blocks = swap(own.reshape(slots), runs, PAIRS)
    totals = call(run_kernel, [(2 * RUNS, SLOT, LANES)], [VMEM] * 3)(blocks, tables["send"], tables["edge_sum"])
    totals = swap(totals, across, FAR)
    borders = call(border_kernel, [slots], [VMEM] * 8)(
        blocks,
        totals,
        tables["gather"],
        tables["local"],
        tables["spread"],
        tables["inject"],
        tables["edge_gather"],
        tables["edge_out"],
    )
    borders = swap(borders, runs, PAIRS).reshape(flat)
    pressure, flux = call(
        band_kernel, [whole, whole], [SMEM] + [VMEM] * 6, [part_scratch, part_scratch, part_scratch, state_scratch]
    )(*fields, borders)
    return (pressure, flux)


def solution(mesh):
    return jax.shard_map(
        on_device,
        mesh=mesh,
        in_specs=(
            P(None, "tm", None, "col"),
            P(None, "tm", None, "col"),
            P(None, "tm", None, "col"),
            P(None, "col"),
            P(None, "col"),
            P(),
        ),
        out_specs=(P(None, "tm", None, "col"), P(None, "tm", None, "col")),
        check_vma=False,
    )
```

time: 78.5 us -> 73.2 us (0.932)
  starting transfers between devices: 16.7 us -> 0 us
  blocking collectives: 48.1 us -> 59.8 us
  waiting for transfers between devices: 1.3 us -> 0 us
    ppermute x2 -> x0, starting transfers between devices: 16.7 us -> none  [the longest x1 13.9 us: on_device(): west = lax.ppermute(edges, 'col', [(i, i + 1) for i in range(count - 1)])]
    all_to_all x3, blocking collectives: 48.1 us -> 59.8 us  [swap(): lax.all_to_all(array, ('tm', 'col'), 0, 0, tiled=True, axis_index_groups=...]
    ppermute x2 -> x0, waiting for transfers between devices: 1.3 us -> none  [the longest x1 1.3 us: on_device(): west = lax.ppermute(edges, 'col', [(i, i + 1) for i in range(count - 1)])]
    pallas_call x5 -> x4, Pallas kernels: 5.56 us -> 6.15 us  [the longest x1 2.82 us: on_device(): call(band_kernel, [whole, whole], [SMEM] + [VMEM] * 6, [part_scratch, par...]
    unnamed x30 -> x40, local copies, waits for them, and re-layouts: 5.57 us -> 5.58 us
  transfers between devices with their start and end apart: 2 -> 0, of which waited for: 1 -> 0; matrix products, arithmetic and copies ran while one was open for 0% -> 0% of each run, Pallas kernels for 0% -> 0%
where the time goes in v2:
time: 73.2 us; the launch traced here: 72.3 us
  blocking collectives  59.8 us (82%)
  Pallas kernels  6.15 us (8%)
  local copies, waits for them, and re-layouts  5.58 us (8%)
  between operations  0.81 us (1%)
    all_to_all x3, blocking collectives, swap(): lax.all_to_all(array, ('tm', 'col'), 0, 0, tiled=True, axis_index_groups=...  59.8 us
    unnamed x40, local copies, waits for them, and re-layouts  5.58 us
    pallas_call x1, Pallas kernels, on_device(): call(band_kernel, [whole, whole], [SMEM] + [VMEM] * 6, [part_scratch, par...  2.82 us
    pallas_call x1, Pallas kernels, on_device(): call(summary_kernel, [flat], [ANY] * 6, [pltpu.SMEM((4,), jnp.int32), plt...  1.62 us

profile of v2, /device:TPU:6, one launch (start us, length us, event | category | flops | bytes accessed | tf_op | source)
XLA Modules:
  0.0 72.3 jit_solution(8582982192105427537)
XLA Ops:
  0.6 0.0 copy-start
  0.6 0.9 %copy-done = f32[4,16,8,128]{3,2,1,0:T(8,128)S(1)} copy-done((f32[4,16,8,128]{3,2,1,0:T(8,128)S(1)}, f32[4,16,8,128]{3,2,1,0:T(8,128)}, u32[]{:S(2)}) %copy-start) | copy-done | bytes 262168
  1.6 0.0 copy-start.2
  1.6 0.9 %copy-done.2 = f32[4,16,8,128]{3,2,1,0:T(8,128)S(1)} copy-done((f32[4,16,8,128]{3,2,1,0:T(8,128)S(1)}, f32[4,16,8,128]{3,2,1,0:T(8,128)}, u32[]{:S(2)}) %copy-start.2) | copy-done | bytes 262168
  2.5 0.0 copy-start.4
  2.5 0.9 %copy-done.4 = f32[4,16,8,128]{3,2,1,0:T(8,128)S(1)} copy-done((f32[4,16,8,128]{3,2,1,0:T(8,128)S(1)}, f32[4,16,8,128]{3,2,1,0:T(8,128)}, u32[]{:S(2)}) %copy-start.4) | copy-done | bytes 262168
  3.5 0.0 copy-start.14
  3.5 0.7 copy-done.14
  4.2 0.0 copy-start.16
  4.2 0.7 copy-done.16
  4.9 0.0 copy-start.18
  4.9 0.7 copy-done.18
  5.5 1.6 %shard_map.149 = f32[768,128]{1,0:T(8,128)S(1)} custom-call(s32[4]{0:T(128)S(1)} %copy-done.18, f32[4,16,8,128]{3,2,1,0:T(8,128)S(1)} %copy-done, f32[4,16,8,128]{3,2,1,0:T(8,128)S(1)} %copy-done.2, f32[4,16,8,128]{3,2,1,0:T(8,128)S(1)} %copy-done.4, s32[8,128]{1,0:T(8,128)S(1)} %copy-done.14, s32[8,128]{1,0:T(8,128)S(1)} %copy-done.16), custom_call_target="tpu_custom_call" | custom-call | tf_op jit(solution)/shard_map/pallas_call | solution.py:520
  7.1 0.0 copy-start.9
  7.2 0.0 copy-start.12
  7.2 0.0 copy-start.11
  7.2 16.3 %all_to_all.15.in_ref = f32[32,24,128]{2,1,0:T(8,128)S(1)} all-to-all(f32[32,24,128]{2,1,0:T(8,128)S(1)} %bitcast.3), channel_id=1, replica_groups={{0,1,8,9,16,17,24,25,32,33,40,41,48,49,56,57,64,65,72,73,80,81,88,89,96..., dimensions={0} | all-to-all | bytes 786432 | tf_op jit(solution)/shard_map/all_to_all | solution.py:489
  23.5 0.0 copy-done.9
  23.5 0.0 copy-done.12
  23.5 0.0 copy-start.6
  23.5 0.0 copy-start.7
  23.5 0.0 copy-start.13
  23.5 0.3 shard_map.150
  23.9 0.0 copy-start.8
  23.9 0.0 copy-start.10
  23.9 29.5 %all_to_all.16.runs_ref = f32[8,24,128]{2,1,0:T(8,128)S(1)} all-to-all(f32[8,24,128]{2,1,0:T(8,128)S(1)} %shard_map.150), channel_id=1, replica_groups={{1,2,129,130,257,258,385,386},{3,4,131,132,259,260,387,388},{5,6,133,13..., dimensions={0} | all-to-all | bytes 196608 | tf_op jit(solution)/shard_map/all_to_all | solution.py:489
  53.5 0.0 copy-done.11
  53.5 0.0 copy-done.6
  53.5 0.0 copy-done.7
  53.5 0.0 copy-done.13
  53.5 0.0 copy-done.8
  53.5 0.0 copy-done.10
  53.5 0.0 copy-start.15
  53.5 0.0 copy-start.17
  53.5 1.4 %shard_map.151 = f32[32,24,128]{2,1,0:T(8,128)S(1)} custom-call(f32[32,24,128]{2,1,0:T(8,128)S(1)} %all_to_all.15.in_ref, f32[8,24,128]{2,1,0:T(8,128)S(1)} %all_to_all.16.runs_ref, f32[4,16,32]{2,1,0:T(8,128)S(1)} %copy-done.13, f32[4,16,256]{2,1,0:T(8,128)S(1)} %copy-done.11, f32[128,128]{1,0:T(8,128)S(1)} %copy-done.10, f32[2,128,16]{2,1,0:T(8,128)S(1)} %copy-done.8, ...), custom_call_target="tpu_custom_call" | custom-call | tf_op jit(solution)/shard_map/pallas_call | solution.py:538
  54.9 0.0 copy-start.1
  54.9 0.0 copy-start.3
  54.9 0.0 copy-start.5
  54.9 13.9 %all_to_all.17 = f32[32,24,128]{2,1,0:T(8,128)S(1)} all-to-all(f32[32,24,128]{2,1,0:T(8,128)S(1)} %shard_map.151), channel_id=1, replica_groups={{0,1,8,9,16,17,24,25,32,33,40,41,48,49,56,57,64,65,72,73,80,81,88,89,96..., dimensions={0} | all-to-all | bytes 786432 | tf_op jit(solution)/shard_map/all_to_all | solution.py:489
  68.9 0.0 copy-start.19
  68.9 0.0 copy-done.15
  68.9 0.0 copy-done.17
  68.9 0.0 copy-done.1
  68.9 0.0 copy-done.3
  68.9 0.0 copy-done.5
  68.9 0.6 copy-done.19
  69.5 2.8 %shard_map.152 = (f32[4,16,8,128]{3,2,1,0:T(8,128)}, f32[4,16,8,128]{3,2,1,0:T(8,128)}) custom-call(s32[4]{0:T(128)S(1)} %copy-done.19, f32[4,16,8,128]{3,2,1,0:T(8,128)S(1)} %copy-done.1, f32[4,16,8,128]{3,2,1,0:T(8,128)S(1)} %copy-done.3, f32[4,16,8,128]{3,2,1,0:T(8,128)S(1)} %copy-done.5, s32[8,128]{1,0:T(8,128)S(1)} %copy-done.15, ...), custom_call_target="tpu_custom_call" | custom-call | tf_op jit(solution)/shard_map/pallas_call | solution.py:549
Async XLA Ops:
  0.6 1.0 %copy-start = (f32[4,16,8,128]{3,2,1,0:T(8,128)S(1)}, f32[4,16,8,128]{3,2,1,0:T(8,128)}, u32[]{:S(2)}) copy-start(f32[4,16,8,128]{3,2,1,0:T(8,128)} %u_ref.1) | copy-start | bytes 786436
  1.6 0.9 %copy-start.2 = (f32[4,16,8,128]{3,2,1,0:T(8,128)S(1)}, f32[4,16,8,128]{3,2,1,0:T(8,128)}, u32[]{:S(2)}) copy-start(f32[4,16,8,128]{3,2,1,0:T(8,128)} %v_ref.1) | copy-start | bytes 786436
  2.5 0.9 %copy-start.4 = (f32[4,16,8,128]{3,2,1,0:T(8,128)S(1)}, f32[4,16,8,128]{3,2,1,0:T(8,128)}, u32[]{:S(2)}) copy-start(f32[4,16,8,128]{3,2,1,0:T(8,128)} %rho_ref.1) | copy-start | bytes 786436
  3.5 0.7 copy-start.14
  4.2 0.7 copy-start.16
  4.9 0.7 copy-start.18
  7.1 16.4 %copy-start.9 = (f32[256,128]{1,0:T(8,128)S(1)}, f32[256,128]{1,0:T(8,128)}, u32[]{:S(2)}) copy-start(f32[256,128]{1,0:T(8,128)} %constant.17.clone.edge_sum_ref) | copy-start | bytes 393220
  7.2 16.4 %copy-start.12 = (f32[4,16,256]{2,1,0:T(8,128)S(1)}, f32[4,16,256]{2,1,0:T(8,128)}, u32[]{:S(2)}) copy-start(f32[4,16,256]{2,1,0:T(8,128)} %constant.16.clone.send_ref) | copy-start | bytes 196612
  7.2 46.3 %copy-start.11 = (f32[4,16,256]{2,1,0:T(8,128)S(1)}, f32[4,16,256]{2,1,0:T(8,128)}, u32[]{:S(2)}) copy-start(f32[4,16,256]{2,1,0:T(8,128)} %constant.19.clone.local_ref) | copy-start | bytes 196612
  23.5 30.0 %copy-start.6 = (f32[384,256]{1,0:T(8,128)S(1)}, f32[384,256]{1,0:T(8,128)}, u32[]{:S(2)}) copy-start(f32[384,256]{1,0:T(8,128)} %constant.23.clone.edge_out_ref) | copy-start | bytes 1179652
  23.5 30.0 %copy-start.7 = (f32[4,128,128]{2,1,0:T(8,128)S(1)}, f32[4,128,128]{2,1,0:T(8,128)}, u32[]{:S(2)}) copy-start(f32[4,128,128]{2,1,0:T(8,128)} %constant.22.clone.edge_gather_ref) | copy-start | bytes 786436
  23.5 30.0 %copy-start.13 = (f32[4,16,32]{2,1,0:T(8,128)S(1)}, f32[4,16,32]{2,1,0:T(8,128)}, u32[]{:S(2)}) copy-start(f32[4,16,32]{2,1,0:T(8,128)} %constant.18.clone.gather_ref) | copy-start | bytes 24580
  23.9 29.6 %copy-start.8 = (f32[2,128,16]{2,1,0:T(8,128)S(1)}, f32[2,128,16]{2,1,0:T(8,128)}, u32[]{:S(2)}) copy-start(f32[2,128,16]{2,1,0:T(8,128)} %constant.21.clone.inject_ref) | copy-start | bytes 49156
  23.9 29.6 %copy-start.10 = (f32[128,128]{1,0:T(8,128)S(1)}, f32[128,128]{1,0:T(8,128)}, u32[]{:S(2)}) copy-start(f32[128,128]{1,0:T(8,128)} %constant.20.clone.spread_ref) | copy-start | bytes 196612
  53.5 15.3 %copy-start.15 = (s32[8,128]{1,0:T(8,128)S(1)}, s32[8,128]{1,0:T(8,128)}, u32[]{:S(2)}) copy-start(s32[8,128]{1,0:T(8,128)} %mask_ref.1) | copy-start | bytes 12292
  53.5 15.3 %copy-start.17 = (s32[8,128]{1,0:T(8,128)S(1)}, s32[8,128]{1,0:T(8,128)}, u32[]{:S(2)}) copy-start(s32[8,128]{1,0:T(8,128)} %start_ref.1) | copy-start | bytes 12292
  54.9 14.0 %copy-start.1 = (f32[4,16,8,128]{3,2,1,0:T(8,128)S(1)}, f32[4,16,8,128]{3,2,1,0:T(8,128)}, u32[]{:S(2)}) copy-start(f32[4,16,8,128]{3,2,1,0:T(8,128)} %u_ref.1) | copy-start | bytes 786436
  54.9 14.0 %copy-start.3 = (f32[4,16,8,128]{3,2,1,0:T(8,128)S(1)}, f32[4,16,8,128]{3,2,1,0:T(8,128)}, u32[]{:S(2)}) copy-start(f32[4,16,8,128]{3,2,1,0:T(8,128)} %v_ref.1) | copy-start | bytes 786436
  54.9 13.9 %copy-start.5 = (f32[4,16,8,128]{3,2,1,0:T(8,128)S(1)}, f32[4,16,8,128]{3,2,1,0:T(8,128)}, u32[]{:S(2)}) copy-start(f32[4,16,8,128]{3,2,1,0:T(8,128)} %rho_ref.1) | copy-start | bytes 786436
  68.9 0.7 copy-start.19

commit v3 on v2

--- a/solution.py
+++ b/solution.py
@@ -115,7 +115,12 @@
 @functools.lru_cache(maxsize=None)
 def plan():
     amat, bvec, cvec, direct = filter_design()
-    summary, coupling, step, _, _ = block_maps(HOURS)
+    summary, coupling, step, _, entering = block_maps(HOURS)
+    basis = []
+    for sign in (1.0, -1.0):
+        part = np.linalg.svd(entering + sign * entering[::-1])[0][:, :4]
+        basis.append(part)
+    coordinates = np.concatenate(basis, axis=1).T @ entering
     own = GROUP * 8
     forward = np.zeros((GROUP + 1, 4, own + 8))
     forward[0][:, own : own + 4] = np.eye(4)
@@ -171,6 +176,8 @@
                 came = power(run_step, other - z - 1)
                 edge_gather[z, from_right, 4:8] = came.T
                 edge_gather[z, from_left, 4:8] = (came @ run_step @ suffix[RUNS - 1 - other]).T
+    for j in range(GROUP):
+        inner[j * 8 : j * 8 + 8] = coordinates @ inner[j * 8 : j * 8 + 8]
     spread = inner[:, :own]
     inject = np.zeros((2, own, 16))
     for tile in range(2):
@@ -178,9 +185,9 @@
         inject[tile, :, 8 + 4 * tile : 12 + 4 * tile] = inner[:, own + 4 :]
     edge_sum = np.zeros((SPAN, LANES))
     edge_sum[:, QUARTER : QUARTER + 8] = run_summary.T
-    edge_out = np.zeros((SPAN + LANES, SPAN))
-    edge_out[:SPAN] = response.T
-    edge_out[SPAN : SPAN + 8] = injected.T
+    edge_response = response.T
+    edge_inject = np.zeros((LANES, SPAN))
+    edge_inject[:8] = injected.T
     tables = dict(
         send=send,
         local=local,
@@ -189,10 +196,11 @@
         inject=inject,
         edge_sum=edge_sum,
         edge_gather=edge_gather,
-        edge_out=edge_out,
+        edge_response=edge_response,
+        edge_inject=edge_inject,
     )
     tables = {name: table.astype(np.float32) for name, table in tables.items()}
-    return dict(tables, amat=amat, cvec=cvec, direct=direct, summary=summary)
+    return dict(tables, amat=amat, cvec=cvec, direct=direct, summary=summary, even=basis[0], odd=basis[1])
 
 
 def place():
@@ -256,7 +264,7 @@
 
 
 def summary_kernel(
-    levels_hbm, u_hbm, v_hbm, rho_hbm, mask_hbm, start_hbm, out_ref, levels_ref, u_ref, v_ref, rho_ref, mask_ref, start_ref, sums_ref, sems
+    levels_hbm, u_hbm, v_hbm, rho_hbm, mask_hbm, start_hbm, out_ref, kept_ref, levels_ref, u_ref, v_ref, rho_ref, mask_ref, start_ref, sums_ref, sems
 ):
     summary = plan()["summary"]
     copies = [
@@ -290,11 +298,11 @@
                 field = pressures(field, depth)
             values = anomalies(field, live[hour])
             for level, value in enumerate(values):
+                kept_ref[which * 3 + level, hour] = value
                 for k in range(8):
                     term = float(summary[k, hour]) * value
                     sums[level][k] = term if hour == 0 else sums[level][k] + term
-            if which < 2:
-                for level, value in enumerate(values + [last_level(values)]):
+                if which < 2:
                     turned = turn(value, QUARTER + hour)
                     at = which * 4 + level
                     west[at] = jnp.where(lane == QUARTER + hour, turned, west[at])
@@ -302,6 +310,9 @@
         for level in range(3):
             for k in range(8):
                 sums_ref[(which * 3 + level) * 8 + k] = sums[level][k]
+    for ends in (west, east):
+        for at in (0, 4):
+            ends[at + 3] = last_level(ends[at : at + 3])
     first = lane < QUARTER
     for k in range(8):
         for v in range(2):
@@ -313,6 +324,40 @@
         for index, quarter in enumerate(QUARTERS):
             part = jnp.where(first, turn(single, -QUARTER * quarter), others.get(quarter, 0.0))
             out_ref[pl.ds(index * SLOT + 16 + k, ROWS, stride=4 * SLOT), :] = part
+
+
+def filter_steps(samples):
+    amat, cvec, direct = plan()["amat"], plan()["cvec"], plan()["direct"]
+    out = [direct * samples[0]]
+    state = [samples[0], None, samples[0], None]
+    for sample in samples[1:]:
+        value = direct * sample
+        for k in range(4):
+            if state[k] is not None:
+                value = value + float(cvec[k]) * state[k]
+        out.append(value)
+        fresh = []
+        for first in (0, 2):
+            real, imag = float(amat[first, first]), float(amat[first + 1, first])
+            if state[first + 1] is None:
+                fresh.append(real * state[first] + sample)
+                fresh.append(imag * state[first])
+            else:
+                fresh.append((real * state[first] - imag * state[first + 1]) + sample)
+                fresh.append(imag * state[first] + real * state[first + 1])
+        state = fresh
+    return out
+
+
+def response_kernel(kept_ref, out_ref):
+    def one(s, carry):
+        samples = filter_steps([kept_ref[s, hour] for hour in range(HOURS)])
+        samples = filter_steps(samples[::-1])[::-1]
+        for hour in range(HOURS):
+            out_ref[s, hour] = samples[hour]
+        return carry
+
+    lax.fori_loop(0, SERIES, one, 0)
 
 
 def blocks_of(in_ref, tile):
@@ -362,7 +407,16 @@
                 out_ref[2 * other + slot_side, pl.ds(v * 8, 8), :] = jnp.where(side == slot_side, mine, across)
 
 
-def edge_flux(in_ref, runs_ref, run, tile, side, edge_gather, edge_out):
+def inner_kernel(in_ref, local_ref, spread_ref, edge_response_ref, base_ref, states_ref, near_ref):
+    run, tile, _ = place()
+    tiles = [blocks_of(in_ref, 0), blocks_of(in_ref, 1)]
+    for which in range(2):
+        base_ref[which] = dot(spread_ref[...], tiles[which])
+    states_ref[...] = dot(local_ref[run], jnp.concatenate(tiles, axis=0))
+    near_ref[...] = dot(edge_hours(in_ref, 1 - tile), edge_response_ref[...])
+
+
+def edge_flux(runs_ref, near, run, side, edge_gather, edge_response, edge_inject):
     lane = lanes_of()
     own = [runs_ref[2 * other + side, pl.ds(16, 8), :] for other in range(RUNS)]
     across = [runs_ref[2 * other + 1 - side, pl.ds(16, 8), :] for other in range(RUNS)]
@@ -372,28 +426,33 @@
         for other in range(RUNS):
             total = jnp.where(lane // 8 == other, turn(parts[other], other * 8 - QUARTER), total)
         sums.append(total)
+    far = jnp.concatenate([runs_ref[2 * run + 1 - side, pl.ds(v * 8, 8), :] for v in range(2)], axis=1)
+    far = dot(far, edge_response)
     states = dot(jnp.concatenate(sums, axis=0), edge_gather)
-    near = edge_hours(in_ref, 1 - tile)
-    far = jnp.concatenate([runs_ref[2 * run + 1 - side, pl.ds(v * 8, 8), :] for v in range(2)], axis=1)
-    hours = jnp.concatenate([near, far], axis=0)
-    banded = dot(jnp.concatenate([hours, states], axis=1), edge_out)
+    added = dot(states, edge_inject)
     row = lax.broadcasted_iota(jnp.int32, (ROWS, SPAN), 0)
-    products = [part * pltpu.roll(part, 4, 0) for part in (banded[0:8], banded[8:16])]
+    products = [part * pltpu.roll(part, 4, 0) for part in (near + added[0:8], far + added[8:16])]
     return jnp.where(row < 4, products[0], products[1])
 
 
 def border_kernel(
-    in_ref, runs_ref, gather_ref, local_ref, spread_ref, inject_ref, edge_gather_ref, edge_out_ref, out_ref
+    base_ref, states_ref, near_ref, runs_ref, gather_ref, inject_ref, edge_gather_ref, edge_response_ref, edge_inject_ref, out_ref
 ):
     run, tile, side = place()
-    flux = edge_flux(in_ref, runs_ref, run, tile, side, edge_gather_ref[run], edge_out_ref[...])
-    tiles = [blocks_of(in_ref, 0), blocks_of(in_ref, 1)]
-    runs = jnp.concatenate([runs_ref[2 * other + side].reshape(3, 8, LANES) for other in range(RUNS)], axis=1)
-    runs = jnp.concatenate([runs[v] for v in range(3)], axis=1)
-    states = dot(gather_ref[run], runs) + dot(local_ref[run], jnp.concatenate(tiles, axis=0))
+    flux = edge_flux(
+        runs_ref, near_ref[...], run, side, edge_gather_ref[run], edge_response_ref[...], edge_inject_ref[...]
+    )
+    runs = jnp.concatenate(
+        [
+            jnp.concatenate([runs_ref[2 * other + side, pl.ds(v * 8, 8), :] for other in range(RUNS)], axis=0)
+            for v in range(3)
+        ],
+        axis=1,
+    )
+    states = dot(gather_ref[run], runs) + states_ref[...]
     first = lanes_of() < QUARTER
     for which in range(2):
-        borders = dot(spread_ref[...], tiles[which]) + dot(inject_ref[which], states)
+        borders = base_ref[which] + dot(inject_ref[which], states)
         for j in range(GROUP):
             for v in range(3):
                 value = borders[j * 8 : j * 8 + 8, v * LANES : (v + 1) * LANES]
@@ -403,31 +462,10 @@
                 out_ref[2 * j + which, pl.ds(v * 8, 8), :] = value
 
 
-def filter_steps(state, samples):
-    amat, cvec, direct = plan()["amat"], plan()["cvec"], plan()["direct"]
-    out = []
-    for sample in samples:
-        value = direct * sample
-        for k in range(4):
-            value = value + float(cvec[k]) * state[k]
-        out.append(value)
-        fresh = []
-        for first in (0, 2):
-            real, imag = float(amat[first, first]), float(amat[first + 1, first])
-            fresh.append((real * state[first] - imag * state[first + 1]) + sample)
-            fresh.append(imag * state[first] + real * state[first + 1])
-        state = fresh
-    return out
-
-
-def band_kernel(
-    levels_ref, u_ref, v_ref, rho_ref, mask_ref, start_ref, borders_ref, press_ref, flux_ref, held, east, north, states_ref
-):
+def band_kernel(response_ref, mask_ref, borders_ref, press_hbm, flux_hbm, press_ref, flux_ref, states_ref, sems):
     _, tile, _ = place()
     column = lax.axis_index("col")
-    mask = mask_ref[...]
-    live = live_hours(mask, start_ref[...])
-    depth = depths(levels_ref)
+    even, odd = plan()["even"], plan()["odd"]
     lane = lanes_of()
     for k in range(8):
         for v in range(3):
@@ -442,22 +480,8 @@
                 for quarter in range(1, 4):
                     total = jnp.where(lane // QUARTER == quarter, turn(parts[quarter], QUARTER * quarter), total)
                 states_ref[64 + k] = total
-    for which, ref in ((1, rho_ref), (0, u_ref), (2, v_ref)):
-        for hour in range(HOURS):
-            field = [ref[level, hour] for level in range(4)]
-            if which == 1:
-                field = pressures(field, depth)
-            for level, value in enumerate(anomalies(field, live[hour])):
-                held[level, hour] = value
-        target = (east, press_ref, north)[which]
-        for level in range(3):
-            states = [states_ref[(which * 3 + level) * 8 + k] for k in range(8)]
-            samples = filter_steps(states[:4], [held[level, hour] for hour in range(HOURS)])
-            samples = filter_steps(states[4:], samples[::-1])[::-1]
-            for hour in range(HOURS):
-                target[level, hour] = samples[hour]
     row = lax.broadcasted_iota(jnp.int32, (ROWS, LANES), 0)
-    half = 0.5 * mask.astype(jnp.float32)
+    half = 0.5 * mask_ref[...].astype(jnp.float32)
     last = lane == LANES - 1
     halos = []
     for level in range(4):
@@ -466,22 +490,45 @@
         from_west = jnp.where(column == 0, 0.0, jnp.where(tile == 0, far, near))
         from_east = jnp.where(column == 2 * len(PAIRS) - 1, 0.0, jnp.where(tile == 0, near, far))
         halos.append((from_west, from_east))
-    for hour in range(HOURS):
-        u_all = [east[level, hour] for level in range(3)]
-        v_all = [north[level, hour] for level in range(3)]
-        p_all = [press_ref[level, hour] for level in range(3)]
-        for values in (u_all, v_all, p_all):
-            values.append(last_level(values))
-        press_ref[3, hour] = p_all[3]
-        for level in range(4):
-            fx = u_all[level] * p_all[level]
-            fy = v_all[level] * p_all[level]
-            from_west, from_east = halos[level]
-            next_x = jnp.where(last, turn(from_east, LANES - 1 - QUARTER - hour), turn(fx, -1))
-            prev_x = jnp.where(lane == 0, turn(from_west, -QUARTER - hour), turn(fx, 1))
-            next_y = jnp.where(row == ROWS - 1, 0.0, pltpu.roll(fy, ROWS - 1, 0))
-            prev_y = jnp.where(row == 0, 0.0, pltpu.roll(fy, 1, 0))
-            flux_ref[level, hour] = half * ((next_x - prev_x) + (next_y - prev_y))
+    copies = []
+    for early in range(HOURS // 2):
+        late = HOURS - 1 - early
+        banded = {early: [], late: []}
+        for s in range(SERIES):
+            states = [states_ref[s * 8 + k] for k in range(8)]
+            sums = []
+            for table, first in ((even, 0), (odd, 4)):
+                total = float(table[early, 0]) * states[first]
+                for k in range(1, 4):
+                    total = total + float(table[early, k]) * states[first + k]
+                sums.append(total)
+            banded[early].append(response_ref[s, early] + (sums[0] + sums[1]))
+            banded[late].append(response_ref[s, late] + (sums[0] - sums[1]))
+        for hour in (early, late):
+            u_all, p_all, v_all = (banded[hour][at : at + 3] for at in (0, 3, 6))
+            for values in (u_all, v_all, p_all):
+                values.append(last_level(values))
+            for level in range(4):
+                press_ref[level, hour] = p_all[level]
+                fx = u_all[level] * p_all[level]
+                fy = v_all[level] * p_all[level]
+                from_west, from_east = halos[level]
+                next_x = jnp.where(last, turn(from_east, LANES - 1 - QUARTER - hour), turn(fx, -1))
+                prev_x = jnp.where(lane == 0, turn(from_west, -QUARTER - hour), turn(fx, 1))
+                next_y = jnp.where(row == ROWS - 1, 0.0, pltpu.roll(fy, ROWS - 1, 0))
+                prev_y = jnp.where(row == 0, 0.0, pltpu.roll(fy, 1, 0))
+                flux_ref[level, hour] = half * ((next_x - prev_x) + (next_y - prev_y))
+        if early % 2 == 1:
+            for begin in (early - 1, late):
+                for source, target in ((press_ref, press_hbm), (flux_ref, flux_hbm)):
+                    copies.append(
+                        pltpu.make_async_copy(
+                            source.at[:, pl.ds(begin, 2)], target.at[:, pl.ds(begin, 2)], sems.at[len(copies)]
+                        )
+                    )
+                    copies[-1].start()
+    for copy in copies:
+        copy.wait()
 
 
 def swap(array, devices, columns):
@@ -490,19 +537,18 @@
 
 
 VMEM = pl.BlockSpec(memory_space=pltpu.VMEM)
-SMEM = pl.BlockSpec(memory_space=pltpu.SMEM)
-ANY = pl.BlockSpec(memory_space=pl.ANY)
-
-
-def call(kernel, shapes, in_specs, scratch=()):
-    shapes = [jax.ShapeDtypeStruct(shape, jnp.float32) for shape in shapes]
-    single = len(shapes) == 1
+HBM = pl.BlockSpec(memory_space=pltpu.HBM)
+
+
+def call(kernel, shapes, in_specs, scratch=(), out_spec=None, flops=10**6, moved=10**6):
+    out_spec = VMEM if out_spec is None else out_spec
     return pl.pallas_call(
         kernel,
-        out_shape=shapes[0] if single else shapes,
+        out_shape=[jax.ShapeDtypeStruct(shape, jnp.float32) for shape in shapes],
         in_specs=in_specs,
-        out_specs=VMEM if single else [VMEM] * len(shapes),
+        out_specs=[out_spec] * len(shapes),
         scratch_shapes=scratch,
+        cost_estimate=pl.CostEstimate(flops=flops, bytes_accessed=moved, transcendentals=0),
         compiler_params=pltpu.CompilerParams(vmem_limit_bytes=32 * 1024 * 1024),
     )
 
@@ -510,17 +556,16 @@
 def on_device(u_vel, v_vel, density, land_mask, start_hour, levels):
     tables = plan()
     whole = (4, HOURS, ROWS, LANES)
+    series = (SERIES, HOURS, ROWS, LANES)
     slots = (OWNERS, SLOT, LANES)
     flat = (OWNERS * SLOT, LANES)
     runs = [[z * GROUP + j for j in range(GROUP)] for z in range(RUNS)]
     across = [[z * GROUP + j for z in range(RUNS)] for j in range(GROUP)]
-    fields = (levels, u_vel, v_vel, density, land_mask, start_hour)
     state_scratch = pltpu.VMEM((SERIES * 8, ROWS, LANES), jnp.float32)
-    part_scratch = pltpu.VMEM((3, HOURS, ROWS, LANES), jnp.float32)
-    own = call(
+    own, kept = call(
         summary_kernel,
-        [flat],
-        [ANY] * 6,
+        [flat, series],
+        [HBM] * 6,
         [
             pltpu.SMEM((4,), jnp.int32),
             pltpu.VMEM(whole, jnp.float32),
@@ -531,24 +576,38 @@
             state_scratch,
             pltpu.SemaphoreType.DMA((6,)),
         ],
-    )(*fields)
+    )(levels, u_vel, v_vel, density, land_mask, start_hour)
     blocks = swap(own.reshape(slots), runs, PAIRS)
-    totals = call(run_kernel, [(2 * RUNS, SLOT, LANES)], [VMEM] * 3)(blocks, tables["send"], tables["edge_sum"])
+    (response,) = call(response_kernel, [series], [VMEM], flops=7 * 10**6)(kept)
+    (totals,) = call(run_kernel, [(2 * RUNS, SLOT, LANES)], [VMEM] * 3)(blocks, tables["send"], tables["edge_sum"])
     totals = swap(totals, across, FAR)
-    borders = call(border_kernel, [slots], [VMEM] * 8)(
-        blocks,
+    base, states, near = call(
+        inner_kernel, [(2, GROUP * 8, 3 * LANES), (16, 3 * LANES), (ROWS, SPAN)], [VMEM] * 4, flops=3 * 10**7
+    )(blocks, tables["local"], tables["spread"], tables["edge_response"])
+    (borders,) = call(border_kernel, [slots], [VMEM] * 9)(
+        base,
+        states,
+        near,
         totals,
         tables["gather"],
-        tables["local"],
-        tables["spread"],
         tables["inject"],
         tables["edge_gather"],
-        tables["edge_out"],
+        tables["edge_response"],
+        tables["edge_inject"],
     )
     borders = swap(borders, runs, PAIRS).reshape(flat)
     pressure, flux = call(
-        band_kernel, [whole, whole], [SMEM] + [VMEM] * 6, [part_scratch, part_scratch, part_scratch, state_scratch]
-    )(*fields, borders)
+        band_kernel,
+        [whole, whole],
+        [VMEM] * 3,
+        [
+            pltpu.VMEM(whole, jnp.float32),
+            pltpu.VMEM(whole, jnp.float32),
+            state_scratch,
+            pltpu.SemaphoreType.DMA((HOURS,)),
+        ],
+        out_spec=HBM,
+    )(response, land_mask, borders)
     return (pressure, flux)
 
 

time: 73.2 us -> 72.9 us (level)
  blocking collectives: 59.8 us -> 16.3 us
  waiting for transfers between devices: 0 us -> 22 us
  starting transfers between devices: 0 us -> 20 us
  Pallas kernels: 6.15 us -> 7.9 us
    all_to_all x3 -> x1, blocking collectives: 59.8 us -> 16.3 us  [swap(): lax.all_to_all(array, ('tm', 'col'), 0, 0, tiled=True, axis_index_groups=...]
    all_to_all x0 -> x2, waiting for transfers between devices: none -> 22 us  [swap(): lax.all_to_all(array, ('tm', 'col'), 0, 0, tiled=True, axis_index_groups=...]
    all_to_all x0 -> x2, starting transfers between devices: none -> 20 us  [swap(): lax.all_to_all(array, ('tm', 'col'), 0, 0, tiled=True, axis_index_groups=...]
    pallas_call x3 -> x5, Pallas kernels: 5.8 us -> 6.91 us  [the longest x1 1.96 us: on_device(): call(band_kernel, [whole, whole], [VMEM] * 3, [pltpu.VMEM(whole, jnp.floa...]
    unnamed x40 -> x32, local copies, waits for them, and re-layouts: 5.58 us -> 4.93 us
  transfers between devices with their start and end apart: 0 -> 2, of which waited for: 0 -> 2; matrix products, arithmetic and copies ran while one was open for 0% -> 0% of each run, Pallas kernels for 0% -> 2%
where the time goes in v3:
time: 72.9 us; the launch traced here: 71.9 us
  waiting for transfers between devices  22 us (30%)
  starting transfers between devices  20 us (27%)
  blocking collectives  16.3 us (22%)
  Pallas kernels  7.9 us (11%)
  local copies, waits for them, and re-layouts  4.93 us (7%)
  between operations  0.76 us (1%)
    all_to_all x2, waiting for transfers between devices, swap(): lax.all_to_all(array, ('tm', 'col'), 0, 0, tiled=True, axis_index_groups=...  22 us
    all_to_all x2, starting transfers between devices, swap(): lax.all_to_all(array, ('tm', 'col'), 0, 0, tiled=True, axis_index_groups=...  20 us
    all_to_all x1, blocking collectives, swap(): lax.all_to_all(array, ('tm', 'col'), 0, 0, tiled=True, axis_index_groups=...  16.3 us
    unnamed x32, local copies, waits for them, and re-layouts  4.93 us
    pallas_call x1, Pallas kernels, on_device(): call(band_kernel, [whole, whole], [VMEM] * 3, [pltpu.VMEM(whole, jnp.floa...  1.96 us
    pallas_call x1, Pallas kernels, on_device(): call(border_kernel, [slots], [VMEM] * 9)  1.71 us
    pallas_call x1, Pallas kernels, on_device(): call(summary_kernel, [flat, series], [HBM] * 6, [pltpu.SMEM((4,), jnp.int...  1.61 us
  transfers between devices with their start and end apart: 2, of which 2 were waited for; matrix products, arithmetic and copies ran while one was open for 0% of the time, Pallas kernels for 2%

profile of v3, /device:TPU:6, one launch (start us, length us, event | category | flops | bytes accessed | tf_op | source)
XLA Modules:
  0.0 71.9 jit_solution(9407574481664578386)
XLA Ops:
  0.6 0.0 copy-start.1
  0.6 0.9 %copy-done.1 = f32[4,16,8,128]{3,2,1,0:T(8,128)S(1)} copy-done((f32[4,16,8,128]{3,2,1,0:T(8,128)S(1)}, f32[4,16,8,128]{3,2,1,0:T(8,128)}, u32[]{:S(2)}) %copy-start.1) | copy-done | bytes 262168
  1.6 0.0 copy-start.2
  1.6 0.9 %copy-done.2 = f32[4,16,8,128]{3,2,1,0:T(8,128)S(1)} copy-done((f32[4,16,8,128]{3,2,1,0:T(8,128)S(1)}, f32[4,16,8,128]{3,2,1,0:T(8,128)}, u32[]{:S(2)}) %copy-start.2) | copy-done | bytes 262168
  2.5 0.0 copy-start.3
  2.5 0.9 %copy-done.3 = f32[4,16,8,128]{3,2,1,0:T(8,128)S(1)} copy-done((f32[4,16,8,128]{3,2,1,0:T(8,128)S(1)}, f32[4,16,8,128]{3,2,1,0:T(8,128)}, u32[]{:S(2)}) %copy-start.3) | copy-done | bytes 262168
  3.5 0.0 copy-start.12
  3.5 0.7 copy-done.12
  4.2 0.0 copy-start.14
  4.2 0.7 copy-done.14
  4.9 0.0 copy-start.15
  4.9 0.7 copy-done.15
  5.5 1.6 %shard_map.158 = (f32[768,128]{1,0:T(8,128)S(1)}, f32[9,16,8,128]{3,2,1,0:T(8,128)S(1)}) custom-call(s32[4]{0:T(128)S(1)} %copy-done.15, f32[4,16,8,128]{3,2,1,0:T(8,128)S(1)} %copy-done.1, f32[4,16,8,128]{3,2,1,0:T(8,128)S(1)} %copy-done.2, f32[4,16,8,128]{3,2,1,0:T(8,128)S(1)} %copy-done.3, s32[8,128]{1,0:T(8,128)S(1)} %copy-done.12, s32[8,128]{1,0:T(8,128)S(1)} %copy-done.14), custom_call_target="tpu_custom_call" | custom-call | flops 1000000 | bytes 1000000 | tf_op jit(solution)/shard_map/pallas_call | solution.py:565
  7.1 0.0 copy-start.5
  7.1 0.0 copy-start.10
  7.2 16.3 %all_to_all.15.in_ref = f32[32,24,128]{2,1,0:T(8,128)S(1)} all-to-all(f32[32,24,128]{2,1,0:T(8,128)S(1)} %bitcast.3), channel_id=1, replica_groups={{0,1,8,9,16,17,24,25,32,33,40,41,48,49,56,57,64,65,72,73,80,81,88,89,96..., dimensions={0} | all-to-all | bytes 786432 | tf_op jit(solution)/shard_map/all_to_all | solution.py:536
  23.5 0.0 copy-done.5
  23.5 0.0 copy-done.10
  23.5 0.0 copy-start
  23.5 1.0 %shard_map.161 = f32[8,24,128]{2,1,0:T(8,128)} custom-call(f32[32,24,128]{2,1,0:T(8,128)S(1)} %all_to_all.15.in_ref, f32[4,16,256]{2,1,0:T(8,128)S(1)} %copy-done.10, f32[256,128]{1,0:T(8,128)S(1)} %copy-done.5), custom_call_target="tpu_custom_call" | custom-call | flops 1000000 | bytes 1000000 | tf_op jit(solution)/shard_map/pallas_call | solution.py:582
  24.5 0.0 copy-start.8
  24.5 0.0 copy-start.9
  24.5 15.0 %all-to-all-start.1 = ((f32[8,24,128]{2,1,0:T(8,128)}), f32[8,24,128]{2,1,0:T(8,128)S(1)}, u32[]{:S(2)}, u32[]{:S(2)}) async-start(f32[8,24,128]{2,1,0:T(8,128)} %shard_map.161), calls=%async_computation.1 | async-start | bytes 196608 | tf_op jit(solution)/shard_map/all_to_all | solution.py:536
  39.5 0.0 copy-done
  39.5 0.0 copy-done.8
  39.5 0.0 copy-done.9
  39.6 0.0 copy-start.4
  39.6 0.0 copy-start.6
  39.6 0.0 copy-start.7
  39.6 0.0 copy-start.11
  39.6 0.7 %shard_map.160 = (f32[2,128,384]{2,1,0:T(8,128)S(1)}, f32[16,384]{1,0:T(8,128)S(1)}, f32[8,256]{1,0:T(8,128)S(1)}) custom-call(f32[32,24,128]{2,1,0:T(8,128)S(1)} %all_to_all.15.in_ref, f32[4,16,256]{2,1,0:T(8,128)S(1)} %copy-done.9, f32[128,128]{1,0:T(8,128)S(1)} %copy-done.8, f32[256,256]{1,0:T(8,128)S(1)} %copy-done), custom_call_target="tpu_custom_call" | custom-call | flops 30000000 | bytes 1000000 | tf_op jit(solution)/shard_map/pallas_call | solution.py:584
  40.3 13.9 %all-to-all-done.1.runs_ref = f32[8,24,128]{2,1,0:T(8,128)S(1)} async-done(((f32[8,24,128]{2,1,0:T(8,128)}), f32[8,24,128]{2,1,0:T(8,128)S(1)}, u32[]{:S(2)}, u32[]{:S(2)}) %all-to-all-start.1) | async-done | bytes 98336 | tf_op jit(solution)/shard_map/all_to_all | solution.py:536
  54.2 0.0 copy-done.4
  54.3 0.0 copy-done.6
  54.3 0.0 copy-done.7
  54.3 0.0 copy-done.11
  54.3 1.7 %shard_map.162 = f32[32,24,128]{2,1,0:T(8,128)} custom-call(f32[2,128,384]{2,1,0:T(8,128)S(1)} %get-tuple-element.9.base_ref, f32[16,384]{1,0:T(8,128)S(1)} %get-tuple-element.10.states_ref, f32[8,256]{1,0:T(8,128)S(1)} %get-tuple-element.11.near_ref, f32[8,24,128]{2,1,0:T(8,128)S(1)} %all-to-all-done.1.runs_ref, f32[4,16,32]{2,1,0:T(8,128)S(1)} %copy-done.11, ...), custom_call_target="tpu_custom_call" | custom-call | flops 1000000 | bytes 1000000 | tf_op jit(solution)/shard_map/pallas_call | solution.py:587
  56.0 5.0 %all-to-all-start.2 = ((f32[32,24,128]{2,1,0:T(8,128)}), f32[32,24,128]{2,1,0:T(8,128)S(1)}, u32[]{:S(2)}, u32[]{:S(2)}) async-start(f32[32,24,128]{2,1,0:T(8,128)} %shard_map.162), calls=%async_computation.2 | async-start | bytes 786432 | tf_op jit(solution)/shard_map/all_to_all | solution.py:536
  61.0 0.0 copy-start.13
  61.0 0.9 %shard_map.159.response_ref = f32[9,16,8,128]{3,2,1,0:T(8,128)S(1)} custom-call(f32[9,16,8,128]{3,2,1,0:T(8,128)S(1)} %get-tuple-element.7.kept_ref), custom_call_target="tpu_custom_call" | custom-call | flops 7000000 | bytes 1000000 | tf_op jit(solution)/shard_map/pallas_call | solution.py:581
  61.9 8.0 %all-to-all-done.2 = f32[32,24,128]{2,1,0:T(8,128)S(1)} async-done(((f32[32,24,128]{2,1,0:T(8,128)}), f32[32,24,128]{2,1,0:T(8,128)S(1)}, u32[]{:S(2)}, u32[]{:S(2)}) %all-to-all-start.2) | async-done | bytes 393248 | tf_op jit(solution)/shard_map/all_to_all | solution.py:536
  70.0 0.0 copy-done.13
  70.0 2.0 %shard_map.163 = (f32[4,16,8,128]{3,2,1,0:T(8,128)}, f32[4,16,8,128]{3,2,1,0:T(8,128)}) custom-call(f32[9,16,8,128]{3,2,1,0:T(8,128)S(1)} %shard_map.159.response_ref, s32[8,128]{1,0:T(8,128)S(1)} %copy-done.13, f32[768,128]{1,0:T(8,128)S(1)} %bitcast.2), custom_call_target="tpu_custom_call" | custom-call | flops 1000000 | bytes 1000000 | tf_op jit(solution)/shard_map/pallas_call | solution.py:599
Async XLA Ops:
  0.6 1.0 %copy-start.1 = (f32[4,16,8,128]{3,2,1,0:T(8,128)S(1)}, f32[4,16,8,128]{3,2,1,0:T(8,128)}, u32[]{:S(2)}) copy-start(f32[4,16,8,128]{3,2,1,0:T(8,128)} %u_hbm.1) | copy-start | bytes 786436
  1.6 0.9 %copy-start.2 = (f32[4,16,8,128]{3,2,1,0:T(8,128)S(1)}, f32[4,16,8,128]{3,2,1,0:T(8,128)}, u32[]{:S(2)}) copy-start(f32[4,16,8,128]{3,2,1,0:T(8,128)} %v_hbm.1) | copy-start | bytes 786436
  2.5 0.9 %copy-start.3 = (f32[4,16,8,128]{3,2,1,0:T(8,128)S(1)}, f32[4,16,8,128]{3,2,1,0:T(8,128)}, u32[]{:S(2)}) copy-start(f32[4,16,8,128]{3,2,1,0:T(8,128)} %rho_hbm.1) | copy-start | bytes 786436
  3.5 0.7 copy-start.12
  4.2 0.7 copy-start.14
  4.9 0.7 copy-start.15
  7.1 16.4 %copy-start.5 = (f32[256,128]{1,0:T(8,128)S(1)}, f32[256,128]{1,0:T(8,128)}, u32[]{:S(2)}) copy-start(f32[256,128]{1,0:T(8,128)} %constant.19.clone.edge_sum_ref) | copy-start | bytes 393220
  7.1 16.4 %copy-start.10 = (f32[4,16,256]{2,1,0:T(8,128)S(1)}, f32[4,16,256]{2,1,0:T(8,128)}, u32[]{:S(2)}) copy-start(f32[4,16,256]{2,1,0:T(8,128)} %constant.18.clone.send_ref) | copy-start | bytes 196612
  23.5 16.0 %copy-start = (f32[256,256]{1,0:T(8,128)S(1)}, f32[256,256]{1,0:T(8,128)}, u32[]{:S(2)}) copy-start(f32[256,256]{1,0:T(8,128)} %constant.22.clone.edge_response_ref) | copy-start | bytes 786436
  24.5 15.0 %copy-start.8 = (f32[128,128]{1,0:T(8,128)S(1)}, f32[128,128]{1,0:T(8,128)}, u32[]{:S(2)}) copy-start(f32[128,128]{1,0:T(8,128)} %constant.21.clone.spread_ref) | copy-start | bytes 196612
  24.5 15.0 %copy-start.9 = (f32[4,16,256]{2,1,0:T(8,128)S(1)}, f32[4,16,256]{2,1,0:T(8,128)}, u32[]{:S(2)}) copy-start(f32[4,16,256]{2,1,0:T(8,128)} %constant.20.clone.local_ref) | copy-start | bytes 196612
  24.5 29.7 %all-to-all-start.1 = ((f32[8,24,128]{2,1,0:T(8,128)}), f32[8,24,128]{2,1,0:T(8,128)S(1)}, u32[]{:S(2)}, u32[]{:S(2)}) async-start(f32[8,24,128]{2,1,0:T(8,128)} %shard_map.161), calls=%async_computation.1 | async-start | bytes 196608 | tf_op jit(solution)/shard_map/all_to_all | solution.py:536
  39.6 14.7 %copy-start.4 = (f32[4,128,128]{2,1,0:T(8,128)S(1)}, f32[4,128,128]{2,1,0:T(8,128)}, u32[]{:S(2)}) copy-start(f32[4,128,128]{2,1,0:T(8,128)} %constant.25.clone.edge_gather_ref) | copy-start | bytes 786436
  39.6 14.7 %copy-start.6 = (f32[128,256]{1,0:T(8,128)S(1)}, f32[128,256]{1,0:T(8,128)}, u32[]{:S(2)}) copy-start(f32[128,256]{1,0:T(8,128)} %constant.26.clone.edge_inject_ref) | copy-start | bytes 393220
  39.6 14.7 %copy-start.7 = (f32[2,128,16]{2,1,0:T(8,128)S(1)}, f32[2,128,16]{2,1,0:T(8,128)}, u32[]{:S(2)}) copy-start(f32[2,128,16]{2,1,0:T(8,128)} %constant.24.clone.inject_ref) | copy-start | bytes 49156
  39.6 14.7 %copy-start.11 = (f32[4,16,32]{2,1,0:T(8,128)S(1)}, f32[4,16,32]{2,1,0:T(8,128)}, u32[]{:S(2)}) copy-start(f32[4,16,32]{2,1,0:T(8,128)} %constant.23.clone.gather_ref) | copy-start | bytes 24580
  56.0 14.0 %all-to-all-start.2 = ((f32[32,24,128]{2,1,0:T(8,128)}), f32[32,24,128]{2,1,0:T(8,128)S(1)}, u32[]{:S(2)}, u32[]{:S(2)}) async-start(f32[32,24,128]{2,1,0:T(8,128)} %shard_map.162), calls=%async_computation.2 | async-start | bytes 786432 | tf_op jit(solution)/shard_map/all_to_all | solution.py:536
  61.0 9.0 %copy-start.13 = (s32[8,128]{1,0:T(8,128)S(1)}, s32[8,128]{1,0:T(8,128)}, u32[]{:S(2)}) copy-start(s32[8,128]{1,0:T(8,128)} %mask_ref.1) | copy-start | bytes 12292

commit v4 on v3

--- a/solution.py
+++ b/solution.py
@@ -544,7 +544,10 @@
     out_spec = VMEM if out_spec is None else out_spec
     return pl.pallas_call(
         kernel,
-        out_shape=[jax.ShapeDtypeStruct(shape, jnp.float32) for shape in shapes],
+        out_shape=[
+            jax.ShapeDtypeStruct(shape, jnp.float32) if out_spec is HBM else pltpu.VMEM(shape, jnp.float32)
+            for shape in shapes
+        ],
         in_specs=in_specs,
         out_specs=[out_spec] * len(shapes),
         scratch_shapes=scratch,
@@ -562,6 +565,7 @@
     runs = [[z * GROUP + j for j in range(GROUP)] for z in range(RUNS)]
     across = [[z * GROUP + j for z in range(RUNS)] for j in range(GROUP)]
     state_scratch = pltpu.VMEM((SERIES * 8, ROWS, LANES), jnp.float32)
+    arguments = (levels, u_vel, v_vel, density, land_mask, start_hour)
     own, kept = call(
         summary_kernel,
         [flat, series],
@@ -576,7 +580,7 @@
             state_scratch,
             pltpu.SemaphoreType.DMA((6,)),
         ],
-    )(levels, u_vel, v_vel, density, land_mask, start_hour)
+    )(*[pltpu.with_memory_space_constraint(array, pltpu.HBM) for array in arguments])
     blocks = swap(own.reshape(slots), runs, PAIRS)
     (response,) = call(response_kernel, [series], [VMEM], flops=7 * 10**6)(kept)
     (totals,) = call(run_kernel, [(2 * RUNS, SLOT, LANES)], [VMEM] * 3)(blocks, tables["send"], tables["edge_sum"])

time: 72.9 us -> 68.3 us (0.937)
  local copies, waits for them, and re-layouts: 4.93 us -> 0.06 us
    unnamed x32 -> x20, local copies, waits for them, and re-layouts: 4.93 us -> 0.06 us
where the time goes in v4:
time: 68.3 us; the launch traced here: 67.5 us
  waiting for transfers between devices  22 us (32%)
  starting transfers between devices  20 us (29%)
  blocking collectives  16.3 us (24%)
  Pallas kernels  8.32 us (12%)
  between operations  0.75 us (1%)
    all_to_all x2, waiting for transfers between devices, swap(): lax.all_to_all(array, ('tm', 'col'), 0, 0, tiled=True, axis_index_groups=...  22 us
    all_to_all x2, starting transfers between devices, swap(): lax.all_to_all(array, ('tm', 'col'), 0, 0, tiled=True, axis_index_groups=...  20 us
    all_to_all x1, blocking collectives, swap(): lax.all_to_all(array, ('tm', 'col'), 0, 0, tiled=True, axis_index_groups=...  16.3 us
    pallas_call x1, Pallas kernels, on_device(): call(summary_kernel, [flat, series], [HBM] * 6, [pltpu.SMEM((4,), jnp.int...  2.03 us
    pallas_call x1, Pallas kernels, on_device(): call(band_kernel, [whole, whole], [VMEM] * 3, [pltpu.VMEM(whole, jnp.floa...  1.96 us
    pallas_call x1, Pallas kernels, on_device(): call(border_kernel, [slots], [VMEM] * 9)  1.71 us
  transfers between devices with their start and end apart: 2, of which 2 were waited for; matrix products, arithmetic and copies ran while one was open for 0% of the time, Pallas kernels for 2%

profile of v4, /device:TPU:6, one launch (start us, length us, event | category | flops | bytes accessed | tf_op | source)
XLA Modules:
  0.0 67.5 jit_solution(16108206174686240133)
XLA Ops:
  0.6 2.0 %shard_map.158 = (f32[768,128]{1,0:T(8,128)S(1)}, f32[9,16,8,128]{3,2,1,0:T(8,128)S(1)}) custom-call(s32[4]{0:T(128)} %levels_hbm.1, f32[4,16,8,128]{3,2,1,0:T(8,128)} %u_hbm.1, f32[4,16,8,128]{3,2,1,0:T(8,128)} %v_hbm.1, f32[4,16,8,128]{3,2,1,0:T(8,128)} %rho_hbm.1, s32[8,128]{1,0:T(8,128)} %mask_ref.1, s32[8,128]{1,0:T(8,128)} %start_hbm.1), custom_call_target="tpu_custom_call" | custom-call | flops 1000000 | bytes 1000000 | tf_op jit(solution)/shard_map/pallas_call | solution.py:569
  2.7 0.0 copy-start.2
  2.7 0.0 copy-start.7
  2.7 16.3 %all_to_all.15.in_ref = f32[32,24,128]{2,1,0:T(8,128)S(1)} all-to-all(f32[32,24,128]{2,1,0:T(8,128)S(1)} %bitcast.3), channel_id=1, replica_groups={{0,1,8,9,16,17,24,25,32,33,40,41,48,49,56,57,64,65,72,73,80,81,88,89,96..., dimensions={0} | all-to-all | bytes 786432 | tf_op jit(solution)/shard_map/all_to_all | solution.py:536
  19.0 0.0 copy-done.2
  19.0 0.0 copy-done.7
  19.0 0.0 copy-start
  19.0 1.0 %shard_map.161 = f32[8,24,128]{2,1,0:T(8,128)} custom-call(f32[32,24,128]{2,1,0:T(8,128)S(1)} %all_to_all.15.in_ref, f32[4,16,256]{2,1,0:T(8,128)S(1)} %copy-done.7, f32[256,128]{1,0:T(8,128)S(1)} %copy-done.2), custom_call_target="tpu_custom_call" | custom-call | flops 1000000 | bytes 1000000 | tf_op jit(solution)/shard_map/pallas_call | solution.py:586
  20.0 0.0 copy-start.5
  20.0 0.0 copy-start.6
  20.0 15.0 %all-to-all-start.1 = ((f32[8,24,128]{2,1,0:T(8,128)}), f32[8,24,128]{2,1,0:T(8,128)S(1)}, u32[]{:S(2)}, u32[]{:S(2)}) async-start(f32[8,24,128]{2,1,0:T(8,128)} %shard_map.161), calls=%async_computation.1 | async-start | bytes 196608 | tf_op jit(solution)/shard_map/all_to_all | solution.py:536
  35.1 0.0 copy-done
  35.1 0.0 copy-done.5
  35.1 0.0 copy-done.6
  35.1 0.0 copy-start.1
  35.1 0.0 copy-start.3
  35.1 0.0 copy-start.4
  35.1 0.0 copy-start.8
  35.1 0.7 %shard_map.160 = (f32[2,128,384]{2,1,0:T(8,128)S(1)}, f32[16,384]{1,0:T(8,128)S(1)}, f32[8,256]{1,0:T(8,128)S(1)}) custom-call(f32[32,24,128]{2,1,0:T(8,128)S(1)} %all_to_all.15.in_ref, f32[4,16,256]{2,1,0:T(8,128)S(1)} %copy-done.6, f32[128,128]{1,0:T(8,128)S(1)} %copy-done.5, f32[256,256]{1,0:T(8,128)S(1)} %copy-done), custom_call_target="tpu_custom_call" | custom-call | flops 30000000 | bytes 1000000 | tf_op jit(solution)/shard_map/pallas_call | solution.py:588
  35.9 13.9 %all-to-all-done.1.runs_ref = f32[8,24,128]{2,1,0:T(8,128)S(1)} async-done(((f32[8,24,128]{2,1,0:T(8,128)}), f32[8,24,128]{2,1,0:T(8,128)S(1)}, u32[]{:S(2)}, u32[]{:S(2)}) %all-to-all-start.1) | async-done | bytes 98336 | tf_op jit(solution)/shard_map/all_to_all | solution.py:536
  49.8 0.0 copy-done.1
  49.8 0.0 copy-done.3
  49.8 0.0 copy-done.4
  49.8 0.0 copy-done.8
  49.8 1.7 %shard_map.162 = f32[32,24,128]{2,1,0:T(8,128)} custom-call(f32[2,128,384]{2,1,0:T(8,128)S(1)} %get-tuple-element.9.base_ref, f32[16,384]{1,0:T(8,128)S(1)} %get-tuple-element.10.states_ref, f32[8,256]{1,0:T(8,128)S(1)} %get-tuple-element.11.near_ref, f32[8,24,128]{2,1,0:T(8,128)S(1)} %all-to-all-done.1.runs_ref, f32[4,16,32]{2,1,0:T(8,128)S(1)} %copy-done.8, ...), custom_call_target="tpu_custom_call" | custom-call | flops 1000000 | bytes 1000000 | tf_op jit(solution)/shard_map/pallas_call | solution.py:591
  51.5 5.0 %all-to-all-start.2 = ((f32[32,24,128]{2,1,0:T(8,128)}), f32[32,24,128]{2,1,0:T(8,128)S(1)}, u32[]{:S(2)}, u32[]{:S(2)}) async-start(f32[32,24,128]{2,1,0:T(8,128)} %shard_map.162), calls=%async_computation.2 | async-start | bytes 786432 | tf_op jit(solution)/shard_map/all_to_all | solution.py:536
  56.5 0.0 copy-start.9
  56.5 0.9 %shard_map.159.response_ref = f32[9,16,8,128]{3,2,1,0:T(8,128)S(1)} custom-call(f32[9,16,8,128]{3,2,1,0:T(8,128)S(1)} %get-tuple-element.7.kept_ref), custom_call_target="tpu_custom_call" | custom-call | flops 7000000 | bytes 1000000 | tf_op jit(solution)/shard_map/pallas_call | solution.py:585
  57.5 8.0 %all-to-all-done.2 = f32[32,24,128]{2,1,0:T(8,128)S(1)} async-done(((f32[32,24,128]{2,1,0:T(8,128)}), f32[32,24,128]{2,1,0:T(8,128)S(1)}, u32[]{:S(2)}, u32[]{:S(2)}) %all-to-all-start.2) | async-done | bytes 393248 | tf_op jit(solution)/shard_map/all_to_all | solution.py:536
  65.5 0.0 copy-done.9
  65.5 2.0 %shard_map.163 = (f32[4,16,8,128]{3,2,1,0:T(8,128)}, f32[4,16,8,128]{3,2,1,0:T(8,128)}) custom-call(f32[9,16,8,128]{3,2,1,0:T(8,128)S(1)} %shard_map.159.response_ref, s32[8,128]{1,0:T(8,128)S(1)} %copy-done.9, f32[768,128]{1,0:T(8,128)S(1)} %bitcast.2), custom_call_target="tpu_custom_call" | custom-call | flops 1000000 | bytes 1000000 | tf_op jit(solution)/shard_map/pallas_call | solution.py:603
Async XLA Ops:
  2.7 16.4 %copy-start.2 = (f32[256,128]{1,0:T(8,128)S(1)}, f32[256,128]{1,0:T(8,128)}, u32[]{:S(2)}) copy-start(f32[256,128]{1,0:T(8,128)} %constant.19.clone.edge_sum_ref) | copy-start | bytes 393220
  2.7 16.4 %copy-start.7 = (f32[4,16,256]{2,1,0:T(8,128)S(1)}, f32[4,16,256]{2,1,0:T(8,128)}, u32[]{:S(2)}) copy-start(f32[4,16,256]{2,1,0:T(8,128)} %constant.18.clone.send_ref) | copy-start | bytes 196612
  19.0 16.0 %copy-start = (f32[256,256]{1,0:T(8,128)S(1)}, f32[256,256]{1,0:T(8,128)}, u32[]{:S(2)}) copy-start(f32[256,256]{1,0:T(8,128)} %constant.22.clone.edge_response_ref) | copy-start | bytes 786436
  20.0 15.0 %copy-start.5 = (f32[128,128]{1,0:T(8,128)S(1)}, f32[128,128]{1,0:T(8,128)}, u32[]{:S(2)}) copy-start(f32[128,128]{1,0:T(8,128)} %constant.21.clone.spread_ref) | copy-start | bytes 196612
  20.0 15.0 %copy-start.6 = (f32[4,16,256]{2,1,0:T(8,128)S(1)}, f32[4,16,256]{2,1,0:T(8,128)}, u32[]{:S(2)}) copy-start(f32[4,16,256]{2,1,0:T(8,128)} %constant.20.clone.local_ref) | copy-start | bytes 196612
  20.0 29.7 %all-to-all-start.1 = ((f32[8,24,128]{2,1,0:T(8,128)}), f32[8,24,128]{2,1,0:T(8,128)S(1)}, u32[]{:S(2)}, u32[]{:S(2)}) async-start(f32[8,24,128]{2,1,0:T(8,128)} %shard_map.161), calls=%async_computation.1 | async-start | bytes 196608 | tf_op jit(solution)/shard_map/all_to_all | solution.py:536
  35.1 14.7 %copy-start.1 = (f32[4,128,128]{2,1,0:T(8,128)S(1)}, f32[4,128,128]{2,1,0:T(8,128)}, u32[]{:S(2)}) copy-start(f32[4,128,128]{2,1,0:T(8,128)} %constant.25.clone.edge_gather_ref) | copy-start | bytes 786436
  35.1 14.7 %copy-start.3 = (f32[128,256]{1,0:T(8,128)S(1)}, f32[128,256]{1,0:T(8,128)}, u32[]{:S(2)}) copy-start(f32[128,256]{1,0:T(8,128)} %constant.26.clone.edge_inject_ref) | copy-start | bytes 393220
  35.1 14.7 %copy-start.4 = (f32[2,128,16]{2,1,0:T(8,128)S(1)}, f32[2,128,16]{2,1,0:T(8,128)}, u32[]{:S(2)}) copy-start(f32[2,128,16]{2,1,0:T(8,128)} %constant.24.clone.inject_ref) | copy-start | bytes 49156
  35.1 14.7 %copy-start.8 = (f32[4,16,32]{2,1,0:T(8,128)S(1)}, f32[4,16,32]{2,1,0:T(8,128)}, u32[]{:S(2)}) copy-start(f32[4,16,32]{2,1,0:T(8,128)} %constant.23.clone.gather_ref) | copy-start | bytes 24580
  51.5 14.0 %all-to-all-start.2 = ((f32[32,24,128]{2,1,0:T(8,128)}), f32[32,24,128]{2,1,0:T(8,128)S(1)}, u32[]{:S(2)}, u32[]{:S(2)}) async-start(f32[32,24,128]{2,1,0:T(8,128)} %shard_map.162), calls=%async_computation.2 | async-start | bytes 786432 | tf_op jit(solution)/shard_map/all_to_all | solution.py:536
  56.5 9.0 %copy-start.9 = (s32[8,128]{1,0:T(8,128)S(1)}, s32[8,128]{1,0:T(8,128)}, u32[]{:S(2)}) copy-start(s32[8,128]{1,0:T(8,128)} %mask_ref.1) | copy-start | bytes 12292

commit v5 on v2

--- a/solution.py
+++ b/solution.py
@@ -17,7 +17,7 @@
 ROWS = 8
 LANES = 128
 QUARTER = 32
-SLOT = 24
+SLOT = 19
 SPAN = GROUP * HOURS
 QUARTERS = (0, 3, 1, 2)
 PAIRS = ((0, 1), (2, 3), (4, 5), (6, 7))
@@ -112,9 +112,19 @@
     return summary, back @ entering, powers[hours], response, injected
 
 
+def direct_form():
+    amat, _, cvec, _ = filter_design()
+    denom = np.poly(amat)
+    outputs = [cvec @ power(amat, hour) for hour in range(4)]
+    rows = [sum(denom[lag] * outputs[row - lag] for lag in range(row + 1)) for row in range(4)]
+    return denom, np.stack(rows)
+
+
 @functools.lru_cache(maxsize=None)
 def plan():
-    amat, bvec, cvec, direct = filter_design()
+    gain = filter_design()[3]
+    scale = gain * gain
+    denom, to_direct = direct_form()
     summary, coupling, step, _, _ = block_maps(HOURS)
     own = GROUP * 8
     forward = np.zeros((GROUP + 1, 4, own + 8))
@@ -129,26 +139,33 @@
         backward[j][:, j * 8 + 4 : j * 8 + 8] += np.eye(4)
     inner = np.zeros((own, own + 8))
     for j in range(GROUP):
-        inner[j * 8 : j * 8 + 4] = forward[j]
-        inner[j * 8 + 4 : j * 8 + 8] = backward[j + 1]
+        inner[j * 8 : j * 8 + 4] = gain * to_direct @ forward[j]
+        inner[j * 8 + 4 : j * 8 + 8] = to_direct @ backward[j + 1]
     run_left = forward[GROUP][:, :own]
     run_right = backward[0][:, :own]
     run_summary, run_coupling, run_step, response, injected = block_maps(SPAN)
+    swapped = [j * 8 + k for k in range(8) for j in range(GROUP)]
     suffix = [np.zeros((4, 4))]
     for m in range(RUNS):
         suffix.append(suffix[-1] + power(run_step, m) @ run_coupling @ power(run_step, m))
     send = np.zeros((RUNS, 16, 2 * own))
     local = np.zeros((RUNS, 16, 2 * own))
     gather = np.zeros((RUNS, 16, RUNS * 8))
+    send_ninth = np.zeros((RUNS, 16, own))
+    local_ninth = np.zeros((RUNS, 16, own))
     edge_gather = np.zeros((RUNS, LANES, LANES))
     for z in range(RUNS):
         after = suffix[RUNS - 1 - z]
+        right = run_right + run_step @ after @ run_left
+        send_ninth[z, 0:4] = run_left[:, swapped]
+        send_ninth[z, 8:12] = right[:, swapped]
+        local_ninth[z, 8:12] = (after @ run_left)[:, swapped]
         for tile in range(2):
             columns = slice(tile * own, (tile + 1) * own)
             ahead = slice(4 * tile, 4 * tile + 4)
             behind = slice(8 + 4 * tile, 12 + 4 * tile)
             send[z, ahead, columns] = run_left
-            send[z, behind, columns] = run_right + run_step @ after @ run_left
+            send[z, behind, columns] = right
             local[z, behind, columns] = after @ run_left
             for other in range(RUNS):
                 here = slice(other * 8 + 4 * tile, other * 8 + 4 * tile + 4)
@@ -177,22 +194,28 @@
         inject[tile, :, 4 * tile : 4 * tile + 4] = inner[:, own : own + 4]
         inject[tile, :, 8 + 4 * tile : 12 + 4 * tile] = inner[:, own + 4 :]
     edge_sum = np.zeros((SPAN, LANES))
-    edge_sum[:, QUARTER : QUARTER + 8] = run_summary.T
+    edge_sum[:, 2 * QUARTER : 2 * QUARTER + 8] = run_summary.T / scale
+    order = [(j // 8) * 8 + (8 - j % 8) % 8 for j in range(GROUP)]
+    places = [order[j] * HOURS + hour for j in range(GROUP) for hour in range(HOURS)]
     edge_out = np.zeros((SPAN + LANES, SPAN))
-    edge_out[:SPAN] = response.T
-    edge_out[SPAN : SPAN + 8] = injected.T
+    edge_out[:SPAN, places] = response.T / scale
+    edge_out[SPAN : SPAN + 8, places] = injected.T
     tables = dict(
         send=send,
         local=local,
         gather=gather,
         spread=spread,
         inject=inject,
+        send_ninth=send_ninth,
+        local_ninth=local_ninth,
+        spread_ninth=spread[swapped][:, swapped],
+        inject_ninth=inject[0][swapped],
         edge_sum=edge_sum,
         edge_gather=edge_gather,
         edge_out=edge_out,
     )
     tables = {name: table.astype(np.float32) for name, table in tables.items()}
-    return dict(tables, amat=amat, cvec=cvec, direct=direct, summary=summary)
+    return dict(tables, denom=denom, scale=scale, summary=summary / scale)
 
 
 def place():
@@ -204,10 +227,10 @@
     return lax.broadcasted_iota(jnp.int32, shape, 1)
 
 
-def live_hours(mask, start):
+def live_hours(mask, start, scale):
     first = lax.axis_index("tm") * HOURS
     ocean = mask == 1
-    return [jnp.where(ocean & (start <= first + hour), 1.0, 0.0) for hour in range(HOURS)]
+    return [jnp.where(ocean & (start <= first + hour), scale, 0.0) for hour in range(HOURS)]
 
 
 def depths(levels_ref):
@@ -255,10 +278,18 @@
     return out
 
 
+def block_transposed(value, lane):
+    value = pltpu.roll(value, 0, 1, stride=HOURS, stride_axis=0)
+    total = value
+    for block in range(1, 8):
+        total = jnp.where(lane // HOURS == block, pltpu.roll(value, 8 - block, 0), total)
+    return pltpu.roll(total, 0, 1, stride=HOURS, stride_axis=0)
+
+
 def summary_kernel(
-    levels_hbm, u_hbm, v_hbm, rho_hbm, mask_hbm, start_hbm, out_ref, levels_ref, u_ref, v_ref, rho_ref, mask_ref, start_ref, sums_ref, sems
+    levels_hbm, u_hbm, v_hbm, rho_hbm, mask_hbm, start_hbm, out_ref, kept_ref, levels_ref, u_ref, v_ref, rho_ref, mask_ref, start_ref, sums_ref, sems
 ):
-    summary = plan()["summary"]
+    summary, scale = plan()["summary"], float(plan()["scale"])
     copies = [
         pltpu.make_async_copy(source, target, sems.at[index])
         for index, (source, target) in enumerate(
@@ -276,11 +307,11 @@
         copy.start()
     for copy in copies[:3]:
         copy.wait()
-    live = live_hours(mask_ref[...], start_ref[...])
+    live = live_hours(mask_ref[...], start_ref[...], scale)
     depth = depths(levels_ref)
     lane = lanes_of()
-    west = [jnp.zeros((ROWS, LANES), jnp.float32) for _ in range(8)]
-    east = list(west)
+    west = jnp.zeros((ROWS, LANES), jnp.float32)
+    east = west
     for which, ref in enumerate((u_ref, rho_ref, v_ref)):
         copies[3 + which].wait()
         sums = [[None] * 8 for _ in range(3)]
@@ -290,73 +321,85 @@
                 field = pressures(field, depth)
             values = anomalies(field, live[hour])
             for level, value in enumerate(values):
+                kept_ref[which * 3 + level, hour] = value
                 for k in range(8):
                     term = float(summary[k, hour]) * value
                     sums[level][k] = term if hour == 0 else sums[level][k] + term
-            if which < 2:
-                for level, value in enumerate(values + [last_level(values)]):
-                    turned = turn(value, QUARTER + hour)
-                    at = which * 4 + level
-                    west[at] = jnp.where(lane == QUARTER + hour, turned, west[at])
-                    east[at] = jnp.where(lane == QUARTER - 1 + hour, turned, east[at])
+                if which < 2:
+                    position = (8 - which * 4 - level) % 8 * HOURS + hour
+                    turned = turn(value, position)
+                    west = jnp.where(lane == position, turned, west)
+                    east = jnp.where(lane == (position - 1) % LANES, turned, east)
         for level in range(3):
             for k in range(8):
                 sums_ref[(which * 3 + level) * 8 + k] = sums[level][k]
-    first = lane < QUARTER
-    for k in range(8):
-        for v in range(2):
+    edges = []
+    for ends in (west, turn(east, 1)):
+        three = -((turn(ends, -HOURS) + turn(ends, -2 * HOURS)) + turn(ends, -3 * HOURS))
+        block = lane // HOURS
+        edges.append(jnp.where((block == 5) | (block == 1), three, ends))
+    spare = {0: edges[0], 3: edges[1]}
+    for v in range(2):
+        for k in range(8):
             parts = transposed([sums_ref[(4 * v + a) * 8 + k] for a in range(4)], lane)
             for index, quarter in enumerate(QUARTERS):
                 out_ref[pl.ds(index * SLOT + v * 8 + k, ROWS, stride=4 * SLOT), :] = parts[quarter]
-        single = sums_ref[64 + k]
-        others = {0: west[k], 3: turn(east[k], 1)}
+        parts = transposed([sums_ref[64 + 4 * v + a] for a in range(4)], lane)
         for index, quarter in enumerate(QUARTERS):
-            part = jnp.where(first, turn(single, -QUARTER * quarter), others.get(quarter, 0.0))
-            out_ref[pl.ds(index * SLOT + 16 + k, ROWS, stride=4 * SLOT), :] = part
+            out_ref[pl.ds(index * SLOT + 16 + v, ROWS, stride=4 * SLOT), :] = parts[quarter]
+    for index, quarter in enumerate(QUARTERS):
+        out_ref[pl.ds(index * SLOT + 18, ROWS, stride=4 * SLOT), :] = spare.get(
+            quarter, jnp.zeros((ROWS, LANES), jnp.float32)
+        )
 
 
 def blocks_of(in_ref, tile):
     return jnp.concatenate(
         [
-            jnp.concatenate([in_ref[2 * j + tile, pl.ds(v * 8, 8), :] for j in range(GROUP)], axis=0)
-            for v in range(3)
+            jnp.concatenate([in_ref[pl.ds((2 * j + tile) * SLOT + v * 8, 8), :] for j in range(GROUP)], axis=0)
+            for v in range(2)
         ],
         axis=1,
     )
 
 
+def ninth_of(in_ref):
+    first = lanes_of((GROUP, LANES)) < QUARTER
+    parts = []
+    for half in range(2):
+        tiles = [in_ref[pl.ds(tile * SLOT + 16 + half, GROUP, stride=2 * SLOT), :] for tile in range(2)]
+        for a in range(4):
+            parts.append(jnp.where(first, turn(tiles[0], -QUARTER * a), turn(tiles[1], QUARTER - QUARTER * a)))
+    return jnp.concatenate(parts, axis=0)
+
+
 def edge_hours(in_ref, tile):
     lane = lanes_of()
-    halves = []
-    for half in range(2):
-        total = jnp.zeros((ROWS, LANES), jnp.float32)
-        for i in range(8):
-            turned = turn(in_ref[2 * (half * 8 + i) + tile, pl.ds(16, 8), :], i * HOURS - QUARTER)
-            total = jnp.where(lane // HOURS == i, turned, total)
-        halves.append(total)
-    return jnp.concatenate(halves, axis=1)
+    rows = in_ref[pl.ds(tile * SLOT + 18, GROUP, stride=2 * SLOT), :]
+    return jnp.concatenate([block_transposed(rows[half * 8 : half * 8 + 8], lane) for half in range(2)], axis=1)
 
 
 def dot(lhs, rhs):
     return jnp.dot(lhs, rhs, precision=HIGH, preferred_element_type=jnp.float32)
 
 
-def run_kernel(in_ref, send_ref, edge_sum_ref, out_ref):
+def run_kernel(in_ref, send_ref, send_ninth_ref, edge_sum_ref, out_ref):
     run, tile, side = place()
     blocks = jnp.concatenate([blocks_of(in_ref, 0), blocks_of(in_ref, 1)], axis=0)
     totals = dot(send_ref[run], blocks)
+    ninth = dot(send_ninth_ref[run], ninth_of(in_ref))
     near = edge_hours(in_ref, 1 - tile)
     far = edge_hours(in_ref, tile)
     sums = dot(jnp.concatenate([near, far], axis=0), edge_sum_ref[...])
-    first = lanes_of() < QUARTER
+    first = lanes_of() < 2 * QUARTER
     for other in range(RUNS):
         for v in range(3):
             lanes = slice(v * LANES, (v + 1) * LANES)
-            mine = jnp.where(other > run, totals[0:8, lanes], totals[8:16, lanes])
             if v == 2:
-                mine = jnp.where(first, mine, sums[0:8])
+                mine = jnp.where(first, jnp.where(other > run, ninth[0:8], ninth[8:16]), sums[0:8])
                 across = sums[8:16]
             else:
+                mine = jnp.where(other > run, totals[0:8, lanes], totals[8:16, lanes])
                 across = far[:, lanes]
             for slot_side in range(2):
                 out_ref[2 * other + slot_side, pl.ds(v * 8, 8), :] = jnp.where(side == slot_side, mine, across)
@@ -370,7 +413,7 @@
     for parts in (own, across):
         total = jnp.zeros((ROWS, LANES), jnp.float32)
         for other in range(RUNS):
-            total = jnp.where(lane // 8 == other, turn(parts[other], other * 8 - QUARTER), total)
+            total = jnp.where(lane // 8 == other, turn(parts[other], other * 8 - 2 * QUARTER), total)
         sums.append(total)
     states = dot(jnp.concatenate(sums, axis=0), edge_gather)
     near = edge_hours(in_ref, 1 - tile)
@@ -379,109 +422,131 @@
     banded = dot(jnp.concatenate([hours, states], axis=1), edge_out)
     row = lax.broadcasted_iota(jnp.int32, (ROWS, SPAN), 0)
     products = [part * pltpu.roll(part, 4, 0) for part in (banded[0:8], banded[8:16])]
-    return jnp.where(row < 4, products[0], products[1])
+    flux = jnp.where(row < 4, products[0], products[1])
+    return jnp.concatenate(
+        [block_transposed(flux[:, half * LANES : (half + 1) * LANES], lane) for half in range(2)], axis=0
+    )
 
 
 def border_kernel(
-    in_ref, runs_ref, gather_ref, local_ref, spread_ref, inject_ref, edge_gather_ref, edge_out_ref, out_ref
+    in_ref,
+    runs_ref,
+    gather_ref,
+    local_ref,
+    spread_ref,
+    inject_ref,
+    local_ninth_ref,
+    spread_ninth_ref,
+    inject_ninth_ref,
+    edge_gather_ref,
+    edge_out_ref,
+    out_ref,
 ):
     run, tile, side = place()
     flux = edge_flux(in_ref, runs_ref, run, tile, side, edge_gather_ref[run], edge_out_ref[...])
+    runs = [
+        jnp.concatenate([runs_ref[2 * other + side, pl.ds(v * 8, 8), :] for other in range(RUNS)], axis=0)
+        for v in range(3)
+    ]
+    gather = dot(gather_ref[run], jnp.concatenate(runs, axis=1))
     tiles = [blocks_of(in_ref, 0), blocks_of(in_ref, 1)]
-    runs = jnp.concatenate([runs_ref[2 * other + side].reshape(3, 8, LANES) for other in range(RUNS)], axis=1)
-    runs = jnp.concatenate([runs[v] for v in range(3)], axis=1)
-    states = dot(gather_ref[run], runs) + dot(local_ref[run], jnp.concatenate(tiles, axis=0))
-    first = lanes_of() < QUARTER
+    states = gather[:, : 2 * LANES] + dot(local_ref[run], jnp.concatenate(tiles, axis=0))
     for which in range(2):
         borders = dot(spread_ref[...], tiles[which]) + dot(inject_ref[which], states)
         for j in range(GROUP):
-            for v in range(3):
-                value = borders[j * 8 : j * 8 + 8, v * LANES : (v + 1) * LANES]
-                if v == 2:
-                    half = flux[:, (j // 8) * LANES : (j // 8 + 1) * LANES]
-                    value = jnp.where(first, value, turn(half, QUARTER - (j % 8) * HOURS))
-                out_ref[2 * j + which, pl.ds(v * 8, 8), :] = value
+            for v in range(2):
+                out_ref[pl.ds((2 * j + which) * SLOT + v * 8, 8), :] = borders[
+                    j * 8 : j * 8 + 8, v * LANES : (v + 1) * LANES
+                ]
+        out_ref[pl.ds(which * SLOT + 18, GROUP, stride=2 * SLOT), :] = flux
+    ninth = ninth_of(in_ref)
+    states = gather[:, 2 * LANES :] + dot(local_ninth_ref[run], ninth)
+    borders = dot(spread_ninth_ref[...], ninth) + dot(inject_ninth_ref[...], states)
+    block = lanes_of((GROUP, LANES)) // QUARTER
+    for which in range(2):
+        for half in range(2):
+            total = jnp.zeros((GROUP, LANES), jnp.float32)
+            for a in range(4):
+                row = (half * 4 + a) * GROUP
+                total = jnp.where(block == a, turn(borders[row : row + GROUP], QUARTER * (a - which)), total)
+            out_ref[pl.ds(which * SLOT + 16 + half, GROUP, stride=2 * SLOT), :] = total
 
 
 def filter_steps(state, samples):
-    amat, cvec, direct = plan()["amat"], plan()["cvec"], plan()["direct"]
+    _, one, two, three, four = (float(value) for value in plan()["denom"])
+    first, second, third, fourth = state
     out = []
     for sample in samples:
-        value = direct * sample
-        for k in range(4):
-            value = value + float(cvec[k]) * state[k]
+        value = sample + first
         out.append(value)
-        fresh = []
-        for first in (0, 2):
-            real, imag = float(amat[first, first]), float(amat[first + 1, first])
-            fresh.append((real * state[first] - imag * state[first + 1]) + sample)
-            fresh.append(imag * state[first] + real * state[first + 1])
-        state = fresh
+        first = second - one * value
+        second = (third - (sample + sample)) - two * value
+        third = fourth - three * value
+        fourth = sample - four * value
     return out
 
 
 def band_kernel(
-    levels_ref, u_ref, v_ref, rho_ref, mask_ref, start_ref, borders_ref, press_ref, flux_ref, held, east, north, states_ref
+    kept_ref, mask_ref, borders_ref, press_hbm, flux_hbm, press_ref, flux_ref, east_ref, north_ref, states_ref, sems
 ):
     _, tile, _ = place()
     column = lax.axis_index("col")
-    mask = mask_ref[...]
-    live = live_hours(mask, start_ref[...])
-    depth = depths(levels_ref)
     lane = lanes_of()
-    for k in range(8):
-        for v in range(3):
+    for v in range(2):
+        for k in range(8):
             parts = [None] * 4
             for index, quarter in enumerate(QUARTERS):
                 parts[quarter] = borders_ref[pl.ds(index * SLOT + v * 8 + k, ROWS, stride=4 * SLOT), :]
-            if v < 2:
-                for a, part in enumerate(transposed(parts, lane)):
-                    states_ref[(4 * v + a) * 8 + k] = part
-            else:
-                total = parts[0]
-                for quarter in range(1, 4):
-                    total = jnp.where(lane // QUARTER == quarter, turn(parts[quarter], QUARTER * quarter), total)
-                states_ref[64 + k] = total
-    for which, ref in ((1, rho_ref), (0, u_ref), (2, v_ref)):
-        for hour in range(HOURS):
-            field = [ref[level, hour] for level in range(4)]
-            if which == 1:
-                field = pressures(field, depth)
-            for level, value in enumerate(anomalies(field, live[hour])):
-                held[level, hour] = value
-        target = (east, press_ref, north)[which]
+            for a, part in enumerate(transposed(parts, lane)):
+                states_ref[(4 * v + a) * 8 + k] = part
+        for index, quarter in enumerate(QUARTERS):
+            parts[quarter] = borders_ref[pl.ds(index * SLOT + 16 + v, ROWS, stride=4 * SLOT), :]
+        for a, part in enumerate(transposed(parts, lane)):
+            states_ref[64 + 4 * v + a] = part
+    copies = []
+
+    def send(source, target):
+        copies.append(pltpu.make_async_copy(source, target, sems.at[len(copies)]))
+        copies[-1].start()
+
+    for which, target in ((1, press_ref), (0, east_ref), (2, north_ref)):
         for level in range(3):
-            states = [states_ref[(which * 3 + level) * 8 + k] for k in range(8)]
-            samples = filter_steps(states[:4], [held[level, hour] for hour in range(HOURS)])
+            s = which * 3 + level
+            states = [states_ref[s * 8 + k] for k in range(8)]
+            samples = filter_steps(states[:4], [kept_ref[s, hour] for hour in range(HOURS)])
             samples = filter_steps(states[4:], samples[::-1])[::-1]
             for hour in range(HOURS):
                 target[level, hour] = samples[hour]
+        if which == 1:
+            for hour in range(HOURS):
+                press_ref[3, hour] = last_level([press_ref[level, hour] for level in range(3)])
+            send(press_ref, press_hbm)
     row = lax.broadcasted_iota(jnp.int32, (ROWS, LANES), 0)
-    half = 0.5 * mask.astype(jnp.float32)
+    half = 0.5 * mask_ref[...].astype(jnp.float32)
     last = lane == LANES - 1
-    halos = []
-    for level in range(4):
-        near = borders_ref[pl.ds(tile * SLOT + 16 + level, ROWS, stride=4 * SLOT), :]
-        far = borders_ref[pl.ds(tile * SLOT + 20 + level, ROWS, stride=4 * SLOT), :]
-        from_west = jnp.where(column == 0, 0.0, jnp.where(tile == 0, far, near))
-        from_east = jnp.where(column == 2 * len(PAIRS) - 1, 0.0, jnp.where(tile == 0, near, far))
-        halos.append((from_west, from_east))
+    halos = borders_ref[pl.ds(tile * SLOT + 18, ROWS, stride=4 * SLOT), :]
+    halos = jnp.where(tile == 0, turn(halos, 64), halos)
+    outside = ((column == 0) & (lane < 64)) | ((column == 2 * len(PAIRS) - 1) & (lane >= 64))
+    halos = jnp.where(outside, 0.0, halos)
     for hour in range(HOURS):
-        u_all = [east[level, hour] for level in range(3)]
-        v_all = [north[level, hour] for level in range(3)]
-        p_all = [press_ref[level, hour] for level in range(3)]
-        for values in (u_all, v_all, p_all):
+        u_all = [east_ref[level, hour] for level in range(3)]
+        v_all = [north_ref[level, hour] for level in range(3)]
+        p_all = [press_ref[level, hour] for level in range(4)]
+        for values in (u_all, v_all):
             values.append(last_level(values))
-        press_ref[3, hour] = p_all[3]
         for level in range(4):
             fx = u_all[level] * p_all[level]
             fy = v_all[level] * p_all[level]
-            from_west, from_east = halos[level]
-            next_x = jnp.where(last, turn(from_east, LANES - 1 - QUARTER - hour), turn(fx, -1))
-            prev_x = jnp.where(lane == 0, turn(from_west, -QUARTER - hour), turn(fx, 1))
+            position = level * HOURS + hour
+            next_x = jnp.where(last, turn(halos, LANES - 1 - 64 - position), turn(fx, -1))
+            prev_x = jnp.where(lane == 0, turn(halos, -position), turn(fx, 1))
             next_y = jnp.where(row == ROWS - 1, 0.0, pltpu.roll(fy, ROWS - 1, 0))
             prev_y = jnp.where(row == 0, 0.0, pltpu.roll(fy, 1, 0))
             flux_ref[level, hour] = half * ((next_x - prev_x) + (next_y - prev_y))
+        if hour % 4 == 3:
+            send(flux_ref.at[:, pl.ds(hour - 3, 4)], flux_hbm.at[:, pl.ds(hour - 3, 4)])
+    for copy in copies:
+        copy.wait()
 
 
 def swap(array, devices, columns):
@@ -490,18 +555,18 @@
 
 
 VMEM = pl.BlockSpec(memory_space=pltpu.VMEM)
-SMEM = pl.BlockSpec(memory_space=pltpu.SMEM)
-ANY = pl.BlockSpec(memory_space=pl.ANY)
-
-
-def call(kernel, shapes, in_specs, scratch=()):
-    shapes = [jax.ShapeDtypeStruct(shape, jnp.float32) for shape in shapes]
-    single = len(shapes) == 1
+HBM = pl.BlockSpec(memory_space=pltpu.HBM)
+
+
+def call(kernel, shapes, in_specs, scratch=(), out_spec=VMEM):
     return pl.pallas_call(
         kernel,
-        out_shape=shapes[0] if single else shapes,
+        out_shape=[
+            jax.ShapeDtypeStruct(shape, jnp.float32) if out_spec is HBM else pltpu.VMEM(shape, jnp.float32)
+            for shape in shapes
+        ],
         in_specs=in_specs,
-        out_specs=VMEM if single else [VMEM] * len(shapes),
+        out_specs=[out_spec] * len(shapes),
         scratch_shapes=scratch,
         compiler_params=pltpu.CompilerParams(vmem_limit_bytes=32 * 1024 * 1024),
     )
@@ -510,17 +575,17 @@
 def on_device(u_vel, v_vel, density, land_mask, start_hour, levels):
     tables = plan()
     whole = (4, HOURS, ROWS, LANES)
-    slots = (OWNERS, SLOT, LANES)
+    part = (3, HOURS, ROWS, LANES)
     flat = (OWNERS * SLOT, LANES)
+    slots = (OWNERS, 1, SLOT * LANES)
     runs = [[z * GROUP + j for j in range(GROUP)] for z in range(RUNS)]
     across = [[z * GROUP + j for z in range(RUNS)] for j in range(GROUP)]
-    fields = (levels, u_vel, v_vel, density, land_mask, start_hour)
     state_scratch = pltpu.VMEM((SERIES * 8, ROWS, LANES), jnp.float32)
-    part_scratch = pltpu.VMEM((3, HOURS, ROWS, LANES), jnp.float32)
-    own = call(
+    arguments = (levels, u_vel, v_vel, density, land_mask, start_hour)
+    own, kept = call(
         summary_kernel,
-        [flat],
-        [ANY] * 6,
+        [flat, (SERIES, HOURS, ROWS, LANES)],
+        [HBM] * 6,
         [
             pltpu.SMEM((4,), jnp.int32),
             pltpu.VMEM(whole, jnp.float32),
@@ -531,24 +596,41 @@
             state_scratch,
             pltpu.SemaphoreType.DMA((6,)),
         ],
-    )(*fields)
-    blocks = swap(own.reshape(slots), runs, PAIRS)
-    totals = call(run_kernel, [(2 * RUNS, SLOT, LANES)], [VMEM] * 3)(blocks, tables["send"], tables["edge_sum"])
+    )(*[pltpu.with_memory_space_constraint(array, pltpu.HBM) for array in arguments])
+    blocks = swap(own.reshape(slots), runs, PAIRS).reshape(flat)
+    (totals,) = call(run_kernel, [(2 * RUNS, 24, LANES)], [VMEM] * 4)(
+        blocks, tables["send"], tables["send_ninth"], tables["edge_sum"]
+    )
     totals = swap(totals, across, FAR)
-    borders = call(border_kernel, [slots], [VMEM] * 8)(
-        blocks,
-        totals,
-        tables["gather"],
-        tables["local"],
-        tables["spread"],
-        tables["inject"],
-        tables["edge_gather"],
-        tables["edge_out"],
-    )
-    borders = swap(borders, runs, PAIRS).reshape(flat)
+    names = (
+        "gather",
+        "local",
+        "spread",
+        "inject",
+        "local_ninth",
+        "spread_ninth",
+        "inject_ninth",
+        "edge_gather",
+        "edge_out",
+    )
+    (borders,) = call(border_kernel, [flat], [VMEM] * (2 + len(names)))(
+        blocks, totals, *[tables[name] for name in names]
+    )
+    borders = swap(borders.reshape(slots), runs, PAIRS).reshape(flat)
     pressure, flux = call(
-        band_kernel, [whole, whole], [SMEM] + [VMEM] * 6, [part_scratch, part_scratch, part_scratch, state_scratch]
-    )(*fields, borders)
+        band_kernel,
+        [whole, whole],
+        [VMEM] * 3,
+        [
+            pltpu.VMEM(whole, jnp.float32),
+            pltpu.VMEM(whole, jnp.float32),
+            pltpu.VMEM(part, jnp.float32),
+            pltpu.VMEM(part, jnp.float32),
+            state_scratch,
+            pltpu.SemaphoreType.DMA((5,)),
+        ],
+        out_spec=HBM,
+    )(kept, land_mask, borders)
     return (pressure, flux)
 
 

time: 73.2 us -> 65.4 us (0.89)
  local copies, waits for them, and re-layouts: 5.58 us -> 0.09 us
  blocking collectives: 59.8 us -> 58 us
    unnamed x40 -> x26, local copies, waits for them, and re-layouts: 5.58 us -> 0.09 us
    all_to_all x3, blocking collectives: 59.8 us -> 58 us  [swap(): lax.all_to_all(array, ('tm', 'col'), 0, 0, tiled=True, axis_index_groups=...]
where the time goes in v5:
time: 65.4 us; the launch traced here: 64.7 us
  blocking collectives  58 us (89%)
  Pallas kernels  5.84 us (9%)
  between operations  0.81 us (1%)
    all_to_all x3, blocking collectives, swap(): lax.all_to_all(array, ('tm', 'col'), 0, 0, tiled=True, axis_index_groups=...  58 us
    pallas_call x1, Pallas kernels, on_device(): call(band_kernel, [whole, whole], [VMEM] * 3, [pltpu.VMEM(whole, jnp.floa...  1.98 us
    pallas_call x1, Pallas kernels, on_device(): call(summary_kernel, [flat, (SERIES, HOURS, ROWS, LANES)], [HBM] * 6, [pl...  1.81 us
    pallas_call x1, Pallas kernels, on_device(): call(border_kernel, [flat], [VMEM] * (2 + len(names)))  1.66 us

profile of v5, /device:TPU:6, one launch (start us, length us, event | category | flops | bytes accessed | tf_op | source)
XLA Modules:
  0.0 64.7 jit_solution(3638284310920677179)
XLA Ops:
  0.6 1.8 %shard_map.185 = (f32[608,128]{1,0:T(8,128)S(1)}, f32[9,16,8,128]{3,2,1,0:T(8,128)S(1)}) custom-call(s32[4]{0:T(128)} %levels_hbm.1, f32[4,16,8,128]{3,2,1,0:T(8,128)} %u_hbm.1, f32[4,16,8,128]{3,2,1,0:T(8,128)} %v_hbm.1, f32[4,16,8,128]{3,2,1,0:T(8,128)} %rho_hbm.1, s32[8,128]{1,0:T(8,128)} %mask_ref.1, s32[8,128]{1,0:T(8,128)} %start_hbm.1), custom_call_target="tpu_custom_call" | custom-call | tf_op jit(solution)/shard_map/pallas_call | solution.py:585
  2.4 0.0 copy-start.3
  2.5 0.0 copy-start.8
  2.5 0.0 copy-start.11
  2.5 0.0 copy-start.4
  2.5 0.0 copy-start.5
  2.5 0.0 copy-start.6
  2.5 0.0 copy-start.7
  2.5 0.0 copy-start.10
  2.5 15.5 %all_to_all.15 = f32[32,1,2432]{2,1,0:T(1,128)S(1)} all-to-all(f32[32,1,2432]{2,1,0:T(1,128)S(1)} %bitcast.8), channel_id=1, replica_groups={{0,1,8,9,16,17,24,25,32,33,40,41,48,49,56,57,64,65,72,73,80,81,88,89,96..., dimensions={0} | all-to-all | bytes 622592 | tf_op jit(solution)/shard_map/all_to_all | solution.py:554
  18.1 0.0 copy-done.3
  18.1 0.0 copy-done.8
  18.1 0.0 copy-done.11
  18.1 0.0 copy-start
  18.1 0.0 copy-start.1
  18.1 0.4 shard_map.186
  18.5 0.0 copy-start.2
  18.5 0.0 copy-start.9
  18.5 29.5 %all_to_all.16.runs_ref = f32[8,24,128]{2,1,0:T(8,128)S(1)} all-to-all(f32[8,24,128]{2,1,0:T(8,128)S(1)} %shard_map.186), channel_id=1, replica_groups={{1,2,129,130,257,258,385,386},{3,4,131,132,259,260,387,388},{5,6,133,13..., dimensions={0} | all-to-all | bytes 196608 | tf_op jit(solution)/shard_map/all_to_all | solution.py:554
  48.0 0.0 copy-done.4
  48.0 0.0 copy-done.5
  48.0 0.0 copy-done.6
  48.0 0.0 copy-done.7
  48.1 0.0 copy-done.10
  48.1 0.0 copy-done
  48.1 0.0 copy-done.1
  48.1 0.0 copy-done.2
  48.1 0.0 copy-done.9
  48.1 1.7 %shard_map.187 = f32[608,128]{1,0:T(8,128)S(1)} custom-call(f32[608,128]{1,0:T(8,128)S(1)} %bitcast.5, f32[8,24,128]{2,1,0:T(8,128)S(1)} %all_to_all.16.runs_ref, f32[4,16,32]{2,1,0:T(8,128)S(1)} %copy-done.10, f32[4,16,256]{2,1,0:T(8,128)S(1)} %copy-done.7, f32[128,128]{1,0:T(8,128)S(1)} %copy-done.6, f32[2,128,16]{2,1,0:T(8,128)S(1)} %copy-done.2, ...), custom_call_target="tpu_custom_call" | custom-call | tf_op jit(solution)/shard_map/pallas_call | solution.py:616
  49.8 0.0 copy-start.12
  49.8 12.9 %all_to_all.17 = f32[32,1,2432]{2,1,0:T(1,128)S(1)} all-to-all(f32[32,1,2432]{2,1,0:T(1,128)S(1)} %bitcast.6), channel_id=1, replica_groups={{0,1,8,9,16,17,24,25,32,33,40,41,48,49,56,57,64,65,72,73,80,81,88,89,96..., dimensions={0} | all-to-all | bytes 622592 | tf_op jit(solution)/shard_map/all_to_all | solution.py:554
  62.7 0.0 copy-done.12
  62.7 2.0 %shard_map.188 = (f32[4,16,8,128]{3,2,1,0:T(8,128)}, f32[4,16,8,128]{3,2,1,0:T(8,128)}) custom-call(f32[9,16,8,128]{3,2,1,0:T(8,128)S(1)} %get-tuple-element.4.kept_ref, s32[8,128]{1,0:T(8,128)S(1)} %copy-done.12, f32[608,128]{1,0:T(8,128)S(1)} %bitcast.7), custom_call_target="tpu_custom_call" | custom-call | tf_op jit(solution)/shard_map/pallas_call | solution.py:620
Async XLA Ops:
  2.4 15.6 %copy-start.3 = (f32[256,128]{1,0:T(8,128)S(1)}, f32[256,128]{1,0:T(8,128)}, u32[]{:S(2)}) copy-start(f32[256,128]{1,0:T(8,128)} %constant.26.clone.edge_sum_ref) | copy-start | bytes 393220
  2.5 15.6 %copy-start.8 = (f32[4,16,256]{2,1,0:T(8,128)S(1)}, f32[4,16,256]{2,1,0:T(8,128)}, u32[]{:S(2)}) copy-start(f32[4,16,256]{2,1,0:T(8,128)} %constant.24.clone.send_ref) | copy-start | bytes 196612
  2.5 15.6 %copy-start.11 = (f32[4,16,128]{2,1,0:T(8,128)S(1)}, f32[4,16,128]{2,1,0:T(8,128)}, u32[]{:S(2)}) copy-start(f32[4,16,128]{2,1,0:T(8,128)} %constant.25.clone.send_ninth_ref) | copy-start | bytes 98308
  2.5 45.6 %copy-start.4 = (f32[128,16]{1,0:T(8,128)S(1)}, f32[128,16]{1,0:T(8,128)}, u32[]{:S(2)}) copy-start(f32[128,16]{1,0:T(8,128)} %constant.33.clone.inject_ninth_ref) | copy-start | bytes 24580
  2.5 45.5 %copy-start.5 = (f32[128,128]{1,0:T(8,128)S(1)}, f32[128,128]{1,0:T(8,128)}, u32[]{:S(2)}) copy-start(f32[128,128]{1,0:T(8,128)} %constant.32.clone.spread_ninth_ref) | copy-start | bytes 196612
  2.5 45.5 %copy-start.6 = (f32[128,128]{1,0:T(8,128)S(1)}, f32[128,128]{1,0:T(8,128)}, u32[]{:S(2)}) copy-start(f32[128,128]{1,0:T(8,128)} %constant.29.clone.spread_ref) | copy-start | bytes 196612
  2.5 45.5 %copy-start.7 = (f32[4,16,256]{2,1,0:T(8,128)S(1)}, f32[4,16,256]{2,1,0:T(8,128)}, u32[]{:S(2)}) copy-start(f32[4,16,256]{2,1,0:T(8,128)} %constant.28.clone.local_ref) | copy-start | bytes 196612
  2.5 45.5 %copy-start.10 = (f32[4,16,32]{2,1,0:T(8,128)S(1)}, f32[4,16,32]{2,1,0:T(8,128)}, u32[]{:S(2)}) copy-start(f32[4,16,32]{2,1,0:T(8,128)} %constant.27.clone.gather_ref) | copy-start | bytes 24580
  18.1 30.0 %copy-start = (f32[384,256]{1,0:T(8,128)S(1)}, f32[384,256]{1,0:T(8,128)}, u32[]{:S(2)}) copy-start(f32[384,256]{1,0:T(8,128)} %constant.35.clone.edge_out_ref) | copy-start | bytes 1179652
  18.1 30.0 %copy-start.1 = (f32[4,128,128]{2,1,0:T(8,128)S(1)}, f32[4,128,128]{2,1,0:T(8,128)}, u32[]{:S(2)}) copy-start(f32[4,128,128]{2,1,0:T(8,128)} %constant.34.clone.edge_gather_ref) | copy-start | bytes 786436
  18.5 29.6 %copy-start.2 = (f32[2,128,16]{2,1,0:T(8,128)S(1)}, f32[2,128,16]{2,1,0:T(8,128)}, u32[]{:S(2)}) copy-start(f32[2,128,16]{2,1,0:T(8,128)} %constant.30.clone.inject_ref) | copy-start | bytes 49156
  18.5 29.6 %copy-start.9 = (f32[4,16,128]{2,1,0:T(8,128)S(1)}, f32[4,16,128]{2,1,0:T(8,128)}, u32[]{:S(2)}) copy-start(f32[4,16,128]{2,1,0:T(8,128)} %constant.31.clone.local_ninth_ref) | copy-start | bytes 98308
  49.8 12.9 %copy-start.12 = (s32[8,128]{1,0:T(8,128)S(1)}, s32[8,128]{1,0:T(8,128)}, u32[]{:S(2)}) copy-start(s32[8,128]{1,0:T(8,128)} %mask_ref.1) | copy-start | bytes 12292

commit v6 on v5

--- a/solution.py
+++ b/solution.py
@@ -3,6 +3,7 @@
 
 import jax
 import jax.numpy as jnp
+import ml_dtypes
 import numpy as np
 from jax import lax
 from jax.experimental import pallas as pl
@@ -120,6 +121,29 @@
     return denom, np.stack(rows)
 
 
+def thirds(table):
+    rest = table.astype(np.float32)
+    out = []
+    for _ in range(3):
+        part = rest.astype(ml_dtypes.bfloat16)
+        out.append(part)
+        rest = rest - part.astype(np.float32)
+    return out
+
+
+def along_rows(table):
+    high, middle, low = thirds(table)
+    first = np.concatenate([np.concatenate([high, high], axis=-1), np.concatenate([middle, middle], axis=-1)], axis=-2)
+    return first, np.concatenate([high, low], axis=-1)
+
+
+def along_depth(table, height):
+    high, middle, low = thirds(table)
+    parts = np.concatenate([high, high, middle, middle, high, low], axis=-1)
+    pad = [(0, 0)] * (parts.ndim - 1) + [(0, height - parts.shape[-1])]
+    return np.pad(parts, pad)
+
+
 @functools.lru_cache(maxsize=None)
 def plan():
     gain = filter_design()[3]
@@ -153,7 +177,7 @@
     gather = np.zeros((RUNS, 16, RUNS * 8))
     send_ninth = np.zeros((RUNS, 16, own))
     local_ninth = np.zeros((RUNS, 16, own))
-    edge_gather = np.zeros((RUNS, LANES, LANES))
+    edge_gather = np.zeros((RUNS, QUARTER, LANES))
     for z in range(RUNS):
         after = suffix[RUNS - 1 - z]
         right = run_right + run_step @ after @ run_left
@@ -197,24 +221,33 @@
     edge_sum[:, 2 * QUARTER : 2 * QUARTER + 8] = run_summary.T / scale
     order = [(j // 8) * 8 + (8 - j % 8) % 8 for j in range(GROUP)]
     places = [order[j] * HOURS + hour for j in range(GROUP) for hour in range(HOURS)]
-    edge_out = np.zeros((SPAN + LANES, SPAN))
-    edge_out[:SPAN, places] = response.T / scale
-    edge_out[SPAN : SPAN + 8, places] = injected.T
+    edge_response = np.zeros((SPAN, SPAN))
+    edge_response[:, places] = response.T / scale
+    edge_inject = np.zeros((8, SPAN))
+    edge_inject[:, places] = injected.T
+    spread_first, spread_second = along_rows(spread)
+    local_tiles = [along_rows(local[:, :, tile * own : (tile + 1) * own]) for tile in range(2)]
+    ninth_first, ninth_second = along_rows(spread[swapped][:, swapped])
+    local_ninth_first, local_ninth_second = along_rows(local_ninth)
     tables = dict(
-        send=send,
-        local=local,
-        gather=gather,
-        spread=spread,
-        inject=inject,
-        send_ninth=send_ninth,
-        local_ninth=local_ninth,
-        spread_ninth=spread[swapped][:, swapped],
-        inject_ninth=inject[0][swapped],
-        edge_sum=edge_sum,
-        edge_gather=edge_gather,
-        edge_out=edge_out,
-    )
-    tables = {name: table.astype(np.float32) for name, table in tables.items()}
+        send=send.astype(np.float32),
+        send_ninth=send_ninth.astype(np.float32),
+        edge_sum=edge_sum.astype(np.float32),
+        gather=along_depth(gather, 256),
+        local_first=np.stack([tile[0] for tile in local_tiles], axis=1),
+        local_second=np.stack([tile[1] for tile in local_tiles], axis=1),
+        spread_first=spread_first,
+        spread_second=spread_second,
+        inject=along_depth(np.concatenate([inject[0], inject[1]]), LANES),
+        local_ninth_first=local_ninth_first,
+        local_ninth_second=local_ninth_second,
+        ninth_first=ninth_first,
+        ninth_second=ninth_second,
+        inject_ninth=along_depth(inject[0][swapped], LANES),
+        edge_gather=along_depth(np.swapaxes(edge_gather, 1, 2), 256).swapaxes(1, 2),
+        edge_response=np.stack(thirds(edge_response)),
+        edge_inject=along_depth(edge_inject.T, LANES).T,
+    )
     return dict(tables, denom=denom, scale=scale, summary=summary / scale)
 
 
@@ -275,6 +308,17 @@
         first, second = halves[i], halves[i + 1]
         out[i] = jnp.where(even, first, turn(second, QUARTER))
         out[i + 1] = jnp.where(even, turn(first, -QUARTER), second)
+    return out
+
+
+def shared(parts, lane, sign):
+    block = lane // QUARTER
+    out = []
+    for i in range(4):
+        total = parts[i]
+        for b in range(1, 4):
+            total = jnp.where(block == b, parts[(i + sign * b) % 4], total)
+        out.append(total)
     return out
 
 
@@ -310,8 +354,8 @@
     live = live_hours(mask_ref[...], start_ref[...], scale)
     depth = depths(levels_ref)
     lane = lanes_of()
-    west = jnp.zeros((ROWS, LANES), jnp.float32)
-    east = west
+    zeros = jnp.zeros((ROWS, LANES), jnp.float32)
+    west, east = zeros, zeros
     for which, ref in enumerate((u_ref, rho_ref, v_ref)):
         copies[3 + which].wait()
         sums = [[None] * 8 for _ in range(3)]
@@ -333,24 +377,36 @@
         for level in range(3):
             for k in range(8):
                 sums_ref[(which * 3 + level) * 8 + k] = sums[level][k]
-    edges = []
+        if which == 1:
+            edges = finished_edges(west, east, lane)
+            for index, quarter in enumerate(QUARTERS):
+                out_ref[pl.ds(index * SLOT + 18, ROWS, stride=4 * SLOT), :] = edges.get(quarter, zeros)
+            lay_out(sums_ref, list(range(4)), out_ref, 0, lane)
+    lay_out(sums_ref, list(range(4, 8)), out_ref, 8, lane)
+    for v in range(2):
+        lay_out_rows([sums_ref[64 + 4 * v + a] for a in range(4)], out_ref, 16 + v, lane)
+
+
+def finished_edges(west, east, lane):
+    block = lane // HOURS
+    out = []
     for ends in (west, turn(east, 1)):
         three = -((turn(ends, -HOURS) + turn(ends, -2 * HOURS)) + turn(ends, -3 * HOURS))
-        block = lane // HOURS
-        edges.append(jnp.where((block == 5) | (block == 1), three, ends))
-    spare = {0: edges[0], 3: edges[1]}
-    for v in range(2):
-        for k in range(8):
-            parts = transposed([sums_ref[(4 * v + a) * 8 + k] for a in range(4)], lane)
-            for index, quarter in enumerate(QUARTERS):
-                out_ref[pl.ds(index * SLOT + v * 8 + k, ROWS, stride=4 * SLOT), :] = parts[quarter]
-        parts = transposed([sums_ref[64 + 4 * v + a] for a in range(4)], lane)
-        for index, quarter in enumerate(QUARTERS):
-            out_ref[pl.ds(index * SLOT + 16 + v, ROWS, stride=4 * SLOT), :] = parts[quarter]
+        out.append(jnp.where((block == 5) | (block == 1), three, ends))
+    return {0: out[0], 3: out[1]}
+
+
+def lay_out(sums_ref, series, out_ref, first, lane):
+    for k in range(8):
+        parts = shared([sums_ref[s * 8 + k] for s in series], lane, 1)
+        for index in range(4):
+            out_ref[pl.ds(index * SLOT + first + k, ROWS, stride=4 * SLOT), :] = parts[index]
+
+
+def lay_out_rows(values, out_ref, row, lane):
+    parts = transposed(values, lane)
     for index, quarter in enumerate(QUARTERS):
-        out_ref[pl.ds(index * SLOT + 18, ROWS, stride=4 * SLOT), :] = spare.get(
-            quarter, jnp.zeros((ROWS, LANES), jnp.float32)
-        )
+        out_ref[pl.ds(index * SLOT + row, ROWS, stride=4 * SLOT), :] = parts[quarter]
 
 
 def blocks_of(in_ref, tile):
@@ -405,7 +461,38 @@
                 out_ref[2 * other + slot_side, pl.ds(v * 8, 8), :] = jnp.where(side == slot_side, mine, across)
 
 
-def edge_flux(in_ref, runs_ref, run, tile, side, edge_gather, edge_out):
+def split(value):
+    high = value.astype(jnp.bfloat16)
+    rest = value - high.astype(jnp.float32)
+    middle = rest.astype(jnp.bfloat16)
+    return high, middle, (rest - middle.astype(jnp.float32)).astype(jnp.bfloat16)
+
+
+def six_below(value, height):
+    high, middle, low = split(value)
+    parts = [high, middle, high, middle, low, high]
+    rest = height - 6 * value.shape[0]
+    if rest:
+        parts.append(jnp.zeros((rest, value.shape[1]), jnp.bfloat16))
+    return jnp.concatenate(parts, axis=0)
+
+
+def product(lhs, rhs):
+    return jnp.dot(lhs, rhs, preferred_element_type=jnp.float32)
+
+
+def mapped(first, second, value):
+    high, middle, low = split(value)
+    upper = product(first, jnp.concatenate([high, middle], axis=0))
+    lower = product(second, jnp.concatenate([low, high], axis=0))
+    rows = 2 * GROUP * 8
+    half = GROUP * 8
+    spread = (upper[:half] + upper[half:rows]) + lower[:half]
+    local = (upper[rows : rows + 16] + upper[rows + 16 :]) + lower[half:]
+    return spread, local
+
+
+def edge_flux(in_ref, runs_ref, run, tile, side, edge_gather, response_ref, edge_inject):
     lane = lanes_of()
     own = [runs_ref[2 * other + side, pl.ds(16, 8), :] for other in range(RUNS)]
     across = [runs_ref[2 * other + 1 - side, pl.ds(16, 8), :] for other in range(RUNS)]
@@ -415,11 +502,20 @@
         for other in range(RUNS):
             total = jnp.where(lane // 8 == other, turn(parts[other], other * 8 - 2 * QUARTER), total)
         sums.append(total)
-    states = dot(jnp.concatenate(sums, axis=0), edge_gather)
+    high, middle, low = (part.astype(jnp.float32) for part in split(jnp.concatenate(sums, axis=0)))
+    first = (high + turn(middle, 32)) + (turn(high, 64) + turn(middle, 96))
+    sums = jnp.concatenate([first, low + turn(high, 32)], axis=1)
+    states = product(sums.astype(jnp.bfloat16), edge_gather)
+    high, middle, low = (part.astype(jnp.float32) for part in split(states))
+    states = (high + turn(middle, 8)) + (turn(high, 16) + turn(middle, 24)) + (turn(low, 32) + turn(high, 40))
     near = edge_hours(in_ref, 1 - tile)
     far = jnp.concatenate([runs_ref[2 * run + 1 - side, pl.ds(v * 8, 8), :] for v in range(2)], axis=1)
-    hours = jnp.concatenate([near, far], axis=0)
-    banded = dot(jnp.concatenate([hours, states], axis=1), edge_out)
+    high, middle, low = split(jnp.concatenate([near, far], axis=0))
+    one = product(jnp.concatenate([high, middle, low], axis=0), response_ref[0])
+    two = product(jnp.concatenate([high, middle], axis=0), response_ref[1])
+    three = product(high, response_ref[2])
+    banded = (one[0:16] + one[16:32]) + (one[32:48] + two[0:16]) + (two[16:32] + three)
+    banded = banded + product(states.astype(jnp.bfloat16), edge_inject)
     row = lax.broadcasted_iota(jnp.int32, (ROWS, SPAN), 0)
     products = [part * pltpu.roll(part, 4, 0) for part in (banded[0:8], banded[8:16])]
     flux = jnp.where(row < 4, products[0], products[1])
@@ -432,43 +528,59 @@
     in_ref,
     runs_ref,
     gather_ref,
-    local_ref,
-    spread_ref,
+    local_first_ref,
+    local_second_ref,
+    spread_first_ref,
+    spread_second_ref,
     inject_ref,
-    local_ninth_ref,
-    spread_ninth_ref,
+    local_ninth_first_ref,
+    local_ninth_second_ref,
+    ninth_first_ref,
+    ninth_second_ref,
     inject_ninth_ref,
     edge_gather_ref,
-    edge_out_ref,
+    edge_response_ref,
+    edge_inject_ref,
     out_ref,
 ):
     run, tile, side = place()
-    flux = edge_flux(in_ref, runs_ref, run, tile, side, edge_gather_ref[run], edge_out_ref[...])
+    flux = edge_flux(in_ref, runs_ref, run, tile, side, edge_gather_ref[run], edge_response_ref, edge_inject_ref[...])
     runs = [
         jnp.concatenate([runs_ref[2 * other + side, pl.ds(v * 8, 8), :] for other in range(RUNS)], axis=0)
         for v in range(3)
     ]
-    gather = dot(gather_ref[run], jnp.concatenate(runs, axis=1))
-    tiles = [blocks_of(in_ref, 0), blocks_of(in_ref, 1)]
-    states = gather[:, : 2 * LANES] + dot(local_ref[run], jnp.concatenate(tiles, axis=0))
+    states = product(gather_ref[run], six_below(jnp.concatenate(runs, axis=1), 256))
+    bases, locals_ = [], []
     for which in range(2):
-        borders = dot(spread_ref[...], tiles[which]) + dot(inject_ref[which], states)
+        base, local = mapped(
+            jnp.concatenate([spread_first_ref[...], local_first_ref[run, which]], axis=0),
+            jnp.concatenate([spread_second_ref[...], local_second_ref[run, which]], axis=0),
+            blocks_of(in_ref, which),
+        )
+        bases.append(base)
+        locals_.append(local)
+    ninth, local = mapped(
+        jnp.concatenate([ninth_first_ref[...], local_ninth_first_ref[run]], axis=0),
+        jnp.concatenate([ninth_second_ref[...], local_ninth_second_ref[run]], axis=0),
+        ninth_of(in_ref),
+    )
+    states = six_below(states + jnp.concatenate([locals_[0] + locals_[1], local], axis=1), LANES)
+    added = product(inject_ref[...], states[:, : 2 * LANES])
+    ninth = ninth + product(inject_ninth_ref[...], states[:, 2 * LANES :])
+    for which in range(2):
         for j in range(GROUP):
+            row = which * GROUP * 8 + j * 8
+            borders = bases[which][j * 8 : j * 8 + 8] + added[row : row + 8]
             for v in range(2):
-                out_ref[pl.ds((2 * j + which) * SLOT + v * 8, 8), :] = borders[
-                    j * 8 : j * 8 + 8, v * LANES : (v + 1) * LANES
-                ]
+                out_ref[pl.ds((2 * j + which) * SLOT + v * 8, 8), :] = borders[:, v * LANES : (v + 1) * LANES]
         out_ref[pl.ds(which * SLOT + 18, GROUP, stride=2 * SLOT), :] = flux
-    ninth = ninth_of(in_ref)
-    states = gather[:, 2 * LANES :] + dot(local_ninth_ref[run], ninth)
-    borders = dot(spread_ninth_ref[...], ninth) + dot(inject_ninth_ref[...], states)
     block = lanes_of((GROUP, LANES)) // QUARTER
     for which in range(2):
         for half in range(2):
             total = jnp.zeros((GROUP, LANES), jnp.float32)
             for a in range(4):
                 row = (half * 4 + a) * GROUP
-                total = jnp.where(block == a, turn(borders[row : row + GROUP], QUARTER * (a - which)), total)
+                total = jnp.where(block == a, turn(ninth[row : row + GROUP], QUARTER * (a - which)), total)
             out_ref[pl.ds(which * SLOT + 16 + half, GROUP, stride=2 * SLOT), :] = total
 
 
@@ -494,10 +606,8 @@
     lane = lanes_of()
     for v in range(2):
         for k in range(8):
-            parts = [None] * 4
-            for index, quarter in enumerate(QUARTERS):
-                parts[quarter] = borders_ref[pl.ds(index * SLOT + v * 8 + k, ROWS, stride=4 * SLOT), :]
-            for a, part in enumerate(transposed(parts, lane)):
+            parts = [borders_ref[pl.ds(index * SLOT + v * 8 + k, ROWS, stride=4 * SLOT), :] for index in range(4)]
+            for a, part in enumerate(shared(parts, lane, -1)):
                 states_ref[(4 * v + a) * 8 + k] = part
         for index, quarter in enumerate(QUARTERS):
             parts[quarter] = borders_ref[pl.ds(index * SLOT + 16 + v, ROWS, stride=4 * SLOT), :]
@@ -509,18 +619,6 @@
         copies.append(pltpu.make_async_copy(source, target, sems.at[len(copies)]))
         copies[-1].start()
 
-    for which, target in ((1, press_ref), (0, east_ref), (2, north_ref)):
-        for level in range(3):
-            s = which * 3 + level
-            states = [states_ref[s * 8 + k] for k in range(8)]
-            samples = filter_steps(states[:4], [kept_ref[s, hour] for hour in range(HOURS)])
-            samples = filter_steps(states[4:], samples[::-1])[::-1]
-            for hour in range(HOURS):
-                target[level, hour] = samples[hour]
-        if which == 1:
-            for hour in range(HOURS):
-                press_ref[3, hour] = last_level([press_ref[level, hour] for level in range(3)])
-            send(press_ref, press_hbm)
     row = lax.broadcasted_iota(jnp.int32, (ROWS, LANES), 0)
     half = 0.5 * mask_ref[...].astype(jnp.float32)
     last = lane == LANES - 1
@@ -528,23 +626,35 @@
     halos = jnp.where(tile == 0, turn(halos, 64), halos)
     outside = ((column == 0) & (lane < 64)) | ((column == 2 * len(PAIRS) - 1) & (lane >= 64))
     halos = jnp.where(outside, 0.0, halos)
-    for hour in range(HOURS):
-        u_all = [east_ref[level, hour] for level in range(3)]
-        v_all = [north_ref[level, hour] for level in range(3)]
-        p_all = [press_ref[level, hour] for level in range(4)]
-        for values in (u_all, v_all):
-            values.append(last_level(values))
-        for level in range(4):
-            fx = u_all[level] * p_all[level]
-            fy = v_all[level] * p_all[level]
+    for level in range(4):
+        if level < 3:
+            for which, target in ((1, press_ref), (0, east_ref), (2, north_ref)):
+                s = which * 3 + level
+                states = [states_ref[s * 8 + k] for k in range(8)]
+                samples = filter_steps(states[:4], [kept_ref[s, hour] for hour in range(HOURS)])
+                samples = filter_steps(states[4:], samples[::-1])[::-1]
+                for hour in range(HOURS):
+                    target[level, hour] = samples[hour]
+        else:
+            for hour in range(HOURS):
+                press_ref[3, hour] = last_level([press_ref[lower, hour] for lower in range(3)])
+        send(press_ref.at[level], press_hbm.at[level])
+        for hour in range(HOURS):
+            press = press_ref[level, hour]
+            if level < 3:
+                u_here, v_here = east_ref[level, hour], north_ref[level, hour]
+            else:
+                u_here = last_level([east_ref[lower, hour] for lower in range(3)])
+                v_here = last_level([north_ref[lower, hour] for lower in range(3)])
+            fx = u_here * press
+            fy = v_here * press
             position = level * HOURS + hour
             next_x = jnp.where(last, turn(halos, LANES - 1 - 64 - position), turn(fx, -1))
             prev_x = jnp.where(lane == 0, turn(halos, -position), turn(fx, 1))
             next_y = jnp.where(row == ROWS - 1, 0.0, pltpu.roll(fy, ROWS - 1, 0))
             prev_y = jnp.where(row == 0, 0.0, pltpu.roll(fy, 1, 0))
             flux_ref[level, hour] = half * ((next_x - prev_x) + (next_y - prev_y))
-        if hour % 4 == 3:
-            send(flux_ref.at[:, pl.ds(hour - 3, 4)], flux_hbm.at[:, pl.ds(hour - 3, 4)])
+        send(flux_ref.at[level], flux_hbm.at[level])
     for copy in copies:
         copy.wait()
 
@@ -604,14 +714,19 @@
     totals = swap(totals, across, FAR)
     names = (
         "gather",
-        "local",
-        "spread",
+        "local_first",
+        "local_second",
+        "spread_first",
+        "spread_second",
         "inject",
-        "local_ninth",
-        "spread_ninth",
+        "local_ninth_first",
+        "local_ninth_second",
+        "ninth_first",
+        "ninth_second",
         "inject_ninth",
         "edge_gather",
-        "edge_out",
+        "edge_response",
+        "edge_inject",
     )
     (borders,) = call(border_kernel, [flat], [VMEM] * (2 + len(names)))(
         blocks, totals, *[tables[name] for name in names]
@@ -627,7 +742,7 @@
             pltpu.VMEM(part, jnp.float32),
             pltpu.VMEM(part, jnp.float32),
             state_scratch,
-            pltpu.SemaphoreType.DMA((5,)),
+            pltpu.SemaphoreType.DMA((8,)),
         ],
         out_spec=HBM,
     )(kept, land_mask, borders)

time: 65.4 us -> 64.2 us (0.982)
  Pallas kernels: 5.84 us -> 4.52 us
    pallas_call x1, Pallas kernels: 1.66 us -> 0.87 us  [on_device(): call(border_kernel, [flat], [VMEM] * (2 + len(names)))]
where the time goes in v6:
time: 64.2 us; the launch traced here: 63.5 us
  blocking collectives  58 us (90%)
  Pallas kernels  4.52 us (7%)
  between operations  0.89 us (1%)
    all_to_all x3, blocking collectives, swap(): lax.all_to_all(array, ('tm', 'col'), 0, 0, tiled=True, axis_index_groups=...  58 us
    pallas_call x1, Pallas kernels, on_device(): call(summary_kernel, [flat, (SERIES, HOURS, ROWS, LANES)], [HBM] * 6, [pl...  1.89 us
    pallas_call x1, Pallas kernels, on_device(): call(band_kernel, [whole, whole], [VMEM] * 3, [pltpu.VMEM(whole, jnp.floa...  1.37 us

profile of v6, /device:TPU:6, one launch (start us, length us, event | category | flops | bytes accessed | tf_op | source)
XLA Modules:
  0.0 63.5 jit_solution(16305199627844507176)
XLA Ops:
  0.6 0.0 copy-start.12
  0.6 0.0 copy-start.16
  0.7 0.0 copy-start.10
  0.7 0.0 copy-start.11
  0.7 0.0 copy-start.13
  0.7 0.0 copy-start.14
  0.7 0.0 copy-start.15
  0.7 1.9 %shard_map.230 = (f32[608,128]{1,0:T(8,128)S(1)}, f32[9,16,8,128]{3,2,1,0:T(8,128)S(1)}) custom-call(s32[4]{0:T(128)} %levels_hbm.1, f32[4,16,8,128]{3,2,1,0:T(8,128)} %u_hbm.1, f32[4,16,8,128]{3,2,1,0:T(8,128)} %v_hbm.1, f32[4,16,8,128]{3,2,1,0:T(8,128)} %rho_hbm.1, s32[8,128]{1,0:T(8,128)} %mask_ref.1, s32[8,128]{1,0:T(8,128)} %start_hbm.1), custom_call_target="tpu_custom_call" | custom-call | tf_op jit(solution)/shard_map/pallas_call | solution.py:695
  2.6 0.0 copy-start.2
  2.6 0.0 copy-start.4
  2.6 0.0 copy-start.5
  2.7 0.0 copy-start.6
  2.7 0.0 copy-start.7
  2.7 0.0 copy-start.8
  2.7 0.0 copy-start.9
  2.7 15.5 %all_to_all.15 = f32[32,1,2432]{2,1,0:T(1,128)S(1)} all-to-all(f32[32,1,2432]{2,1,0:T(1,128)S(1)} %bitcast.8), channel_id=1, replica_groups={{0,1,8,9,16,17,24,25,32,33,40,41,48,49,56,57,64,65,72,73,80,81,88,89,96..., dimensions={0} | all-to-all | bytes 622592 | tf_op jit(solution)/shard_map/all_to_all | solution.py:664
  18.2 0.0 copy-done.12
  18.2 0.0 copy-done.16
  18.2 0.0 copy-done.2
  18.2 0.0 copy-start
  18.2 0.0 copy-start.1
  18.3 0.4 shard_map.231
  18.6 0.0 copy-start.3
  18.7 29.5 %all_to_all.16.runs_ref = f32[8,24,128]{2,1,0:T(8,128)S(1)} all-to-all(f32[8,24,128]{2,1,0:T(8,128)S(1)} %shard_map.231), channel_id=1, replica_groups={{1,2,129,130,257,258,385,386},{3,4,131,132,259,260,387,388},{5,6,133,13..., dimensions={0} | all-to-all | bytes 196608 | tf_op jit(solution)/shard_map/all_to_all | solution.py:664
  48.2 0.0 copy-done.10
  48.2 0.0 copy-done.11
  48.2 0.0 copy-done.13
  48.2 0.0 copy-done.14
  48.2 0.0 copy-done.15
  48.2 0.0 copy-done.4
  48.2 0.0 copy-done.5
  48.2 0.0 copy-done.6
  48.2 0.0 copy-done.7
  48.2 0.0 copy-done.8
  48.3 0.0 copy-done.9
  48.3 0.0 copy-done
  48.3 0.0 copy-done.1
  48.3 0.0 copy-done.3
  48.3 0.9 %shard_map.232 = f32[608,128]{1,0:T(8,128)S(1)} custom-call(f32[608,128]{1,0:T(8,128)S(1)} %bitcast.5, f32[8,24,128]{2,1,0:T(8,128)S(1)} %all_to_all.16.runs_ref, bf16[4,16,256]{2,1,0:T(8,128)(2,1)S(1)} %copy-done.15, bf16[4,2,32,256]{3,2,1,0:T(8,128)(2,1)S(1)} %copy-done.5, bf16[4,2,16,256]{3,2,1,0:T(8,128)(2,1)S(1)} %copy-done.11, ...), custom_call_target="tpu_custom_call" | custom-call | tf_op jit(solution)/shard_map/pallas_call | solution.py:731
  49.2 0.0 copy-start.17
  49.2 12.9 %all_to_all.17 = f32[32,1,2432]{2,1,0:T(1,128)S(1)} all-to-all(f32[32,1,2432]{2,1,0:T(1,128)S(1)} %bitcast.6), channel_id=1, replica_groups={{0,1,8,9,16,17,24,25,32,33,40,41,48,49,56,57,64,65,72,73,80,81,88,89,96..., dimensions={0} | all-to-all | bytes 622592 | tf_op jit(solution)/shard_map/all_to_all | solution.py:664
  62.1 0.0 copy-done.17
  62.1 1.4 %shard_map.233 = (f32[4,16,8,128]{3,2,1,0:T(8,128)}, f32[4,16,8,128]{3,2,1,0:T(8,128)}) custom-call(f32[9,16,8,128]{3,2,1,0:T(8,128)S(1)} %get-tuple-element.4.kept_ref, s32[8,128]{1,0:T(8,128)S(1)} %copy-done.17, f32[608,128]{1,0:T(8,128)S(1)} %bitcast.7), custom_call_target="tpu_custom_call" | custom-call | tf_op jit(solution)/shard_map/pallas_call | solution.py:735
Async XLA Ops:
  0.6 17.6 %copy-start.12 = (f32[4,16,256]{2,1,0:T(8,128)S(1)}, f32[4,16,256]{2,1,0:T(8,128)}, u32[]{:S(2)}) copy-start(f32[4,16,256]{2,1,0:T(8,128)} %constant.34.clone.send_ref) | copy-start | bytes 196612
  0.6 17.6 %copy-start.16 = (f32[4,16,128]{2,1,0:T(8,128)S(1)}, f32[4,16,128]{2,1,0:T(8,128)}, u32[]{:S(2)}) copy-start(f32[4,16,128]{2,1,0:T(8,128)} %constant.35.clone.send_ninth_ref) | copy-start | bytes 98308
  0.7 47.5 %copy-start.10 = (bf16[128,256]{1,0:T(8,128)(2,1)S(1)}, bf16[128,256]{1,0:T(8,128)(2,1)}, u32[]{:S(2)}) copy-start(bf16[128,256]{1,0:T(8,128)(2,1)} %constant.41.clone.spread_second_ref) | copy-start | bytes 196612
  0.7 47.5 %copy-start.11 = (bf16[4,2,16,256]{3,2,1,0:T(8,128)(2,1)S(1)}, bf16[4,2,16,256]{3,2,1,0:T(8,128)(2,1)}, u32[]{:S(2)}) copy-start(bf16[4,2,16,256]{3,2,1,0:T(8,128)(2,1)} %constant.39.clone.local_second_ref) | copy-start | bytes 196612
  0.7 47.5 %copy-start.13 = (bf16[128,128]{1,0:T(8,128)(2,1)S(1)}, bf16[128,128]{1,0:T(8,128)(2,1)}, u32[]{:S(2)}) copy-start(bf16[128,128]{1,0:T(8,128)(2,1)} %constant.47.clone.inject_ninth_ref) | copy-start | bytes 98308
  0.7 47.5 %copy-start.14 = (bf16[4,16,256]{2,1,0:T(8,128)(2,1)S(1)}, bf16[4,16,256]{2,1,0:T(8,128)(2,1)}, u32[]{:S(2)}) copy-start(bf16[4,16,256]{2,1,0:T(8,128)(2,1)} %constant.44.clone.local_ninth_second_ref) | copy-start | bytes 98308
  0.7 47.5 %copy-start.15 = (bf16[4,16,256]{2,1,0:T(8,128)(2,1)S(1)}, bf16[4,16,256]{2,1,0:T(8,128)(2,1)}, u32[]{:S(2)}) copy-start(bf16[4,16,256]{2,1,0:T(8,128)(2,1)} %constant.37.clone.gather_ref) | copy-start | bytes 98308
  2.6 15.6 %copy-start.2 = (f32[256,128]{1,0:T(8,128)S(1)}, f32[256,128]{1,0:T(8,128)}, u32[]{:S(2)}) copy-start(f32[256,128]{1,0:T(8,128)} %constant.36.clone.edge_sum_ref) | copy-start | bytes 393220
  2.6 45.6 %copy-start.4 = (bf16[256,256]{1,0:T(8,128)(2,1)S(1)}, bf16[256,256]{1,0:T(8,128)(2,1)}, u32[]{:S(2)}) copy-start(bf16[256,256]{1,0:T(8,128)(2,1)} %constant.40.clone.spread_first_ref) | copy-start | bytes 393220
  2.6 45.6 %copy-start.5 = (bf16[4,2,32,256]{3,2,1,0:T(8,128)(2,1)S(1)}, bf16[4,2,32,256]{3,2,1,0:T(8,128)(2,1)}, u32[]{:S(2)}) copy-start(bf16[4,2,32,256]{3,2,1,0:T(8,128)(2,1)} %constant.38.clone.local_first_ref) | copy-start | bytes 393220
  2.7 45.6 %copy-start.6 = (bf16[128,256]{1,0:T(8,128)(2,1)S(1)}, bf16[128,256]{1,0:T(8,128)(2,1)}, u32[]{:S(2)}) copy-start(bf16[128,256]{1,0:T(8,128)(2,1)} %constant.50.clone.edge_inject_ref) | copy-start | bytes 196612
  2.7 45.6 %copy-start.7 = (bf16[128,256]{1,0:T(8,128)(2,1)S(1)}, bf16[128,256]{1,0:T(8,128)(2,1)}, u32[]{:S(2)}) copy-start(bf16[128,256]{1,0:T(8,128)(2,1)} %constant.46.clone.ninth_second_ref) | copy-start | bytes 196612
  2.7 45.6 %copy-start.8 = (bf16[4,32,256]{2,1,0:T(8,128)(2,1)S(1)}, bf16[4,32,256]{2,1,0:T(8,128)(2,1)}, u32[]{:S(2)}) copy-start(bf16[4,32,256]{2,1,0:T(8,128)(2,1)} %constant.43.clone.local_ninth_first_ref) | copy-start | bytes 196612
  2.7 45.6 %copy-start.9 = (bf16[256,128]{1,0:T(8,128)(2,1)S(1)}, bf16[256,128]{1,0:T(8,128)(2,1)}, u32[]{:S(2)}) copy-start(bf16[256,128]{1,0:T(8,128)(2,1)} %constant.42.clone.inject_ref) | copy-start | bytes 196612
  18.2 30.0 %copy-start = (bf16[3,256,256]{2,1,0:T(8,128)(2,1)S(1)}, bf16[3,256,256]{2,1,0:T(8,128)(2,1)}, u32[]{:S(2)}) copy-start(bf16[3,256,256]{2,1,0:T(8,128)(2,1)} %constant.49.clone.edge_response_ref) | copy-start | bytes 1179652
  18.2 30.0 %copy-start.1 = (bf16[4,256,128]{2,1,0:T(8,128)(2,1)S(1)}, bf16[4,256,128]{2,1,0:T(8,128)(2,1)}, u32[]{:S(2)}) copy-start(bf16[4,256,128]{2,1,0:T(8,128)(2,1)} %constant.48.clone.edge_gather_ref) | copy-start | bytes 786436
  18.6 29.6 %copy-start.3 = (bf16[256,256]{1,0:T(8,128)(2,1)S(1)}, bf16[256,256]{1,0:T(8,128)(2,1)}, u32[]{:S(2)}) copy-start(bf16[256,256]{1,0:T(8,128)(2,1)} %constant.45.clone.ninth_first_ref) | copy-start | bytes 393220
  49.2 13.0 %copy-start.17 = (s32[8,128]{1,0:T(8,128)S(1)}, s32[8,128]{1,0:T(8,128)}, u32[]{:S(2)}) copy-start(s32[8,128]{1,0:T(8,128)} %mask_ref.1) | copy-start | bytes 12292

commit v7 on v6

--- a/solution.py
+++ b/solution.py
@@ -176,13 +176,14 @@
     local = np.zeros((RUNS, 16, 2 * own))
     gather = np.zeros((RUNS, 16, RUNS * 8))
     send_ninth = np.zeros((RUNS, 16, own))
+    gather_ninth = np.zeros((RUNS, 16, 4 * RUNS))
     local_ninth = np.zeros((RUNS, 16, own))
     edge_gather = np.zeros((RUNS, QUARTER, LANES))
     for z in range(RUNS):
         after = suffix[RUNS - 1 - z]
         right = run_right + run_step @ after @ run_left
-        send_ninth[z, 0:4] = run_left[:, swapped]
-        send_ninth[z, 8:12] = right[:, swapped]
+        send_ninth[z, 0:4] = run_left[[0, 2, 1, 3]][:, swapped]
+        send_ninth[z, 8:12] = right[[0, 2, 1, 3]][:, swapped]
         local_ninth[z, 8:12] = (after @ run_left)[:, swapped]
         for tile in range(2):
             columns = slice(tile * own, (tile + 1) * own)
@@ -199,6 +200,7 @@
                     gather[z, behind, here] = after @ run_step @ came
                 if other > z:
                     gather[z, behind, here] = power(run_step, other - z - 1)
+        gather_ninth[z] = gather[z].reshape(16, RUNS, 8)[:, :, :4].swapaxes(1, 2).reshape(16, 4 * RUNS)
         for other in range(RUNS):
             from_left = slice(other * 8, other * 8 + 4)
             from_right = slice(other * 8 + 4, other * 8 + 8)
@@ -217,8 +219,7 @@
     for tile in range(2):
         inject[tile, :, 4 * tile : 4 * tile + 4] = inner[:, own : own + 4]
         inject[tile, :, 8 + 4 * tile : 12 + 4 * tile] = inner[:, own + 4 :]
-    edge_sum = np.zeros((SPAN, LANES))
-    edge_sum[:, 2 * QUARTER : 2 * QUARTER + 8] = run_summary.T / scale
+    edge_sum = np.tile(run_summary.T / scale, (1, LANES // 8))
     order = [(j // 8) * 8 + (8 - j % 8) % 8 for j in range(GROUP)]
     places = [order[j] * HOURS + hour for j in range(GROUP) for hour in range(HOURS)]
     edge_response = np.zeros((SPAN, SPAN))
@@ -234,6 +235,7 @@
         send_ninth=send_ninth.astype(np.float32),
         edge_sum=edge_sum.astype(np.float32),
         gather=along_depth(gather, 256),
+        gather_ninth=along_depth(gather_ninth, LANES),
         local_first=np.stack([tile[0] for tile in local_tiles], axis=1),
         local_second=np.stack([tile[1] for tile in local_tiles], axis=1),
         spread_first=spread_first,
@@ -447,18 +449,31 @@
     near = edge_hours(in_ref, 1 - tile)
     far = edge_hours(in_ref, tile)
     sums = dot(jnp.concatenate([near, far], axis=0), edge_sum_ref[...])
-    first = lanes_of() < 2 * QUARTER
+    lane = lanes_of()
+    row = lax.broadcasted_iota(jnp.int32, (ROWS, LANES), 0)
+
+    def packed(value):
+        return jnp.where(lane < 64, value, turn(pltpu.roll(value, 6, 0), 64))
+
+    def in_row(value):
+        value = jnp.where(lane // 8 == 15 - row, value, 0.0)
+        for shift in (4, 2, 1):
+            value = value + pltpu.roll(value, shift, 0)
+        return value
+
+    left, right = packed(ninth[0:8]), packed(ninth[8:16])
+    near_row, far_row = in_row(sums[0:8]), in_row(sums[8:16])
     for other in range(RUNS):
-        for v in range(3):
-            lanes = slice(v * LANES, (v + 1) * LANES)
-            if v == 2:
-                mine = jnp.where(first, jnp.where(other > run, ninth[0:8], ninth[8:16]), sums[0:8])
-                across = sums[8:16]
-            else:
-                mine = jnp.where(other > run, totals[0:8, lanes], totals[8:16, lanes])
-                across = far[:, lanes]
-            for slot_side in range(2):
-                out_ref[2 * other + slot_side, pl.ds(v * 8, 8), :] = jnp.where(side == slot_side, mine, across)
+        later = other > run
+        rest = jnp.where(row == 2, near_row, jnp.where(later, left, right))
+        for slot_side in range(2):
+            base = (2 * other + slot_side) * SLOT
+            mine = side == slot_side
+            for v in range(2):
+                lanes = slice(v * LANES, (v + 1) * LANES)
+                main = jnp.where(later, totals[0:8, lanes], totals[8:16, lanes])
+                out_ref[pl.ds(base + v * 8, 8), :] = jnp.where(mine, main, far[:, lanes])
+            out_ref[pl.ds(base + 16, 3), :] = jnp.where(mine, rest, far_row)[0:3]
 
 
 def split(value):
@@ -494,13 +509,14 @@
 
 def edge_flux(in_ref, runs_ref, run, tile, side, edge_gather, response_ref, edge_inject):
     lane = lanes_of()
-    own = [runs_ref[2 * other + side, pl.ds(16, 8), :] for other in range(RUNS)]
-    across = [runs_ref[2 * other + 1 - side, pl.ds(16, 8), :] for other in range(RUNS)]
     sums = []
-    for parts in (own, across):
+    for which in (side, 1 - side):
+        rows = runs_ref[pl.ds(which * SLOT + 18, RUNS, stride=2 * SLOT), :]
         total = jnp.zeros((ROWS, LANES), jnp.float32)
         for other in range(RUNS):
-            total = jnp.where(lane // 8 == other, turn(parts[other], other * 8 - 2 * QUARTER), total)
+            value = jnp.broadcast_to(rows[other : other + 1], (ROWS, LANES))
+            value = pltpu.roll(value, 8 * other + 8, 1, stride=8, stride_axis=0)
+            total = jnp.where(lane // 8 == other, value, total)
         sums.append(total)
     high, middle, low = (part.astype(jnp.float32) for part in split(jnp.concatenate(sums, axis=0)))
     first = (high + turn(middle, 32)) + (turn(high, 64) + turn(middle, 96))
@@ -509,7 +525,10 @@
     high, middle, low = (part.astype(jnp.float32) for part in split(states))
     states = (high + turn(middle, 8)) + (turn(high, 16) + turn(middle, 24)) + (turn(low, 32) + turn(high, 40))
     near = edge_hours(in_ref, 1 - tile)
-    far = jnp.concatenate([runs_ref[2 * run + 1 - side, pl.ds(v * 8, 8), :] for v in range(2)], axis=1)
+    far = jnp.zeros((ROWS, SPAN), jnp.float32)
+    for slot in range(2 * RUNS):
+        value = jnp.concatenate([runs_ref[pl.ds(slot * SLOT + v * 8, 8), :] for v in range(2)], axis=1)
+        far = jnp.where(2 * run + 1 - side == slot, value, far)
     high, middle, low = split(jnp.concatenate([near, far], axis=0))
     one = product(jnp.concatenate([high, middle, low], axis=0), response_ref[0])
     two = product(jnp.concatenate([high, middle], axis=0), response_ref[1])
@@ -528,6 +547,7 @@
     in_ref,
     runs_ref,
     gather_ref,
+    gather_ninth_ref,
     local_first_ref,
     local_second_ref,
     spread_first_ref,
@@ -545,11 +565,17 @@
 ):
     run, tile, side = place()
     flux = edge_flux(in_ref, runs_ref, run, tile, side, edge_gather_ref[run], edge_response_ref, edge_inject_ref[...])
-    runs = [
-        jnp.concatenate([runs_ref[2 * other + side, pl.ds(v * 8, 8), :] for other in range(RUNS)], axis=0)
-        for v in range(3)
-    ]
+    runs = []
+    for v in range(2):
+        parts = []
+        for other in range(RUNS):
+            slots = [runs_ref[pl.ds((2 * other + i) * SLOT + v * 8, 8), :] for i in range(2)]
+            parts.append(jnp.where(side == 0, slots[0], slots[1]))
+        runs.append(jnp.concatenate(parts, axis=0))
     states = product(gather_ref[run], six_below(jnp.concatenate(runs, axis=1), 256))
+    pairs = [runs_ref[pl.ds(side * SLOT + 16 + i, RUNS, stride=2 * SLOT), :] for i in range(2)]
+    runs = jnp.concatenate([turn(pair, shift) for pair in pairs for shift in (0, 64)], axis=0)
+    states_ninth = product(gather_ninth_ref[run], six_below(runs, LANES))
     bases, locals_ = [], []
     for which in range(2):
         base, local = mapped(
@@ -564,7 +590,8 @@
         jnp.concatenate([ninth_second_ref[...], local_ninth_second_ref[run]], axis=0),
         ninth_of(in_ref),
     )
-    states = six_below(states + jnp.concatenate([locals_[0] + locals_[1], local], axis=1), LANES)
+    states = jnp.concatenate([states + (locals_[0] + locals_[1]), states_ninth + local], axis=1)
+    states = six_below(states, LANES)
     added = product(inject_ref[...], states[:, : 2 * LANES])
     ninth = ninth + product(inject_ninth_ref[...], states[:, 2 * LANES :])
     for which in range(2):
@@ -623,6 +650,7 @@
     half = 0.5 * mask_ref[...].astype(jnp.float32)
     last = lane == LANES - 1
     halos = borders_ref[pl.ds(tile * SLOT + 18, ROWS, stride=4 * SLOT), :]
+    halos = jnp.where(lane < 64, halos, pltpu.roll(halos, 4, 0))
     halos = jnp.where(tile == 0, turn(halos, 64), halos)
     outside = ((column == 0) & (lane < 64)) | ((column == 2 * len(PAIRS) - 1) & (lane >= 64))
     halos = jnp.where(outside, 0.0, halos)
@@ -659,8 +687,7 @@
         copy.wait()
 
 
-def swap(array, devices, columns):
-    groups = [[tm * 8 + col for tm in some for col in pair] for some in devices for pair in columns]
+def swap(array, groups):
     return lax.all_to_all(array, ("tm", "col"), 0, 0, tiled=True, axis_index_groups=groups)
 
 
@@ -688,8 +715,14 @@
     part = (3, HOURS, ROWS, LANES)
     flat = (OWNERS * SLOT, LANES)
     slots = (OWNERS, 1, SLOT * LANES)
-    runs = [[z * GROUP + j for j in range(GROUP)] for z in range(RUNS)]
-    across = [[z * GROUP + j for z in range(RUNS)] for j in range(GROUP)]
+    runs = [
+        [(z * GROUP + j) * 8 + col for j in range(GROUP) for col in pair] for z in range(RUNS) for pair in PAIRS
+    ]
+    across = [
+        [(z * GROUP + mine) * 8 + col for z in range(RUNS) for mine, col in zip((j, j ^ 8), pair)]
+        for j in range(GROUP)
+        for pair in FAR
+    ]
     state_scratch = pltpu.VMEM((SERIES * 8, ROWS, LANES), jnp.float32)
     arguments = (levels, u_vel, v_vel, density, land_mask, start_hour)
     own, kept = call(
@@ -707,13 +740,14 @@
             pltpu.SemaphoreType.DMA((6,)),
         ],
     )(*[pltpu.with_memory_space_constraint(array, pltpu.HBM) for array in arguments])
-    blocks = swap(own.reshape(slots), runs, PAIRS).reshape(flat)
-    (totals,) = call(run_kernel, [(2 * RUNS, 24, LANES)], [VMEM] * 4)(
+    blocks = swap(own.reshape(slots), runs).reshape(flat)
+    (totals,) = call(run_kernel, [(2 * RUNS * SLOT, LANES)], [VMEM] * 4)(
         blocks, tables["send"], tables["send_ninth"], tables["edge_sum"]
     )
-    totals = swap(totals, across, FAR)
+    totals = swap(totals.reshape(2 * RUNS, 1, SLOT * LANES), across).reshape(2 * RUNS * SLOT, LANES)
     names = (
         "gather",
+        "gather_ninth",
         "local_first",
         "local_second",
         "spread_first",
@@ -731,7 +765,7 @@
     (borders,) = call(border_kernel, [flat], [VMEM] * (2 + len(names)))(
         blocks, totals, *[tables[name] for name in names]
     )
-    borders = swap(borders.reshape(slots), runs, PAIRS).reshape(flat)
+    borders = swap(borders.reshape(slots), runs).reshape(flat)
     pressure, flux = call(
         band_kernel,
         [whole, whole],

time: 64.2 us -> 63 us (0.981)
  blocking collectives: 58 us -> 56.7 us
    all_to_all x3, blocking collectives: 58 us -> 56.7 us  [swap(): lax.all_to_all(array, ('tm', 'col'), 0, 0, tiled=True, axis_index_groups=...]
where the time goes in v7:
time: 63 us; the launch traced here: 62.3 us
  blocking collectives  56.7 us (90%)
  Pallas kernels  4.56 us (7%)
  between operations  0.9 us (1%)
    all_to_all x3, blocking collectives, swap(): lax.all_to_all(array, ('tm', 'col'), 0, 0, tiled=True, axis_index_groups=...  56.7 us
    pallas_call x1, Pallas kernels, on_device(): call(summary_kernel, [flat, (SERIES, HOURS, ROWS, LANES)], [HBM] * 6, [pl...  1.91 us
    pallas_call x1, Pallas kernels, on_device(): call(band_kernel, [whole, whole], [VMEM] * 3, [pltpu.VMEM(whole, jnp.floa...  1.37 us

profile of v7, /device:TPU:6, one launch (start us, length us, event | category | flops | bytes accessed | tf_op | source)
XLA Modules:
  0.0 62.3 jit_solution(1450057154425760419)
XLA Ops:
  0.6 0.0 copy-start.12
  0.6 0.0 copy-start.16
  0.7 0.0 copy-start.9
  0.7 0.0 copy-start.10
  0.7 0.0 copy-start.11
  0.7 0.0 copy-start.13
  0.7 0.0 copy-start.14
  0.7 0.0 copy-start.15
  0.7 1.9 %shard_map.239 = (f32[608,128]{1,0:T(8,128)S(1)}, f32[9,16,8,128]{3,2,1,0:T(8,128)S(1)}) custom-call(s32[4]{0:T(128)} %levels_hbm.1, f32[4,16,8,128]{3,2,1,0:T(8,128)} %u_hbm.1, f32[4,16,8,128]{3,2,1,0:T(8,128)} %v_hbm.1, f32[4,16,8,128]{3,2,1,0:T(8,128)} %rho_hbm.1, s32[8,128]{1,0:T(8,128)} %mask_ref.1, s32[8,128]{1,0:T(8,128)} %start_hbm.1), custom_call_target="tpu_custom_call" | custom-call | tf_op jit(solution)/shard_map/pallas_call | solution.py:728
  2.6 0.0 copy-start.2
  2.7 0.0 copy-start.3
  2.7 0.0 copy-start.4
  2.7 0.0 copy-start.5
  2.7 0.0 copy-start.7
  2.7 0.0 copy-start.8
  2.7 15.5 %all_to_all.15 = f32[32,1,2432]{2,1,0:T(1,128)S(1)} all-to-all(f32[32,1,2432]{2,1,0:T(1,128)S(1)} %bitcast.11), channel_id=1, replica_groups={{0,1,8,9,16,17,24,25,32,33,40,41,48,49,56,57,64,65,72,73,80,81,88,89,96..., dimensions={0} | all-to-all | bytes 622592 | tf_op jit(solution)/shard_map/all_to_all | solution.py:691
  18.2 0.0 copy-start
  18.2 0.0 copy-done.12
  18.2 0.0 copy-done.16
  18.2 0.0 copy-done.2
  18.2 0.0 copy-start.1
  18.3 0.4 shard_map.240
  18.7 0.0 copy-start.6
  18.7 0.0 copy-start.17
  18.7 27.6 %all_to_all.16 = f32[8,1,2432]{2,1,0:T(1,128)S(1)} all-to-all(f32[8,1,2432]{2,1,0:T(1,128)S(1)} %bitcast.12), channel_id=1, replica_groups={{1,66,129,194,257,322,385,450},{3,68,131,196,259,324,387,452},{5,70,133..., dimensions={0} | all-to-all | bytes 155648 | tf_op jit(solution)/shard_map/all_to_all | solution.py:691
  46.3 0.0 copy-done.9
  46.3 0.0 copy-done.10
  46.3 0.0 copy-done.11
  46.3 0.0 copy-done.13
  46.3 0.0 copy-done.14
  46.3 0.0 copy-done.15
  46.4 0.0 copy-done.3
  46.4 0.0 copy-done.4
  46.4 0.0 copy-done.5
  46.4 0.0 copy-done.7
  46.4 0.0 copy-done.8
  46.4 0.0 copy-done
  46.4 0.0 copy-done.1
  46.4 0.0 copy-done.6
  46.4 0.0 copy-done.17
  46.4 0.9 %shard_map.241 = f32[608,128]{1,0:T(8,128)S(1)} custom-call(f32[608,128]{1,0:T(8,128)S(1)} %bitcast.7, f32[152,128]{1,0:T(8,128)S(1)} %bitcast.10, bf16[4,16,256]{2,1,0:T(8,128)(2,1)S(1)} %copy-done.15, bf16[4,16,128]{2,1,0:T(8,128)(2,1)S(1)} %copy-done.17, bf16[4,2,32,256]{3,2,1,0:T(8,128)(2,1)S(1)} %copy-done.5, bf16[4,2,16,256]{3,2,1,0:T(8,128)(2,1)S(1)} %copy-done.11, ...), custom_call_target="tpu_custom_call" | custom-call | tf_op jit(solution)/shard_map/pallas_call | solution.py:765
  47.3 0.0 copy-start.18
  47.3 13.5 %all_to_all.17 = f32[32,1,2432]{2,1,0:T(1,128)S(1)} all-to-all(f32[32,1,2432]{2,1,0:T(1,128)S(1)} %bitcast.8), channel_id=1, replica_groups={{0,1,8,9,16,17,24,25,32,33,40,41,48,49,56,57,64,65,72,73,80,81,88,89,96..., dimensions={0} | all-to-all | bytes 622592 | tf_op jit(solution)/shard_map/all_to_all | solution.py:691
  60.9 0.0 copy-done.18
  60.9 1.4 %shard_map.242 = (f32[4,16,8,128]{3,2,1,0:T(8,128)}, f32[4,16,8,128]{3,2,1,0:T(8,128)}) custom-call(f32[9,16,8,128]{3,2,1,0:T(8,128)S(1)} %get-tuple-element.4.kept_ref, s32[8,128]{1,0:T(8,128)S(1)} %copy-done.18, f32[608,128]{1,0:T(8,128)S(1)} %bitcast.9), custom_call_target="tpu_custom_call" | custom-call | tf_op jit(solution)/shard_map/pallas_call | solution.py:769
Async XLA Ops:
  0.6 17.6 %copy-start.12 = (f32[4,16,256]{2,1,0:T(8,128)S(1)}, f32[4,16,256]{2,1,0:T(8,128)}, u32[]{:S(2)}) copy-start(f32[4,16,256]{2,1,0:T(8,128)} %constant.36.clone.send_ref) | copy-start | bytes 196612
  0.6 17.6 %copy-start.16 = (f32[4,16,128]{2,1,0:T(8,128)S(1)}, f32[4,16,128]{2,1,0:T(8,128)}, u32[]{:S(2)}) copy-start(f32[4,16,128]{2,1,0:T(8,128)} %constant.37.clone.send_ninth_ref) | copy-start | bytes 98308
  0.7 45.7 %copy-start.9 = (bf16[256,128]{1,0:T(8,128)(2,1)S(1)}, bf16[256,128]{1,0:T(8,128)(2,1)}, u32[]{:S(2)}) copy-start(bf16[256,128]{1,0:T(8,128)(2,1)} %constant.45.clone.inject_ref) | copy-start | bytes 196612
  0.7 45.7 %copy-start.10 = (bf16[128,256]{1,0:T(8,128)(2,1)S(1)}, bf16[128,256]{1,0:T(8,128)(2,1)}, u32[]{:S(2)}) copy-start(bf16[128,256]{1,0:T(8,128)(2,1)} %constant.44.clone.spread_second_ref) | copy-start | bytes 196612
  0.7 45.6 %copy-start.11 = (bf16[4,2,16,256]{3,2,1,0:T(8,128)(2,1)S(1)}, bf16[4,2,16,256]{3,2,1,0:T(8,128)(2,1)}, u32[]{:S(2)}) copy-start(bf16[4,2,16,256]{3,2,1,0:T(8,128)(2,1)} %constant.42.clone.local_second_ref) | copy-start | bytes 196612
  0.7 45.6 %copy-start.13 = (bf16[128,128]{1,0:T(8,128)(2,1)S(1)}, bf16[128,128]{1,0:T(8,128)(2,1)}, u32[]{:S(2)}) copy-start(bf16[128,128]{1,0:T(8,128)(2,1)} %constant.50.clone.inject_ninth_ref) | copy-start | bytes 98308
  0.7 45.6 %copy-start.14 = (bf16[4,16,256]{2,1,0:T(8,128)(2,1)S(1)}, bf16[4,16,256]{2,1,0:T(8,128)(2,1)}, u32[]{:S(2)}) copy-start(bf16[4,16,256]{2,1,0:T(8,128)(2,1)} %constant.47.clone.local_ninth_second_ref) | copy-start | bytes 98308
  0.7 45.6 %copy-start.15 = (bf16[4,16,256]{2,1,0:T(8,128)(2,1)S(1)}, bf16[4,16,256]{2,1,0:T(8,128)(2,1)}, u32[]{:S(2)}) copy-start(bf16[4,16,256]{2,1,0:T(8,128)(2,1)} %constant.39.clone.gather_ref) | copy-start | bytes 98308
  2.6 15.6 %copy-start.2 = (f32[256,128]{1,0:T(8,128)S(1)}, f32[256,128]{1,0:T(8,128)}, u32[]{:S(2)}) copy-start(f32[256,128]{1,0:T(8,128)} %constant.38.clone.edge_sum_ref) | copy-start | bytes 393220
  2.7 43.7 %copy-start.3 = (bf16[256,256]{1,0:T(8,128)(2,1)S(1)}, bf16[256,256]{1,0:T(8,128)(2,1)}, u32[]{:S(2)}) copy-start(bf16[256,256]{1,0:T(8,128)(2,1)} %constant.48.clone.ninth_first_ref) | copy-start | bytes 393220
  2.7 43.7 %copy-start.4 = (bf16[256,256]{1,0:T(8,128)(2,1)S(1)}, bf16[256,256]{1,0:T(8,128)(2,1)}, u32[]{:S(2)}) copy-start(bf16[256,256]{1,0:T(8,128)(2,1)} %constant.43.clone.spread_first_ref) | copy-start | bytes 393220
  2.7 43.7 %copy-start.5 = (bf16[4,2,32,256]{3,2,1,0:T(8,128)(2,1)S(1)}, bf16[4,2,32,256]{3,2,1,0:T(8,128)(2,1)}, u32[]{:S(2)}) copy-start(bf16[4,2,32,256]{3,2,1,0:T(8,128)(2,1)} %constant.41.clone.local_first_ref) | copy-start | bytes 393220
  2.7 43.7 %copy-start.7 = (bf16[128,256]{1,0:T(8,128)(2,1)S(1)}, bf16[128,256]{1,0:T(8,128)(2,1)}, u32[]{:S(2)}) copy-start(bf16[128,256]{1,0:T(8,128)(2,1)} %constant.49.clone.ninth_second_ref) | copy-start | bytes 196612
  2.7 43.7 %copy-start.8 = (bf16[4,32,256]{2,1,0:T(8,128)(2,1)S(1)}, bf16[4,32,256]{2,1,0:T(8,128)(2,1)}, u32[]{:S(2)}) copy-start(bf16[4,32,256]{2,1,0:T(8,128)(2,1)} %constant.46.clone.local_ninth_first_ref) | copy-start | bytes 196612
  18.2 28.2 %copy-start = (bf16[3,256,256]{2,1,0:T(8,128)(2,1)S(1)}, bf16[3,256,256]{2,1,0:T(8,128)(2,1)}, u32[]{:S(2)}) copy-start(bf16[3,256,256]{2,1,0:T(8,128)(2,1)} %constant.52.clone.edge_response_ref) | copy-start | bytes 1179652
  18.2 28.2 %copy-start.1 = (bf16[4,256,128]{2,1,0:T(8,128)(2,1)S(1)}, bf16[4,256,128]{2,1,0:T(8,128)(2,1)}, u32[]{:S(2)}) copy-start(bf16[4,256,128]{2,1,0:T(8,128)(2,1)} %constant.51.clone.edge_gather_ref) | copy-start | bytes 786436
  18.7 27.8 %copy-start.6 = (bf16[128,256]{1,0:T(8,128)(2,1)S(1)}, bf16[128,256]{1,0:T(8,128)(2,1)}, u32[]{:S(2)}) copy-start(bf16[128,256]{1,0:T(8,128)(2,1)} %constant.53.clone.edge_inject_ref) | copy-start | bytes 196612
  18.7 27.8 %copy-start.17 = (bf16[4,16,128]{2,1,0:T(8,128)(2,1)S(1)}, bf16[4,16,128]{2,1,0:T(8,128)(2,1)}, u32[]{:S(2)}) copy-start(bf16[4,16,128]{2,1,0:T(8,128)(2,1)} %constant.40.clone.gather_ninth_ref) | copy-start | bytes 49156
  47.3 13.6 %copy-start.18 = (s32[8,128]{1,0:T(8,128)S(1)}, s32[8,128]{1,0:T(8,128)}, u32[]{:S(2)}) copy-start(s32[8,128]{1,0:T(8,128)} %mask_ref.1) | copy-start | bytes 12292

commit v8 on v7

--- a/solution.py
+++ b/solution.py
@@ -22,7 +22,11 @@
 SPAN = GROUP * HOURS
 QUARTERS = (0, 3, 1, 2)
 PAIRS = ((0, 1), (2, 3), (4, 5), (6, 7))
-FAR = ((1, 2), (3, 4), (5, 6), (7, 0))
+MEETINGS = (
+    ((1, 2, 0), (5, 6, 0), (0, 4, 8), (3, 7, 8)),
+    ((2, 5, 8), (1, 6, 8), (0, 4, 8), (3, 7, 8)),
+)
+SECOND = tuple(sum(1 << meeting[1] for meeting in meetings) for meetings in MEETINGS)
 HIGH = lax.Precision.HIGHEST
 
 
@@ -254,8 +258,10 @@
 
 
 def place():
-    tile = lax.axis_index("col") % 2
-    return lax.axis_index("tm") // GROUP, tile, 1 - tile
+    device, column = lax.axis_index("tm"), lax.axis_index("col")
+    odd = device % 2
+    second = jnp.where(odd == 0, SECOND[0], SECOND[1])
+    return device // GROUP, (column + odd) % 2, lax.shift_right_logical(second, column) & 1
 
 
 def lanes_of(shape=(ROWS, LANES)):
@@ -381,8 +387,8 @@
                 sums_ref[(which * 3 + level) * 8 + k] = sums[level][k]
         if which == 1:
             edges = finished_edges(west, east, lane)
-            for index, quarter in enumerate(QUARTERS):
-                out_ref[pl.ds(index * SLOT + 18, ROWS, stride=4 * SLOT), :] = edges.get(quarter, zeros)
+            for index in range(4):
+                out_ref[pl.ds(index * SLOT + 18, ROWS, stride=4 * SLOT), :] = edges[(0, 1, 1, 0)[index]]
             lay_out(sums_ref, list(range(4)), out_ref, 0, lane)
     lay_out(sums_ref, list(range(4, 8)), out_ref, 8, lane)
     for v in range(2):
@@ -395,7 +401,7 @@
     for ends in (west, turn(east, 1)):
         three = -((turn(ends, -HOURS) + turn(ends, -2 * HOURS)) + turn(ends, -3 * HOURS))
         out.append(jnp.where((block == 5) | (block == 1), three, ends))
-    return {0: out[0], 3: out[1]}
+    return out
 
 
 def lay_out(sums_ref, series, out_ref, first, lane):
@@ -628,8 +634,8 @@
 def band_kernel(
     kept_ref, mask_ref, borders_ref, press_hbm, flux_hbm, press_ref, flux_ref, east_ref, north_ref, states_ref, sems
 ):
-    _, tile, _ = place()
     column = lax.axis_index("col")
+    tile = column % 2
     lane = lanes_of()
     for v in range(2):
         for k in range(8):
@@ -650,7 +656,9 @@
     half = 0.5 * mask_ref[...].astype(jnp.float32)
     last = lane == LANES - 1
     halos = borders_ref[pl.ds(tile * SLOT + 18, ROWS, stride=4 * SLOT), :]
-    halos = jnp.where(lane < 64, halos, pltpu.roll(halos, 4, 0))
+    other = borders_ref[pl.ds((3 - tile) * SLOT + 18, ROWS, stride=4 * SLOT), :]
+    half_way = (column == 3) | (column == 4)
+    halos = jnp.where(half_way & (lane >= 64), pltpu.roll(other, 4, 0), halos)
     halos = jnp.where(tile == 0, turn(halos, 64), halos)
     outside = ((column == 0) & (lane < 64)) | ((column == 2 * len(PAIRS) - 1) & (lane >= 64))
     halos = jnp.where(outside, 0.0, halos)
@@ -719,9 +727,9 @@
         [(z * GROUP + j) * 8 + col for j in range(GROUP) for col in pair] for z in range(RUNS) for pair in PAIRS
     ]
     across = [
-        [(z * GROUP + mine) * 8 + col for z in range(RUNS) for mine, col in zip((j, j ^ 8), pair)]
+        [(z * GROUP + mine) * 8 + col for z in range(RUNS) for mine, col in ((j, first), (j ^ flip, second))]
         for j in range(GROUP)
-        for pair in FAR
+        for first, second, flip in MEETINGS[j % 2]
     ]
     state_scratch = pltpu.VMEM((SERIES * 8, ROWS, LANES), jnp.float32)
     arguments = (levels, u_vel, v_vel, density, land_mask, start_hour)

time: 63 us -> 61.4 us (0.975)
  the two profiles are of different devices: /device:TPU:6 before, /device:TPU:1 now
where the time goes in v8:
time: 61.4 us; the launch traced here: 61.1 us
  blocking collectives  55.5 us (90%)
  Pallas kernels  4.57 us (7%)
  between operations  0.9 us (1%)
    all_to_all x3, blocking collectives, swap(): lax.all_to_all(array, ('tm', 'col'), 0, 0, tiled=True, axis_index_groups=...  55.5 us
    pallas_call x1, Pallas kernels, on_device(): call(summary_kernel, [flat, (SERIES, HOURS, ROWS, LANES)], [HBM] * 6, [pl...  1.91 us
    pallas_call x1, Pallas kernels, on_device(): call(band_kernel, [whole, whole], [VMEM] * 3, [pltpu.VMEM(whole, jnp.floa...  1.38 us

profile of v8, /device:TPU:1, one launch (start us, length us, event | category | flops | bytes accessed | tf_op | source)
XLA Modules:
  0.0 61.1 jit_solution(3498024500338867746)
XLA Ops:
  0.6 0.0 copy-start.12
  0.6 0.0 copy-start.16
  0.7 0.0 copy-start.9
  0.7 0.0 copy-start.10
  0.7 0.0 copy-start.11
  0.7 0.0 copy-start.13
  0.7 0.0 copy-start.14
  0.7 0.0 copy-start.15
  0.7 1.9 %shard_map.239 = (f32[608,128]{1,0:T(8,128)S(1)}, f32[9,16,8,128]{3,2,1,0:T(8,128)S(1)}) custom-call(s32[4]{0:T(128)} %levels_hbm.1, f32[4,16,8,128]{3,2,1,0:T(8,128)} %u_hbm.1, f32[4,16,8,128]{3,2,1,0:T(8,128)} %v_hbm.1, f32[4,16,8,128]{3,2,1,0:T(8,128)} %rho_hbm.1, s32[8,128]{1,0:T(8,128)} %mask_ref.1, s32[8,128]{1,0:T(8,128)} %start_hbm.1), custom_call_target="tpu_custom_call" | custom-call | tf_op jit(solution)/shard_map/pallas_call | solution.py:736
  2.6 0.0 copy-start.2
  2.7 0.0 copy-start.3
  2.7 0.0 copy-start.4
  2.7 0.0 copy-start.5
  2.7 0.0 copy-start.7
  2.7 0.0 copy-start.8
  2.7 18.1 %all_to_all.15 = f32[32,1,2432]{2,1,0:T(1,128)S(1)} all-to-all(f32[32,1,2432]{2,1,0:T(1,128)S(1)} %bitcast.11), channel_id=1, replica_groups={{0,1,8,9,16,17,24,25,32,33,40,41,48,49,56,57,64,65,72,73,80,81,88,89,96..., dimensions={0} | all-to-all | bytes 622592 | tf_op jit(solution)/shard_map/all_to_all | solution.py:699
  20.8 0.0 copy-start
  20.8 0.0 copy-done.12
  20.8 0.0 copy-done.16
  20.8 0.0 copy-done.2
  20.8 0.0 copy-start.1
  20.8 0.4 shard_map.240
  21.2 0.0 copy-start.6
  21.2 0.0 copy-start.17
  21.2 22.7 %all_to_all.16 = f32[8,1,2432]{2,1,0:T(1,128)S(1)} all-to-all(f32[8,1,2432]{2,1,0:T(1,128)S(1)} %bitcast.12), channel_id=1, replica_groups={{1,2,129,130,257,258,385,386},{5,6,133,134,261,262,389,390},{0,68,128,1..., dimensions={0} | all-to-all | bytes 155648 | tf_op jit(solution)/shard_map/all_to_all | solution.py:699
  44.0 0.0 copy-done.9
  44.0 0.0 copy-done.10
  44.0 0.0 copy-done.11
  44.0 0.0 copy-done.13
  44.0 0.0 copy-done.14
  44.0 0.0 copy-done.15
  44.0 0.0 copy-done.3
  44.0 0.0 copy-done.4
  44.0 0.0 copy-done.5
  44.0 0.0 copy-done.7
  44.1 0.0 copy-done.8
  44.1 0.0 copy-done
  44.1 0.0 copy-done.1
  44.1 0.0 copy-done.6
  44.1 0.0 copy-done.17
  44.1 0.9 %shard_map.241 = f32[608,128]{1,0:T(8,128)S(1)} custom-call(f32[608,128]{1,0:T(8,128)S(1)} %bitcast.7, f32[152,128]{1,0:T(8,128)S(1)} %bitcast.10, bf16[4,16,256]{2,1,0:T(8,128)(2,1)S(1)} %copy-done.15, bf16[4,16,128]{2,1,0:T(8,128)(2,1)S(1)} %copy-done.17, bf16[4,2,32,256]{3,2,1,0:T(8,128)(2,1)S(1)} %copy-done.5, bf16[4,2,16,256]{3,2,1,0:T(8,128)(2,1)S(1)} %copy-done.11, ...), custom_call_target="tpu_custom_call" | custom-call | tf_op jit(solution)/shard_map/pallas_call | solution.py:773
  45.0 0.0 copy-start.18
  45.0 14.7 %all_to_all.17 = f32[32,1,2432]{2,1,0:T(1,128)S(1)} all-to-all(f32[32,1,2432]{2,1,0:T(1,128)S(1)} %bitcast.8), channel_id=1, replica_groups={{0,1,8,9,16,17,24,25,32,33,40,41,48,49,56,57,64,65,72,73,80,81,88,89,96..., dimensions={0} | all-to-all | bytes 622592 | tf_op jit(solution)/shard_map/all_to_all | solution.py:699
  59.7 0.0 copy-done.18
  59.7 1.4 %shard_map.242 = (f32[4,16,8,128]{3,2,1,0:T(8,128)}, f32[4,16,8,128]{3,2,1,0:T(8,128)}) custom-call(f32[9,16,8,128]{3,2,1,0:T(8,128)S(1)} %get-tuple-element.4.kept_ref, s32[8,128]{1,0:T(8,128)S(1)} %copy-done.18, f32[608,128]{1,0:T(8,128)S(1)} %bitcast.9), custom_call_target="tpu_custom_call" | custom-call | tf_op jit(solution)/shard_map/pallas_call | solution.py:777
Async XLA Ops:
  0.6 20.2 %copy-start.12 = (f32[4,16,256]{2,1,0:T(8,128)S(1)}, f32[4,16,256]{2,1,0:T(8,128)}, u32[]{:S(2)}) copy-start(f32[4,16,256]{2,1,0:T(8,128)} %constant.36.clone.send_ref) | copy-start | bytes 196612
  0.6 20.1 %copy-start.16 = (f32[4,16,128]{2,1,0:T(8,128)S(1)}, f32[4,16,128]{2,1,0:T(8,128)}, u32[]{:S(2)}) copy-start(f32[4,16,128]{2,1,0:T(8,128)} %constant.37.clone.send_ninth_ref) | copy-start | bytes 98308
  0.7 43.3 %copy-start.9 = (bf16[256,128]{1,0:T(8,128)(2,1)S(1)}, bf16[256,128]{1,0:T(8,128)(2,1)}, u32[]{:S(2)}) copy-start(bf16[256,128]{1,0:T(8,128)(2,1)} %constant.45.clone.inject_ref) | copy-start | bytes 196612
  0.7 43.3 %copy-start.10 = (bf16[128,256]{1,0:T(8,128)(2,1)S(1)}, bf16[128,256]{1,0:T(8,128)(2,1)}, u32[]{:S(2)}) copy-start(bf16[128,256]{1,0:T(8,128)(2,1)} %constant.44.clone.spread_second_ref) | copy-start | bytes 196612
  0.7 43.3 %copy-start.11 = (bf16[4,2,16,256]{3,2,1,0:T(8,128)(2,1)S(1)}, bf16[4,2,16,256]{3,2,1,0:T(8,128)(2,1)}, u32[]{:S(2)}) copy-start(bf16[4,2,16,256]{3,2,1,0:T(8,128)(2,1)} %constant.42.clone.local_second_ref) | copy-start | bytes 196612
  0.7 43.3 %copy-start.13 = (bf16[128,128]{1,0:T(8,128)(2,1)S(1)}, bf16[128,128]{1,0:T(8,128)(2,1)}, u32[]{:S(2)}) copy-start(bf16[128,128]{1,0:T(8,128)(2,1)} %constant.50.clone.inject_ninth_ref) | copy-start | bytes 98308
  0.7 43.3 %copy-start.14 = (bf16[4,16,256]{2,1,0:T(8,128)(2,1)S(1)}, bf16[4,16,256]{2,1,0:T(8,128)(2,1)}, u32[]{:S(2)}) copy-start(bf16[4,16,256]{2,1,0:T(8,128)(2,1)} %constant.47.clone.local_ninth_second_ref) | copy-start | bytes 98308
  0.7 43.3 %copy-start.15 = (bf16[4,16,256]{2,1,0:T(8,128)(2,1)S(1)}, bf16[4,16,256]{2,1,0:T(8,128)(2,1)}, u32[]{:S(2)}) copy-start(bf16[4,16,256]{2,1,0:T(8,128)(2,1)} %constant.39.clone.gather_ref) | copy-start | bytes 98308
  2.6 18.1 %copy-start.2 = (f32[256,128]{1,0:T(8,128)S(1)}, f32[256,128]{1,0:T(8,128)}, u32[]{:S(2)}) copy-start(f32[256,128]{1,0:T(8,128)} %constant.38.clone.edge_sum_ref) | copy-start | bytes 393220
  2.7 41.4 %copy-start.3 = (bf16[256,256]{1,0:T(8,128)(2,1)S(1)}, bf16[256,256]{1,0:T(8,128)(2,1)}, u32[]{:S(2)}) copy-start(bf16[256,256]{1,0:T(8,128)(2,1)} %constant.48.clone.ninth_first_ref) | copy-start | bytes 393220
  2.7 41.4 %copy-start.4 = (bf16[256,256]{1,0:T(8,128)(2,1)S(1)}, bf16[256,256]{1,0:T(8,128)(2,1)}, u32[]{:S(2)}) copy-start(bf16[256,256]{1,0:T(8,128)(2,1)} %constant.43.clone.spread_first_ref) | copy-start | bytes 393220
  2.7 41.4 %copy-start.5 = (bf16[4,2,32,256]{3,2,1,0:T(8,128)(2,1)S(1)}, bf16[4,2,32,256]{3,2,1,0:T(8,128)(2,1)}, u32[]{:S(2)}) copy-start(bf16[4,2,32,256]{3,2,1,0:T(8,128)(2,1)} %constant.41.clone.local_first_ref) | copy-start | bytes 393220
  2.7 41.4 %copy-start.7 = (bf16[128,256]{1,0:T(8,128)(2,1)S(1)}, bf16[128,256]{1,0:T(8,128)(2,1)}, u32[]{:S(2)}) copy-start(bf16[128,256]{1,0:T(8,128)(2,1)} %constant.49.clone.ninth_second_ref) | copy-start | bytes 196612
  2.7 41.4 %copy-start.8 = (bf16[4,32,256]{2,1,0:T(8,128)(2,1)S(1)}, bf16[4,32,256]{2,1,0:T(8,128)(2,1)}, u32[]{:S(2)}) copy-start(bf16[4,32,256]{2,1,0:T(8,128)(2,1)} %constant.46.clone.local_ninth_first_ref) | copy-start | bytes 196612
  20.8 23.3 %copy-start = (bf16[3,256,256]{2,1,0:T(8,128)(2,1)S(1)}, bf16[3,256,256]{2,1,0:T(8,128)(2,1)}, u32[]{:S(2)}) copy-start(bf16[3,256,256]{2,1,0:T(8,128)(2,1)} %constant.52.clone.edge_response_ref) | copy-start | bytes 1179652
  20.8 23.3 %copy-start.1 = (bf16[4,256,128]{2,1,0:T(8,128)(2,1)S(1)}, bf16[4,256,128]{2,1,0:T(8,128)(2,1)}, u32[]{:S(2)}) copy-start(bf16[4,256,128]{2,1,0:T(8,128)(2,1)} %constant.51.clone.edge_gather_ref) | copy-start | bytes 786436
  21.2 22.9 %copy-start.6 = (bf16[128,256]{1,0:T(8,128)(2,1)S(1)}, bf16[128,256]{1,0:T(8,128)(2,1)}, u32[]{:S(2)}) copy-start(bf16[128,256]{1,0:T(8,128)(2,1)} %constant.53.clone.edge_inject_ref) | copy-start | bytes 196612
  21.2 22.9 %copy-start.17 = (bf16[4,16,128]{2,1,0:T(8,128)(2,1)S(1)}, bf16[4,16,128]{2,1,0:T(8,128)(2,1)}, u32[]{:S(2)}) copy-start(bf16[4,16,128]{2,1,0:T(8,128)(2,1)} %constant.40.clone.gather_ninth_ref) | copy-start | bytes 49156
  45.0 14.7 %copy-start.18 = (s32[8,128]{1,0:T(8,128)S(1)}, s32[8,128]{1,0:T(8,128)}, u32[]{:S(2)}) copy-start(s32[8,128]{1,0:T(8,128)} %mask_ref.1) | copy-start | bytes 12292

commit v9 on v8

--- a/solution.py
+++ b/solution.py
@@ -23,8 +23,8 @@
 QUARTERS = (0, 3, 1, 2)
 PAIRS = ((0, 1), (2, 3), (4, 5), (6, 7))
 MEETINGS = (
-    ((1, 2, 0), (5, 6, 0), (0, 4, 8), (3, 7, 8)),
-    ((2, 5, 8), (1, 6, 8), (0, 4, 8), (3, 7, 8)),
+    ((1, 2, 0), (5, 6, 0), (0, 3, 0), (4, 7, 0)),
+    ((2, 5, 8), (3, 7, 8), (0, 1, 0), (4, 6, 0)),
 )
 SECOND = tuple(sum(1 << meeting[1] for meeting in meetings) for meetings in MEETINGS)
 HIGH = lax.Precision.HIGHEST

time: 61.4 us -> 60 us (0.977)
  blocking collectives: 55.5 us -> 54.1 us
    all_to_all x3, blocking collectives: 55.5 us -> 54.1 us  [swap(): lax.all_to_all(array, ('tm', 'col'), 0, 0, tiled=True, axis_index_groups=...]
where the time goes in v9:
time: 60 us; the launch traced here: 59.7 us
  blocking collectives  54.1 us (90%)
  Pallas kernels  4.57 us (8%)
  between operations  0.9 us (2%)
    all_to_all x3, blocking collectives, swap(): lax.all_to_all(array, ('tm', 'col'), 0, 0, tiled=True, axis_index_groups=...  54.1 us
    pallas_call x1, Pallas kernels, on_device(): call(summary_kernel, [flat, (SERIES, HOURS, ROWS, LANES)], [HBM] * 6, [pl...  1.91 us
    pallas_call x1, Pallas kernels, on_device(): call(band_kernel, [whole, whole], [VMEM] * 3, [pltpu.VMEM(whole, jnp.floa...  1.38 us

profile of v9, /device:TPU:1, one launch (start us, length us, event | category | flops | bytes accessed | tf_op | source)
XLA Modules:
  0.0 59.7 jit_solution(9642842172124153549)
XLA Ops:
  0.6 0.0 copy-start.12
  0.6 0.0 copy-start.16
  0.7 0.0 copy-start.9
  0.7 0.0 copy-start.10
  0.7 0.0 copy-start.11
  0.7 0.0 copy-start.13
  0.7 0.0 copy-start.14
  0.7 0.0 copy-start.15
  0.7 1.9 %shard_map.239 = (f32[608,128]{1,0:T(8,128)S(1)}, f32[9,16,8,128]{3,2,1,0:T(8,128)S(1)}) custom-call(s32[4]{0:T(128)} %levels_hbm.1, f32[4,16,8,128]{3,2,1,0:T(8,128)} %u_hbm.1, f32[4,16,8,128]{3,2,1,0:T(8,128)} %v_hbm.1, f32[4,16,8,128]{3,2,1,0:T(8,128)} %rho_hbm.1, s32[8,128]{1,0:T(8,128)} %mask_ref.1, s32[8,128]{1,0:T(8,128)} %start_hbm.1), custom_call_target="tpu_custom_call" | custom-call | tf_op jit(solution)/shard_map/pallas_call | solution.py:736
  2.6 0.0 copy-start.2
  2.7 0.0 copy-start.3
  2.7 0.0 copy-start.4
  2.7 0.0 copy-start.5
  2.7 0.0 copy-start.7
  2.7 0.0 copy-start.8
  2.7 18.1 %all_to_all.15 = f32[32,1,2432]{2,1,0:T(1,128)S(1)} all-to-all(f32[32,1,2432]{2,1,0:T(1,128)S(1)} %bitcast.11), channel_id=1, replica_groups={{0,1,8,9,16,17,24,25,32,33,40,41,48,49,56,57,64,65,72,73,80,81,88,89,96..., dimensions={0} | all-to-all | bytes 622592 | tf_op jit(solution)/shard_map/all_to_all | solution.py:699
  20.8 0.0 copy-start
  20.8 0.0 copy-done.12
  20.8 0.0 copy-done.16
  20.8 0.0 copy-done.2
  20.8 0.0 copy-start.1
  20.8 0.4 shard_map.240
  21.2 0.0 copy-start.6
  21.2 0.0 copy-start.17
  21.2 19.7 %all_to_all.16 = f32[8,1,2432]{2,1,0:T(1,128)S(1)} all-to-all(f32[8,1,2432]{2,1,0:T(1,128)S(1)} %bitcast.12), channel_id=1, replica_groups={{1,2,129,130,257,258,385,386},{5,6,133,134,261,262,389,390},{0,3,128,13..., dimensions={0} | all-to-all | bytes 155648 | tf_op jit(solution)/shard_map/all_to_all | solution.py:699
  41.0 0.0 copy-done.9
  41.0 0.0 copy-done.10
  41.0 0.0 copy-done.11
  41.0 0.0 copy-done.13
  41.0 0.0 copy-done.14
  41.0 0.0 copy-done.15
  41.0 0.0 copy-done.3
  41.0 0.0 copy-done.4
  41.0 0.0 copy-done.5
  41.0 0.0 copy-done.7
  41.0 0.0 copy-done.8
  41.0 0.0 copy-done
  41.1 0.0 copy-done.1
  41.1 0.0 copy-done.6
  41.1 0.0 copy-done.17
  41.1 0.9 %shard_map.241 = f32[608,128]{1,0:T(8,128)S(1)} custom-call(f32[608,128]{1,0:T(8,128)S(1)} %bitcast.7, f32[152,128]{1,0:T(8,128)S(1)} %bitcast.10, bf16[4,16,256]{2,1,0:T(8,128)(2,1)S(1)} %copy-done.15, bf16[4,16,128]{2,1,0:T(8,128)(2,1)S(1)} %copy-done.17, bf16[4,2,32,256]{3,2,1,0:T(8,128)(2,1)S(1)} %copy-done.5, bf16[4,2,16,256]{3,2,1,0:T(8,128)(2,1)S(1)} %copy-done.11, ...), custom_call_target="tpu_custom_call" | custom-call | tf_op jit(solution)/shard_map/pallas_call | solution.py:773
  42.0 0.0 copy-start.18
  42.0 16.3 %all_to_all.17 = f32[32,1,2432]{2,1,0:T(1,128)S(1)} all-to-all(f32[32,1,2432]{2,1,0:T(1,128)S(1)} %bitcast.8), channel_id=1, replica_groups={{0,1,8,9,16,17,24,25,32,33,40,41,48,49,56,57,64,65,72,73,80,81,88,89,96..., dimensions={0} | all-to-all | bytes 622592 | tf_op jit(solution)/shard_map/all_to_all | solution.py:699
  58.3 0.0 copy-done.18
  58.3 1.4 %shard_map.242 = (f32[4,16,8,128]{3,2,1,0:T(8,128)}, f32[4,16,8,128]{3,2,1,0:T(8,128)}) custom-call(f32[9,16,8,128]{3,2,1,0:T(8,128)S(1)} %get-tuple-element.4.kept_ref, s32[8,128]{1,0:T(8,128)S(1)} %copy-done.18, f32[608,128]{1,0:T(8,128)S(1)} %bitcast.9), custom_call_target="tpu_custom_call" | custom-call | tf_op jit(solution)/shard_map/pallas_call | solution.py:777
Async XLA Ops:
  0.6 20.2 %copy-start.12 = (f32[4,16,256]{2,1,0:T(8,128)S(1)}, f32[4,16,256]{2,1,0:T(8,128)}, u32[]{:S(2)}) copy-start(f32[4,16,256]{2,1,0:T(8,128)} %constant.36.clone.send_ref) | copy-start | bytes 196612
  0.6 20.1 %copy-start.16 = (f32[4,16,128]{2,1,0:T(8,128)S(1)}, f32[4,16,128]{2,1,0:T(8,128)}, u32[]{:S(2)}) copy-start(f32[4,16,128]{2,1,0:T(8,128)} %constant.37.clone.send_ninth_ref) | copy-start | bytes 98308
  0.7 40.3 %copy-start.9 = (bf16[256,128]{1,0:T(8,128)(2,1)S(1)}, bf16[256,128]{1,0:T(8,128)(2,1)}, u32[]{:S(2)}) copy-start(bf16[256,128]{1,0:T(8,128)(2,1)} %constant.45.clone.inject_ref) | copy-start | bytes 196612
  0.7 40.3 %copy-start.10 = (bf16[128,256]{1,0:T(8,128)(2,1)S(1)}, bf16[128,256]{1,0:T(8,128)(2,1)}, u32[]{:S(2)}) copy-start(bf16[128,256]{1,0:T(8,128)(2,1)} %constant.44.clone.spread_second_ref) | copy-start | bytes 196612
  0.7 40.3 %copy-start.11 = (bf16[4,2,16,256]{3,2,1,0:T(8,128)(2,1)S(1)}, bf16[4,2,16,256]{3,2,1,0:T(8,128)(2,1)}, u32[]{:S(2)}) copy-start(bf16[4,2,16,256]{3,2,1,0:T(8,128)(2,1)} %constant.42.clone.local_second_ref) | copy-start | bytes 196612
  0.7 40.3 %copy-start.13 = (bf16[128,128]{1,0:T(8,128)(2,1)S(1)}, bf16[128,128]{1,0:T(8,128)(2,1)}, u32[]{:S(2)}) copy-start(bf16[128,128]{1,0:T(8,128)(2,1)} %constant.50.clone.inject_ninth_ref) | copy-start | bytes 98308
  0.7 40.3 %copy-start.14 = (bf16[4,16,256]{2,1,0:T(8,128)(2,1)S(1)}, bf16[4,16,256]{2,1,0:T(8,128)(2,1)}, u32[]{:S(2)}) copy-start(bf16[4,16,256]{2,1,0:T(8,128)(2,1)} %constant.47.clone.local_ninth_second_ref) | copy-start | bytes 98308
  0.7 40.3 %copy-start.15 = (bf16[4,16,256]{2,1,0:T(8,128)(2,1)S(1)}, bf16[4,16,256]{2,1,0:T(8,128)(2,1)}, u32[]{:S(2)}) copy-start(bf16[4,16,256]{2,1,0:T(8,128)(2,1)} %constant.39.clone.gather_ref) | copy-start | bytes 98308
  2.6 18.1 %copy-start.2 = (f32[256,128]{1,0:T(8,128)S(1)}, f32[256,128]{1,0:T(8,128)}, u32[]{:S(2)}) copy-start(f32[256,128]{1,0:T(8,128)} %constant.38.clone.edge_sum_ref) | copy-start | bytes 393220
  2.7 38.3 %copy-start.3 = (bf16[256,256]{1,0:T(8,128)(2,1)S(1)}, bf16[256,256]{1,0:T(8,128)(2,1)}, u32[]{:S(2)}) copy-start(bf16[256,256]{1,0:T(8,128)(2,1)} %constant.48.clone.ninth_first_ref) | copy-start | bytes 393220
  2.7 38.3 %copy-start.4 = (bf16[256,256]{1,0:T(8,128)(2,1)S(1)}, bf16[256,256]{1,0:T(8,128)(2,1)}, u32[]{:S(2)}) copy-start(bf16[256,256]{1,0:T(8,128)(2,1)} %constant.43.clone.spread_first_ref) | copy-start | bytes 393220
  2.7 38.3 %copy-start.5 = (bf16[4,2,32,256]{3,2,1,0:T(8,128)(2,1)S(1)}, bf16[4,2,32,256]{3,2,1,0:T(8,128)(2,1)}, u32[]{:S(2)}) copy-start(bf16[4,2,32,256]{3,2,1,0:T(8,128)(2,1)} %constant.41.clone.local_first_ref) | copy-start | bytes 393220
  2.7 38.3 %copy-start.7 = (bf16[128,256]{1,0:T(8,128)(2,1)S(1)}, bf16[128,256]{1,0:T(8,128)(2,1)}, u32[]{:S(2)}) copy-start(bf16[128,256]{1,0:T(8,128)(2,1)} %constant.49.clone.ninth_second_ref) | copy-start | bytes 196612
  2.7 38.3 %copy-start.8 = (bf16[4,32,256]{2,1,0:T(8,128)(2,1)S(1)}, bf16[4,32,256]{2,1,0:T(8,128)(2,1)}, u32[]{:S(2)}) copy-start(bf16[4,32,256]{2,1,0:T(8,128)(2,1)} %constant.46.clone.local_ninth_first_ref) | copy-start | bytes 196612
  20.8 20.3 %copy-start = (bf16[3,256,256]{2,1,0:T(8,128)(2,1)S(1)}, bf16[3,256,256]{2,1,0:T(8,128)(2,1)}, u32[]{:S(2)}) copy-start(bf16[3,256,256]{2,1,0:T(8,128)(2,1)} %constant.52.clone.edge_response_ref) | copy-start | bytes 1179652
  20.8 20.3 %copy-start.1 = (bf16[4,256,128]{2,1,0:T(8,128)(2,1)S(1)}, bf16[4,256,128]{2,1,0:T(8,128)(2,1)}, u32[]{:S(2)}) copy-start(bf16[4,256,128]{2,1,0:T(8,128)(2,1)} %constant.51.clone.edge_gather_ref) | copy-start | bytes 786436
  21.2 19.9 %copy-start.6 = (bf16[128,256]{1,0:T(8,128)(2,1)S(1)}, bf16[128,256]{1,0:T(8,128)(2,1)}, u32[]{:S(2)}) copy-start(bf16[128,256]{1,0:T(8,128)(2,1)} %constant.53.clone.edge_inject_ref) | copy-start | bytes 196612
  21.2 19.8 %copy-start.17 = (bf16[4,16,128]{2,1,0:T(8,128)(2,1)S(1)}, bf16[4,16,128]{2,1,0:T(8,128)(2,1)}, u32[]{:S(2)}) copy-start(bf16[4,16,128]{2,1,0:T(8,128)(2,1)} %constant.40.clone.gather_ninth_ref) | copy-start | bytes 49156
  42.0 16.3 %copy-start.18 = (s32[8,128]{1,0:T(8,128)S(1)}, s32[8,128]{1,0:T(8,128)}, u32[]{:S(2)}) copy-start(s32[8,128]{1,0:T(8,128)} %mask_ref.1) | copy-start | bytes 12292

commit v10 on v9

--- a/solution.py
+++ b/solution.py
@@ -22,11 +22,9 @@
 SPAN = GROUP * HOURS
 QUARTERS = (0, 3, 1, 2)
 PAIRS = ((0, 1), (2, 3), (4, 5), (6, 7))
-MEETINGS = (
-    ((1, 2, 0), (5, 6, 0), (0, 3, 0), (4, 7, 0)),
-    ((2, 5, 8), (3, 7, 8), (0, 1, 0), (4, 6, 0)),
-)
+MEETINGS = (((1, 2, 0), (5, 6, 0)), ((2, 5, 8),))
 SECOND = tuple(sum(1 << meeting[1] for meeting in meetings) for meetings in MEETINGS)
+ALONE = tuple(255 - sum((1 << meeting[0]) + (1 << meeting[1]) for meeting in meetings) for meetings in MEETINGS)
 HIGH = lax.Precision.HIGHEST
 
 
@@ -261,7 +259,11 @@
     device, column = lax.axis_index("tm"), lax.axis_index("col")
     odd = device % 2
     second = jnp.where(odd == 0, SECOND[0], SECOND[1])
-    return device // GROUP, (column + odd) % 2, lax.shift_right_logical(second, column) & 1
+    alone = jnp.where(odd == 0, ALONE[0], ALONE[1])
+    second = lax.shift_right_logical(second, column) & 1
+    alone = lax.shift_right_logical(alone, column) & 1
+    side = jnp.where(alone == 1, (device // 2) % 2, second)
+    return device // GROUP, (column + odd) % 2, side
 
 
 def lanes_of(shape=(ROWS, LANES)):
@@ -730,6 +732,11 @@
         [(z * GROUP + mine) * 8 + col for z in range(RUNS) for mine, col in ((j, first), (j ^ flip, second))]
         for j in range(GROUP)
         for first, second, flip in MEETINGS[j % 2]
+    ] + [
+        [(z * GROUP + i) * 8 + col for z in range(RUNS) for i in (j, j ^ 2)]
+        for j in range(GROUP)
+        for col in range(8)
+        if j & 2 == 0 and ALONE[j % 2] >> col & 1
     ]
     state_scratch = pltpu.VMEM((SERIES * 8, ROWS, LANES), jnp.float32)
     arguments = (levels, u_vel, v_vel, density, land_mask, start_hour)

time: 60 us -> 58.6 us (0.977)
  the two profiles are of different devices: /device:TPU:1 before, /device:TPU:6 now
where the time goes in v10:
time: 58.6 us; the launch traced here: 57.7 us
  blocking collectives  52.1 us (89%)
  Pallas kernels  4.57 us (8%)
  between operations  0.9 us (2%)
    all_to_all x3, blocking collectives, swap(): lax.all_to_all(array, ('tm', 'col'), 0, 0, tiled=True, axis_index_groups=...  52.1 us
    pallas_call x1, Pallas kernels, on_device(): call(summary_kernel, [flat, (SERIES, HOURS, ROWS, LANES)], [HBM] * 6, [pl...  1.91 us
    pallas_call x1, Pallas kernels, on_device(): call(band_kernel, [whole, whole], [VMEM] * 3, [pltpu.VMEM(whole, jnp.floa...  1.38 us

profile of v10, /device:TPU:6, one launch (start us, length us, event | category | flops | bytes accessed | tf_op | source)
XLA Modules:
  0.0 57.7 jit_solution(198519560251078191)
XLA Ops:
  0.6 0.0 copy-start.12
  0.6 0.0 copy-start.16
  0.7 0.0 copy-start.9
  0.7 0.0 copy-start.10
  0.7 0.0 copy-start.11
  0.7 0.0 copy-start.13
  0.7 0.0 copy-start.14
  0.7 0.0 copy-start.15
  0.7 1.9 %shard_map.239 = (f32[608,128]{1,0:T(8,128)S(1)}, f32[9,16,8,128]{3,2,1,0:T(8,128)S(1)}) custom-call(s32[4]{0:T(128)} %levels_hbm.1, f32[4,16,8,128]{3,2,1,0:T(8,128)} %u_hbm.1, f32[4,16,8,128]{3,2,1,0:T(8,128)} %v_hbm.1, f32[4,16,8,128]{3,2,1,0:T(8,128)} %rho_hbm.1, s32[8,128]{1,0:T(8,128)} %mask_ref.1, s32[8,128]{1,0:T(8,128)} %start_hbm.1), custom_call_target="tpu_custom_call" | custom-call | tf_op jit(solution)/shard_map/pallas_call | solution.py:743
  2.6 0.0 copy-start.2
  2.7 0.0 copy-start.3
  2.7 0.0 copy-start.4
  2.7 0.0 copy-start.5
  2.7 0.0 copy-start.7
  2.7 0.0 copy-start.8
  2.7 15.5 %all_to_all.15 = f32[32,1,2432]{2,1,0:T(1,128)S(1)} all-to-all(f32[32,1,2432]{2,1,0:T(1,128)S(1)} %bitcast.11), channel_id=1, replica_groups={{0,1,8,9,16,17,24,25,32,33,40,41,48,49,56,57,64,65,72,73,80,81,88,89,96..., dimensions={0} | all-to-all | bytes 622592 | tf_op jit(solution)/shard_map/all_to_all | solution.py:701
  18.2 0.0 copy-start
  18.2 0.0 copy-done.12
  18.2 0.0 copy-done.16
  18.2 0.0 copy-done.2
  18.2 0.0 copy-start.1
  18.3 0.4 shard_map.240
  18.7 0.0 copy-start.6
  18.7 0.0 copy-start.17
  18.7 22.7 %all_to_all.16 = f32[8,1,2432]{2,1,0:T(1,128)S(1)} all-to-all(f32[8,1,2432]{2,1,0:T(1,128)S(1)} %bitcast.12), channel_id=1, replica_groups={{1,2,129,130,257,258,385,386},{5,6,133,134,261,262,389,390},{10,77,138,..., dimensions={0} | all-to-all | bytes 155648 | tf_op jit(solution)/shard_map/all_to_all | solution.py:701
  41.4 0.0 copy-done.9
  41.4 0.0 copy-done.10
  41.4 0.0 copy-done.11
  41.4 0.0 copy-done.13
  41.4 0.0 copy-done.14
  41.4 0.0 copy-done.15
  41.4 0.0 copy-done.3
  41.4 0.0 copy-done.4
  41.4 0.0 copy-done.5
  41.4 0.0 copy-done.7
  41.5 0.0 copy-done.8
  41.5 0.0 copy-done
  41.5 0.0 copy-done.1
  41.5 0.0 copy-done.6
  41.5 0.0 copy-done.17
  41.5 0.9 %shard_map.241 = f32[608,128]{1,0:T(8,128)S(1)} custom-call(f32[608,128]{1,0:T(8,128)S(1)} %bitcast.7, f32[152,128]{1,0:T(8,128)S(1)} %bitcast.10, bf16[4,16,256]{2,1,0:T(8,128)(2,1)S(1)} %copy-done.15, bf16[4,16,128]{2,1,0:T(8,128)(2,1)S(1)} %copy-done.17, bf16[4,2,32,256]{3,2,1,0:T(8,128)(2,1)S(1)} %copy-done.5, bf16[4,2,16,256]{3,2,1,0:T(8,128)(2,1)S(1)} %copy-done.11, ...), custom_call_target="tpu_custom_call" | custom-call | tf_op jit(solution)/shard_map/pallas_call | solution.py:780
  42.4 0.0 copy-start.18
  42.4 13.9 %all_to_all.17 = f32[32,1,2432]{2,1,0:T(1,128)S(1)} all-to-all(f32[32,1,2432]{2,1,0:T(1,128)S(1)} %bitcast.8), channel_id=1, replica_groups={{0,1,8,9,16,17,24,25,32,33,40,41,48,49,56,57,64,65,72,73,80,81,88,89,96..., dimensions={0} | all-to-all | bytes 622592 | tf_op jit(solution)/shard_map/all_to_all | solution.py:701
  56.3 0.0 copy-done.18
  56.3 1.4 %shard_map.242 = (f32[4,16,8,128]{3,2,1,0:T(8,128)}, f32[4,16,8,128]{3,2,1,0:T(8,128)}) custom-call(f32[9,16,8,128]{3,2,1,0:T(8,128)S(1)} %get-tuple-element.4.kept_ref, s32[8,128]{1,0:T(8,128)S(1)} %copy-done.18, f32[608,128]{1,0:T(8,128)S(1)} %bitcast.9), custom_call_target="tpu_custom_call" | custom-call | tf_op jit(solution)/shard_map/pallas_call | solution.py:784
Async XLA Ops:
  0.6 17.6 %copy-start.12 = (f32[4,16,256]{2,1,0:T(8,128)S(1)}, f32[4,16,256]{2,1,0:T(8,128)}, u32[]{:S(2)}) copy-start(f32[4,16,256]{2,1,0:T(8,128)} %constant.36.clone.send_ref) | copy-start | bytes 196612
  0.6 17.6 %copy-start.16 = (f32[4,16,128]{2,1,0:T(8,128)S(1)}, f32[4,16,128]{2,1,0:T(8,128)}, u32[]{:S(2)}) copy-start(f32[4,16,128]{2,1,0:T(8,128)} %constant.37.clone.send_ninth_ref) | copy-start | bytes 98308
  0.7 40.7 %copy-start.9 = (bf16[256,128]{1,0:T(8,128)(2,1)S(1)}, bf16[256,128]{1,0:T(8,128)(2,1)}, u32[]{:S(2)}) copy-start(bf16[256,128]{1,0:T(8,128)(2,1)} %constant.45.clone.inject_ref) | copy-start | bytes 196612
  0.7 40.7 %copy-start.10 = (bf16[128,256]{1,0:T(8,128)(2,1)S(1)}, bf16[128,256]{1,0:T(8,128)(2,1)}, u32[]{:S(2)}) copy-start(bf16[128,256]{1,0:T(8,128)(2,1)} %constant.44.clone.spread_second_ref) | copy-start | bytes 196612
  0.7 40.7 %copy-start.11 = (bf16[4,2,16,256]{3,2,1,0:T(8,128)(2,1)S(1)}, bf16[4,2,16,256]{3,2,1,0:T(8,128)(2,1)}, u32[]{:S(2)}) copy-start(bf16[4,2,16,256]{3,2,1,0:T(8,128)(2,1)} %constant.42.clone.local_second_ref) | copy-start | bytes 196612
  0.7 40.7 %copy-start.13 = (bf16[128,128]{1,0:T(8,128)(2,1)S(1)}, bf16[128,128]{1,0:T(8,128)(2,1)}, u32[]{:S(2)}) copy-start(bf16[128,128]{1,0:T(8,128)(2,1)} %constant.50.clone.inject_ninth_ref) | copy-start | bytes 98308
  0.7 40.7 %copy-start.14 = (bf16[4,16,256]{2,1,0:T(8,128)(2,1)S(1)}, bf16[4,16,256]{2,1,0:T(8,128)(2,1)}, u32[]{:S(2)}) copy-start(bf16[4,16,256]{2,1,0:T(8,128)(2,1)} %constant.47.clone.local_ninth_second_ref) | copy-start | bytes 98308
  0.7 40.7 %copy-start.15 = (bf16[4,16,256]{2,1,0:T(8,128)(2,1)S(1)}, bf16[4,16,256]{2,1,0:T(8,128)(2,1)}, u32[]{:S(2)}) copy-start(bf16[4,16,256]{2,1,0:T(8,128)(2,1)} %constant.39.clone.gather_ref) | copy-start | bytes 98308
  2.6 15.6 %copy-start.2 = (f32[256,128]{1,0:T(8,128)S(1)}, f32[256,128]{1,0:T(8,128)}, u32[]{:S(2)}) copy-start(f32[256,128]{1,0:T(8,128)} %constant.38.clone.edge_sum_ref) | copy-start | bytes 393220
  2.7 38.8 %copy-start.3 = (bf16[256,256]{1,0:T(8,128)(2,1)S(1)}, bf16[256,256]{1,0:T(8,128)(2,1)}, u32[]{:S(2)}) copy-start(bf16[256,256]{1,0:T(8,128)(2,1)} %constant.48.clone.ninth_first_ref) | copy-start | bytes 393220
  2.7 38.8 %copy-start.4 = (bf16[256,256]{1,0:T(8,128)(2,1)S(1)}, bf16[256,256]{1,0:T(8,128)(2,1)}, u32[]{:S(2)}) copy-start(bf16[256,256]{1,0:T(8,128)(2,1)} %constant.43.clone.spread_first_ref) | copy-start | bytes 393220
  2.7 38.8 %copy-start.5 = (bf16[4,2,32,256]{3,2,1,0:T(8,128)(2,1)S(1)}, bf16[4,2,32,256]{3,2,1,0:T(8,128)(2,1)}, u32[]{:S(2)}) copy-start(bf16[4,2,32,256]{3,2,1,0:T(8,128)(2,1)} %constant.41.clone.local_first_ref) | copy-start | bytes 393220
  2.7 38.8 %copy-start.7 = (bf16[128,256]{1,0:T(8,128)(2,1)S(1)}, bf16[128,256]{1,0:T(8,128)(2,1)}, u32[]{:S(2)}) copy-start(bf16[128,256]{1,0:T(8,128)(2,1)} %constant.49.clone.ninth_second_ref) | copy-start | bytes 196612
  2.7 38.7 %copy-start.8 = (bf16[4,32,256]{2,1,0:T(8,128)(2,1)S(1)}, bf16[4,32,256]{2,1,0:T(8,128)(2,1)}, u32[]{:S(2)}) copy-start(bf16[4,32,256]{2,1,0:T(8,128)(2,1)} %constant.46.clone.local_ninth_first_ref) | copy-start | bytes 196612
  18.2 23.2 %copy-start = (bf16[3,256,256]{2,1,0:T(8,128)(2,1)S(1)}, bf16[3,256,256]{2,1,0:T(8,128)(2,1)}, u32[]{:S(2)}) copy-start(bf16[3,256,256]{2,1,0:T(8,128)(2,1)} %constant.52.clone.edge_response_ref) | copy-start | bytes 1179652
  18.2 23.2 %copy-start.1 = (bf16[4,256,128]{2,1,0:T(8,128)(2,1)S(1)}, bf16[4,256,128]{2,1,0:T(8,128)(2,1)}, u32[]{:S(2)}) copy-start(bf16[4,256,128]{2,1,0:T(8,128)(2,1)} %constant.51.clone.edge_gather_ref) | copy-start | bytes 786436
  18.7 22.8 %copy-start.6 = (bf16[128,256]{1,0:T(8,128)(2,1)S(1)}, bf16[128,256]{1,0:T(8,128)(2,1)}, u32[]{:S(2)}) copy-start(bf16[128,256]{1,0:T(8,128)(2,1)} %constant.53.clone.edge_inject_ref) | copy-start | bytes 196612
  18.7 22.8 %copy-start.17 = (bf16[4,16,128]{2,1,0:T(8,128)(2,1)S(1)}, bf16[4,16,128]{2,1,0:T(8,128)(2,1)}, u32[]{:S(2)}) copy-start(bf16[4,16,128]{2,1,0:T(8,128)(2,1)} %constant.40.clone.gather_ninth_ref) | copy-start | bytes 49156
  42.4 13.9 %copy-start.18 = (s32[8,128]{1,0:T(8,128)S(1)}, s32[8,128]{1,0:T(8,128)}, u32[]{:S(2)}) copy-start(s32[8,128]{1,0:T(8,128)} %mask_ref.1) | copy-start | bytes 12292
